TPU v7x, 32 devices: a whole 2x2x4 slice. The times are simulated.
32 devices in a mesh: gr: 8 (over z, y), gc: 4 (over x, core).
Axes of the slice: x: 2, y: 2, z: 4, core: 2. Of those that a mesh axis runs over, the one named last changes fastest.
Arguments:
- features: bfloat16 [4, 1024, 256], P('gc', 'gr'), may hold values from -6 to 6
- weight: bfloat16 [256, 256], replicated, may hold values from -0.375 to 0.375
- grad_out: bfloat16 [8, 512, 256], P('gr', 'gc'), may hold values from -6 to 6
- block_rows: int32 [8, 4, 6], P('gr', 'gc'), may hold values from 0 to 3, as said below
- block_cols: int32 [8, 4, 6], P('gr', 'gc'), may hold values from 0 to 7
- block_counts: int32 [8, 4], P('gr', 'gc'), may hold values from 1 to 6, as said below
- block_values: bfloat16 [8, 4, 6, 128, 128], P('gr', 'gc'), may hold values from -0.3125 to 0.3125
Outputs:
- activated: bfloat16 [8, 512, 256], P('gr', 'gc')
- grad_weight: float32 [256, 256], replicated
- grad_features: float32 [4, 1024, 256], P('gc', 'gr')
Inputs may be any that keep to these rules, and one draw needn't show every extreme that they name: Each tile's block positions (block_rows, block_cols) are distinct over its 6 slots. `block_counts`: some tile has all 6 slots live.
All inputs are finite; a program needn't handle non-finite values.
Results may differ from a plain program's by a relative error of at most 0.03.
Values may be sent and summed in bfloat16 or wider, within the bound.
No kernel may reach another device: no remote copies, remote signals or barrier semaphores. Data moves between devices by JAX's collectives and lax.ppermute only.
A program may use at most 64 MiB of HBM per device.

v0:
```python
import math

import jax
import jax.numpy as jnp
from jax import lax
from jax.sharding import PartitionSpec as P


def apply_blocks(source, block_values, block_rows, block_cols, live_count, out_blocks, transposed):
    slot_total = block_values.shape[0]
    group_size = math.gcd(slot_total, 16)
    group_total = slot_total // group_size
    block_side = block_values.shape[-1]
    width = source.shape[-1]

    def one_group(group_index, accum_rows):
        first_slot = group_index * group_size
        values_here = lax.dynamic_slice_in_dim(block_values, first_slot, group_size, 0)
        rows_here = lax.dynamic_slice_in_dim(block_rows, first_slot, group_size, 0)
        cols_here = lax.dynamic_slice_in_dim(block_cols, first_slot, group_size, 0)
        live_slots = first_slot + jnp.arange(group_size, dtype=jnp.int32) < live_count
        values_here = jnp.where(live_slots[:, None, None], values_here, jnp.zeros_like(values_here))
        if transposed:
            picked = source[rows_here]
            products = jnp.einsum(
                "gba,gbf->gaf", values_here, picked, preferred_element_type=jnp.float32
            )
            return accum_rows.at[cols_here].add(products)
        picked = source[cols_here]
        products = jnp.einsum(
            "gab,gbf->gaf", values_here, picked, preferred_element_type=jnp.float32
        )
        return accum_rows.at[rows_here].add(products)

    initial = jnp.zeros((out_blocks, block_side, width), jnp.float32)
    return lax.fori_loop(0, group_total, one_group, initial)


def weight_sum(hidden, grad_pre):
    local_terms = lax.dot_general(
        hidden, grad_pre, (((0,), (0,)), ((), ())), preferred_element_type=jnp.float32
    )
    return lax.psum(local_terms, ("gr", "gc"))


def per_device(features, weight, grad_out, block_rows, block_cols, block_counts, block_values):
    block_side = block_values.shape[-1]
    width = features.shape[-1]
    node_rows = features.shape[1]
    tile_values = block_values[0, 0]
    tile_rows = block_rows[0, 0]
    tile_cols = block_cols[0, 0]
    live_count = block_counts[0, 0]
    column_feats = lax.all_gather(features, "gr", axis=1, tiled=True)
    column_feats = column_feats.reshape(-1, block_side, width)
    row_blocks = lax.axis_size("gc") * node_rows // block_side
    col_blocks = column_feats.shape[0]
    partial_rows = apply_blocks(
        column_feats, tile_values, tile_rows, tile_cols, live_count, row_blocks, False
    )
    aggregated = lax.psum_scatter(
        partial_rows.reshape(row_blocks * block_side, width).astype(jnp.bfloat16),
        "gc",
        scatter_dimension=0,
        tiled=True,
    )
    pre = jnp.dot(aggregated, weight, preferred_element_type=jnp.float32)
    activated = jax.nn.silu(pre).astype(jnp.bfloat16)
    sigmoid_pre = jax.nn.sigmoid(pre)
    grad_pre = (
        grad_out[0].astype(jnp.float32) * sigmoid_pre * (1.0 + pre * (1.0 - sigmoid_pre))
    ).astype(jnp.bfloat16)
    grad_hidden = lax.dot_general(
        grad_pre, weight, (((1,), (1,)), ((), ())), preferred_element_type=jnp.float32
    ).astype(jnp.bfloat16)
    grad_block_rows = lax.all_gather(grad_hidden, "gc", axis=0, tiled=True)
    grad_block_rows = grad_block_rows.reshape(row_blocks, block_side, width)
    partial_cols = apply_blocks(
        grad_block_rows, tile_values, tile_rows, tile_cols, live_count, col_blocks, True
    )
    grad_features = lax.psum_scatter(
        partial_cols.reshape(col_blocks * block_side, width).astype(jnp.bfloat16),
        "gr",
        scatter_dimension=0,
        tiled=True,
    ).astype(jnp.float32)
    grad_weight = weight_sum(aggregated, grad_pre)
    return (
        activated.reshape(1, node_rows, width),
        grad_weight,
        grad_features.reshape(1, node_rows, width),
    )


def solution(mesh):
    placed = (
        P("gc", "gr", None),
        P(),
        P("gr", "gc", None),
        P("gr", "gc", None),
        P("gr", "gc", None),
        P("gr", "gc"),
        P("gr", "gc", None, None, None),
    )
    return jax.shard_map(
        per_device,
        mesh=mesh,
        in_specs=placed,
        out_specs=(P("gr", "gc", None), P(), P("gc", "gr", None)),
        check_vma=False,
    )
```

profile of v0, /device:TPU:0, one launch (start us, length us, event | category | flops | bytes accessed | tf_op | source)
XLA Modules:
  0.0 286.1 jit_solution(6831112088682565272)
XLA Ops:
  7.2 0.0 copy-start
  7.2 0.0 reduce-scatter.3.cloned.1.call-start
  7.2 33.2 %all_gather.6 = bf16[1,1024,256]{2,1,0:T(8,128)(2,1)S(1)} all-gather(bf16[1,128,256]{2,1,0:T(8,128)(2,1)} %param.11), channel_id=1, replica_groups=mesh['gr'=8,'gc'=4] {'gr'}, dimensions={1}, use_global_device_ids=true | all-gather | bytes 589824 | tf_op jit(solution)/shard_map/all_gather | solution.py:54
  40.4 0.0 copy-start.1
  40.4 0.0 copy-start.3
  40.4 0.0 copy-start.4
  40.5 0.9 copy-done.1
  41.4 0.0 copy-done.3
  41.4 0.0 copy-done.4
  41.4 6.8 %while.26 = (s32[]{:T(128)}, f32[4,128,256]{2,1,0:T(8,128)S(1)}, s32[6]{0:T(128)S(1)}, s32[]{:T(128)}, bf16[6,128,128]{2,1,0:T(8,128)(2,1)S(1)}, /*index=5*/s32[...) while((s32[]{:T(128)}, f32[4,128,256]{2,1,0:T(8,128)S(1)}, ...), condition=%wide.region_2.3_spmd, body=%wide.region_0.2_spmd.sunk | while | flops 16876564 | bytes 1512165 | solution.py:36
  41.4 0.7 add_compare_fusion.4
  42.0 0.1 compare_select_fusion.6
  42.1 0.6 gather_fusion
  42.7 0.2 fusion.34
  42.9 0.7 scatter_fusion
  43.6 0.7 add_compare_fusion.4
  44.3 0.1 compare_select_fusion.6
  44.4 0.6 gather_fusion
  45.0 0.2 fusion.34
  45.2 0.7 scatter_fusion
  45.9 0.7 add_compare_fusion.4
  46.6 0.1 compare_select_fusion.6
  46.7 0.6 gather_fusion
  47.2 0.2 fusion.34
  47.5 0.7 scatter_fusion
  48.2 0.7 convert_element_type.28
  48.9 0.0 reduce-scatter.3.cloned.1.call-update
  48.9 0.0 reduce-scatter.5.cloned.1.call-start
  49.0 0.0 copy-start.5
  49.0 0.2 copy.10
  49.2 21.1 %reduce-scatter.3.cloned.1.call-done = bf16[128,256]{1,0:T(8,128)(2,1)} async-done(((bf16[512,256]{1,0:T(8,128)(2,1)}), bf16[128,256]{1,0:T(8,128)(2,1)}) %reduce-scatter.3.cloned.1.call-update) | async-done | bytes 65552 | tf_op jit(solution)/shard_map/reduce_scatter | solution.py:61
  70.2 0.0 copy-done
  70.2 0.0 copy-done.5
  70.2 1.7 fusion.15
  71.9 0.2 convolution_convert_fusion
  72.1 5.8 %all_gather.7 = bf16[512,256]{1,0:T(8,128)(2,1)S(1)} all-gather(bf16[128,256]{1,0:T(8,128)(2,1)S(1)} %convolution_convert_fusion), channel_id=1, replica_groups=mesh['gr'=8,'gc'=4] {'gc'}, dimensions={0}, use_global_device_ids=true | all-gather | bytes 327680 | tf_op jit(solution)/shard_map/all_gather | solution.py:76
  77.9 0.1 broadcast_in_dim.74
  78.0 6.8 %while.27 = (s32[]{:T(128)}, f32[8,128,256]{2,1,0:T(8,128)S(1)}, s32[6]{0:T(128)S(1)}, s32[]{:T(128)}, bf16[6,128,128]{1,2,0:T(8,128)(2,1)S(1)}, /*index=5*/s32[...) while((s32[]{:T(128)}, f32[8,128,256]{2,1,0:T(8,128)S(1)}, ...), condition=%wide.region_7.8_spmd, body=%wide.region_5.0_spmd.sunk | while | flops 16876564 | bytes 1512165 | solution.py:36
  78.0 0.7 add_compare_fusion.5
  78.7 0.1 compare_select_fusion.7
  78.8 0.6 gather_fusion.1
  79.3 0.2 fusion.37
  79.6 0.7 scatter_fusion.1
  80.3 0.7 add_compare_fusion.5
  80.9 0.1 compare_select_fusion.7
  81.0 0.6 gather_fusion.1
  81.6 0.2 fusion.37
  81.8 0.7 scatter_fusion.1
  82.6 0.7 add_compare_fusion.5
  83.2 0.1 compare_select_fusion.7
  83.3 0.6 gather_fusion.1
  83.9 0.2 fusion.37
  84.1 0.7 scatter_fusion.1
  84.8 0.8 convert_element_type.35
  85.6 0.0 copy-start.2
  85.6 0.0 reduce-scatter.5.cloned.1.call-update
  85.7 0.0 all-reduce.2.cloned.1.call-start
  85.7 0.8 copy-done.2
  86.5 0.9 fusion.17
  87.4 0.0 all-reduce.2.cloned.1.call-update
  87.4 60.4 %reduce-scatter.5.cloned.1.call-done = bf16[128,256]{1,0:T(8,128)(2,1)} async-done(((bf16[1024,256]{1,0:T(8,128)(2,1)}), bf16[128,256]{1,0:T(8,128)(2,1)}) %reduce-scatter.5.cloned.1.call-update) | async-done | bytes 65552 | tf_op jit(solution)/shard_map/reduce_scatter | solution.py:81
  147.8 1.5 bitcast_convert_fusion
  149.3 128.6 %all-reduce.2.cloned.1.call-done = f32[256,256]{1,0:T(8,128)} async-done(((f32[256,256]{1,0:T(8,128)}), f32[256,256]{1,0:T(8,128)}) %all-reduce.2.cloned.1.call-update) | async-done | bytes 262160 | tf_op jit(solution)/shard_map/psum | solution.py:43
  277.9 1.7 copy.28
  (7 shorter events, 0.1 us)
Async XLA Ops:
  7.2 63.1 %copy-start = (bf16[256,256]{1,0:T(8,128)(2,1)S(1)}, bf16[256,256]{1,0:T(8,128)(2,1)}, u32[]{:S(2)}) copy-start(bf16[256,256]{1,0:T(8,128)(2,1)} %param.12) | copy-start | bytes 393220
  7.2 63.0 %reduce-scatter.3.cloned.1.call-start = ((), (), s32[]{:S(2)}) async-start(), calls=%async_computation.2 | async-start | bytes 327680 | tf_op jit(solution)/shard_map/reduce_scatter | solution.py:61
  40.4 0.9 copy-start.1
  40.4 0.9 copy-start.3
  40.4 0.9 copy-start.4
  48.9 98.8 %reduce-scatter.5.cloned.1.call-start = ((), (), s32[]{:S(2)}) async-start(), calls=%async_computation.4 | async-start | bytes 589824 | tf_op jit(solution)/shard_map/reduce_scatter | solution.py:81
  49.0 21.2 %copy-start.5 = (bf16[1,128,256]{2,1,0:T(8,128)(2,1)S(1)}, bf16[1,128,256]{2,1,0:T(8,128)(2,1)}, u32[]{:S(2)}) copy-start(bf16[1,128,256]{2,1,0:T(8,128)(2,1)} %param.13) | copy-start | bytes 196612
  85.6 0.8 copy-start.2
  85.7 192.2 %all-reduce.2.cloned.1.call-start = ((), (), s32[]{:S(2)}) async-start(), calls=%async_computation.3 | async-start | bytes 524288 | tf_op jit(solution)/shard_map/psum | solution.py:43
Sparse Core Ops, SparseCore 0:
  49.1 21.1 reduce-scatter.2
  85.8 61.9 reduce-scatter.4
  153.9 123.9 all-reduce.1
where the time goes:
time: 286 us
  waiting for transfers between devices  210 us (73%)
  blocking collectives  39 us (14%)
  between operations  13.8 us (5%)
  other arithmetic  11.7 us (4%)
  local copies, waits for them, and re-layouts  6.95 us (2%)
  matrix products  4.17 us (1%)
    psum x1, waiting for transfers between devices, weight_sum(): return lax.psum(local_terms, ('gr', 'gc'))  129 us
    reduce_scatter x1, waiting for transfers between devices, per_device(): lax.psum_scatter(partial_cols.reshape(col_blocks * block_side, width).ast...  60.4 us
    all_gather x1, blocking collectives, per_device(): column_feats = lax.all_gather(features, 'gr', axis=1, tiled=True)  33.2 us
    reduce_scatter x1, waiting for transfers between devices, per_device(): lax.psum_scatter(partial_rows.reshape(row_blocks * block_side, width).ast...  21.1 us
    all_gather x1, blocking collectives, per_device(): grad_block_rows = lax.all_gather(grad_hidden, 'gc', axis=0, tiled=True)  5.79 us
  transfers between devices with their start and end apart: 3, of which 3 were waited for; matrix products, arithmetic and copies ran while one was open for 1% of the time, Pallas kernels for 0%

commit v1 on v0

v1 whole, which is shorter than its diff:
```python
import functools

import jax
import jax.numpy as jnp
from jax import lax
from jax.experimental import pallas as pl
from jax.experimental.pallas import tpu as pltpu
from jax.sharding import PartitionSpec as P

VMEM = pl.BlockSpec(memory_space=pltpu.VMEM)
SMEM = pl.BlockSpec(memory_space=pltpu.SMEM)
FULL = (((1,), (0,)), ((), ()))
LEFT_T = (((0,), (0,)), ((), ()))
RIGHT_T = (((1,), (1,)), ((), ()))


def f32(value):
    return value.astype(jnp.float32)


def bf16(value):
    return value.astype(jnp.bfloat16)


def swap(value, axis, mask):
    size = lax.axis_size(axis)
    return lax.ppermute(value, axis, [(i, i ^ mask) for i in range(size)])


def bits_of(axis):
    return [1 << b for b in range(lax.axis_size(axis).bit_length() - 1)]


def params(nbytes):
    return pltpu.CompilerParams(vmem_limit_bytes=nbytes)


def per_slot(count, slots, body):
    if slots <= 8:
        for s in range(slots):
            pl.when(s < count)(functools.partial(body, s))
    else:
        lax.fori_loop(0, count, lambda s, _: (body(s), 0)[1], 0)


def forward_kernel(layout, send_masks, keep_masks, info, values, *refs):
    pieces, (send, keep, source, total) = refs[: len(layout)], refs[len(layout):]
    slots, side = values.shape[0], values.shape[1]
    for masks, piece in zip(layout, pieces):
        for n, m in enumerate(masks):
            source[m] = piece[pl.ds(n * side, side), :]
    total[...] = jnp.zeros_like(total)

    def one(s):
        total[info[s]] += lax.dot_general(
            values[s], source[info[slots + s]], FULL, preferred_element_type=jnp.float32
        )

    per_slot(info[2 * slots], slots, one)
    for n, m in enumerate(send_masks):
        send[pl.ds(n * side, side), :] = bf16(total[m])
    for n, m in enumerate(keep_masks):
        keep[pl.ds(n * side, side), :] = bf16(total[m])


def backward_kernel(layout, out_layout, info, values, *refs):
    pieces, rest = refs[: len(layout)], refs[len(layout):]
    outs, (source, total) = rest[: len(out_layout)], rest[len(out_layout):]
    slots, side = values.shape[0], values.shape[1]
    for masks, piece in zip(layout, pieces):
        for n, m in enumerate(masks):
            source[m] = piece[pl.ds(n * side, side), :]
    total[...] = jnp.zeros_like(total)

    def one(s):
        total[info[slots + s]] += lax.dot_general(
            values[s], source[info[s]], LEFT_T, preferred_element_type=jnp.float32
        )

    per_slot(info[2 * slots], slots, one)
    for masks, out in zip(out_layout, outs):
        for n, m in enumerate(masks):
            out[pl.ds(n * side, side), :] = bf16(total[m])


def dense_kernel(mine, near, far, weight, grad_out, activated, hidden, grad_pre, grad_hidden):
    rows = far.shape[0]
    summed = f32(mine[:rows, :]) + f32(near[:rows, :]) + f32(far[...])
    h = bf16(summed)
    w = weight[...]
    pre = lax.dot_general(h, w, FULL, preferred_element_type=jnp.float32)
    s = jax.nn.sigmoid(pre)
    activated[...] = bf16(pre * s)
    g = bf16(f32(grad_out[...]) * s * (1.0 + pre * (1.0 - s)))
    hidden[...] = h
    grad_pre[...] = g
    grad_hidden[...] = bf16(
        lax.dot_general(g, w, RIGHT_T, preferred_element_type=jnp.float32)
    )


def per_device(features, weight, grad_out, block_rows, block_cols, block_counts, block_values):
    side, width = features.shape[1:]
    values = block_values[0, 0]
    slots = values.shape[0]
    gr_size, gc_size = lax.axis_size("gr"), lax.axis_size("gc")
    gr, gc = lax.axis_index("gr"), lax.axis_index("gc")
    outer = [m for m in range(0, gr_size, 2)]
    far_first = sorted(outer[2:]) + [2]
    block = jax.ShapeDtypeStruct((side, width), jnp.bfloat16)

    def stacked(n):
        return jax.ShapeDtypeStruct((n * side, width), jnp.bfloat16)

    limit = 48 * 2**20
    info = jnp.concatenate([block_rows[0, 0] ^ gc, block_cols[0, 0] ^ gr, block_counts[0]])

    with jax.named_scope("gather_features"):
        x = features[0]
        direct = {m: swap(x, "gr", m) for m in far_first}
        near = swap(jnp.concatenate([x, direct[2]], axis=0), "gr", 1)
        sides = {m: swap(direct[m], "gr", 1) for m in far_first[:-1]}
    layout = [(0,), (2,), (1, 3)]
    pieces = [x, direct[2], near]
    for m in far_first[:-1]:
        layout += [(m,), (m + 1,)]
        pieces += [direct[m], sides[m]]

    with jax.named_scope("forward_blocks"):
        send_masks = [m for m in range(gc_size) if m & 1]
        keep_masks = [m for m in range(gc_size) if not m & 1]
        send, keep = pl.pallas_call(
            functools.partial(forward_kernel, layout, send_masks, keep_masks),
            out_shape=[stacked(len(send_masks)), stacked(len(keep_masks))],
            in_specs=[SMEM] + [VMEM] * (1 + len(pieces)),
            out_specs=[VMEM, VMEM],
            scratch_shapes=[
                pltpu.VMEM((gr_size, side, width), jnp.bfloat16),
                pltpu.VMEM((gc_size, side, width), jnp.float32),
            ],
            compiler_params=params(limit),
        )(info, values, *pieces)

    with jax.named_scope("sum_rows"):
        got = swap(send, "gc", 1)
        held = len(keep_masks)
        for bit in reversed(bits_of("gc")[1:]):
            half = held // 2 * side
            outgoing = bf16(f32(keep[half:]) + f32(got[half:]))
            if held > 2:
                keep = bf16(f32(keep[:half]) + f32(got[:half]))
                got = swap(outgoing, "gc", bit)
            else:
                last = swap(outgoing, "gc", bit)
            held //= 2

    with jax.named_scope("dense"):
        activated, hidden, grad_pre, grad_hidden = pl.pallas_call(
            dense_kernel,
            out_shape=[block] * 4,
            in_specs=[VMEM] * 5,
            out_specs=[VMEM] * 4,
            compiler_params=params(limit),
        )(keep, got, last, weight, grad_out[0])

    with jax.named_scope("gather_grad_hidden"):
        held = {0: grad_hidden}
        for bit in reversed(bits_of("gc")):
            held.update({m | bit: swap(v, "gc", bit) for m, v in list(held.items())})

    with jax.named_scope("backward_blocks"):
        far = far_first[:-1]
        out_layout = [tuple(m + 1 for m in far), (3, 1), tuple(far), (2, 0)]
        far_send, near_send, far_keep, near_keep = pl.pallas_call(
            functools.partial(backward_kernel, [(m,) for m in held], out_layout),
            out_shape=[stacked(len(masks)) for masks in out_layout],
            in_specs=[SMEM] + [VMEM] * (1 + len(held)),
            out_specs=[VMEM] * 4,
            scratch_shapes=[
                pltpu.VMEM((gc_size, side, width), jnp.bfloat16),
                pltpu.VMEM((gr_size, side, width), jnp.float32),
            ],
            compiler_params=params(limit),
        )(info, values, *held.values())

    with jax.named_scope("sum_columns"):
        far_got = swap(far_send, "gr", 1)
        near_got = swap(near_send, "gr", 1)
        terms = []
        for n, m in enumerate(far):
            rows = slice(n * side, (n + 1) * side)
            terms.append(swap(bf16(f32(far_keep[rows]) + f32(far_got[rows])), "gr", m))
        terms.append(swap(bf16(f32(near_keep[:side]) + f32(near_got[:side])), "gr", 2))
        grad_features = f32(near_keep[side:]) + f32(near_got[side:])
        for term in terms:
            grad_features = grad_features + f32(term)

    with jax.named_scope("sum_weight"):
        local = bf16(lax.dot_general(hidden, grad_pre, LEFT_T, preferred_element_type=jnp.float32))
        half = width // 2
        upper = (gc & 1) == 0
        top, bottom = local[:half], local[half:]
        running = f32(jnp.where(upper, top, bottom)) + f32(
            swap(jnp.where(upper, bottom, top), "gc", 1)
        )
        for axis, bits in (("gc", bits_of("gc")[1:]), ("gr", bits_of("gr"))):
            for bit in bits:
                mine = bf16(running)
                running = f32(mine) + f32(swap(mine, axis, bit))
        other = swap(running, "gc", 1)
        grad_weight = jnp.where(
            upper, jnp.concatenate([running, other]), jnp.concatenate([other, running])
        )
    return activated[None], grad_weight, grad_features[None]


def solution(mesh):
    placed = (
        P("gc", "gr", None),
        P(),
        P("gr", "gc", None),
        P("gr", "gc", None),
        P("gr", "gc", None),
        P("gr", "gc"),
        P("gr", "gc", None, None, None),
    )
    return jax.shard_map(
        per_device,
        mesh=mesh,
        in_specs=placed,
        out_specs=(P("gr", "gc", None), P(), P("gc", "gr", None)),
        check_vma=False,
    )
```

time: 286 us -> 53.3 us (0.19)
  waiting for transfers between devices: 210 us -> 20.1 us
  blocking collectives: 39 us -> 0 us
  starting transfers between devices: 0.12 us -> 26.9 us
  between operations: 13.8 us -> 1.43 us
  other arithmetic: 11.7 us -> 2.61 us
  local copies, waits for them, and re-layouts: 6.95 us -> 0.03 us
  matrix products: 4.17 us -> 0.2 us
    psum x1 -> x0, waiting for transfers between devices: 129 us -> none  [weight_sum(): return lax.psum(local_terms, ('gr', 'gc'))]
    reduce_scatter x2 -> x0, waiting for transfers between devices: 81.4 us -> none  [the longest x1 60.4 us: per_device(): lax.psum_scatter(partial_cols.reshape(col_blocks * block_side, width).ast...]
    all_gather x2 -> x0, blocking collectives: 39 us -> none  [the longest x1 33.2 us: per_device(): column_feats = lax.all_gather(features, 'gr', axis=1, tiled=True)]
    ppermute x0 -> x22, starting transfers between devices: none -> 26.9 us  [swap(): return lax.ppermute(value, axis, [(i, i ^ mask) for i in range(size)])]
    ppermute x0 -> x22, waiting for transfers between devices: none -> 20.1 us  [swap(): return lax.ppermute(value, axis, [(i, i ^ mask) for i in range(size)])]
    scatter-add x6 -> x0, other arithmetic: 4.16 us -> none  [the longest x3 2.08 us: one_group(): return accum_rows.at[rows_here].add(products)]
    dot_general x9 -> x1, matrix products: 4.17 us -> 0.2 us  [per_device(): lax.dot_general(hidden, grad_pre, LEFT_T, preferred_element_type=jnp.floa...]
    lt x6 -> x0, other arithmetic: 3.92 us -> none  [one_group(): first_slot + jnp.arange(group_size, dtype=jnp.int32) < live_count]
  transfers between devices with their start and end apart: 3 -> 22, of which waited for: 3 -> 12; matrix products, arithmetic and copies ran while one was open for 1% -> 3% of each run, Pallas kernels for 0% -> 2%
where the time goes in v1:
time: 53.3 us; the launch traced here: 53.8 us
  starting transfers between devices  26.9 us (50%)
  waiting for transfers between devices  20.1 us (38%)
  other arithmetic  2.61 us (5%)
  Pallas kernels  2.5 us (5%)
  between operations  1.43 us (3%)
    ppermute x22, starting transfers between devices, swap(): return lax.ppermute(value, axis, [(i, i ^ mask) for i in range(size)])  26.9 us
    ppermute x22, waiting for transfers between devices, swap(): return lax.ppermute(value, axis, [(i, i ^ mask) for i in range(size)])  20.1 us
  transfers between devices with their start and end apart: 22, of which 12 were waited for; matrix products, arithmetic and copies ran while one was open for 3% of the time, Pallas kernels for 2%

profile of v1, /device:TPU:0, one launch (start us, length us, event | category | flops | bytes accessed | tf_op | source)
XLA Modules:
  0.0 53.8 jit_solution(8176769654194231931)
XLA Ops:
  0.6 0.0 copy-start
  0.6 3.1 %collective-permute-start = (bf16[128,256]{1,0:T(8,128)(2,1)}, bf16[128,256]{1,0:T(8,128)(2,1)S(1)}, u32[]{:S(2)}, u32[]{:S(2)}) collective-permute-start(bf16[128,256]{1,0:T(8,128)(2,1)} %bitcast.16), channel_id=1, source_target_pairs={{0,8},{4,12},{8,0},{12,4},{16,24},{20,28},{24,16},{28,20},{1,9},{5... | collective-permute-start | bytes 196616 | tf_op jit(solution)/shard_map/gather_features/ppermute | solution.py:27
  3.7 2.6 %collective-permute-start.2 = (bf16[128,256]{1,0:T(8,128)(2,1)}, bf16[128,256]{1,0:T(8,128)(2,1)S(1)}, u32[]{:S(2)}, u32[]{:S(2)}) collective-permute-start(bf16[128,256]{1,0:T(8,128)(2,1)} %bitcast.17), channel_id=1, source_target_pairs={{0,16},{4,20},{8,24},{12,28},{16,0},{20,4},{24,8},{28,12},{1,17},{... | collective-permute-start | bytes 196616 | tf_op jit(solution)/shard_map/gather_features/ppermute | solution.py:27
  6.3 0.0 collective-permute-start.4
  6.3 0.0 copy-start.4
  6.3 0.0 copy-start.5
  6.3 0.0 copy-start.1
  6.3 0.0 collective-permute-done.refs_1_
  6.3 0.9 %pad_maximum_fusion = bf16[256,256]{1,0:T(8,128)(2,1)S(1)} fusion(bf16[128,256]{1,0:T(8,128)(2,1)S(1)} %collective-permute-done.refs_1_, bf16[128,256]{1,0:T(8,128)(2,1)} %bitcast.19), kind=kLoop, calls=%fused_computation.2 | loop fusion | flops 262144 | bytes 262144 | tf_op jit(solution)/shard_map/gather_features/concatenate | solution.py:121
  7.3 1.8 %collective-permute-start.1 = (bf16[256,256]{1,0:T(8,128)(2,1)S(1)}, bf16[256,256]{1,0:T(8,128)(2,1)S(1)}, u32[]{:S(2)}, u32[]{:S(2)}) collective-permute-start(bf16[256,256]{1,0:T(8,128)(2,1)S(1)} %pad_maximum_fusion), channel_id=1, source_target_pairs={{0,4},{4,0},{8,12},{12,8},{16,20},{20,16},{24,28},{28,24},{1,5},{5... | collective-permute-start | bytes 393224 | tf_op jit(solution)/shard_map/gather_features/ppermute | solution.py:27
  9.1 0.0 copy-done.4
  9.1 0.0 copy-done.5
  9.7 1.5 %collective-permute-done.2.refs_3_ = bf16[128,256]{1,0:T(8,128)(2,1)S(1)} collective-permute-done((bf16[128,256]{1,0:T(8,128)(2,1)}, bf16[128,256]{1,0:T(8,128)(2,1)S(1)}, u32[]{:S(2)}, u32[]{:S(2)}) %collective-permute-start.2) | collective-permute-done | bytes 65568 | tf_op jit(solution)/shard_map/gather_features/ppermute | solution.py:27
  11.2 1.5 %collective-permute-start.3 = (bf16[128,256]{1,0:T(8,128)(2,1)S(1)}, bf16[128,256]{1,0:T(8,128)(2,1)S(1)}, u32[]{:S(2)}, u32[]{:S(2)}) collective-permute-start(bf16[128,256]{1,0:T(8,128)(2,1)S(1)} %collective-permute-done.2.refs_3_), channel_id=1, source_target_pairs={{0,4},{4,0},{8,12},{12,8},{16,20},{20,16},{24,28},{28,24},{1,5},{5... | collective-permute-start | bytes 196616 | tf_op jit(solution)/shard_map/gather_features/ppermute | solution.py:27
  12.7 0.0 collective-permute-done.4.refs_5_
  12.7 1.4 %collective-permute-start.5 = (bf16[128,256]{1,0:T(8,128)(2,1)S(1)}, bf16[128,256]{1,0:T(8,128)(2,1)S(1)}, u32[]{:S(2)}, u32[]{:S(2)}) collective-permute-start(bf16[128,256]{1,0:T(8,128)(2,1)S(1)} %collective-permute-done.4.refs_5_), channel_id=1, source_target_pairs={{0,4},{4,0},{8,12},{12,8},{16,20},{20,16},{24,28},{28,24},{1,5},{5... | collective-permute-start | bytes 196616 | tf_op jit(solution)/shard_map/gather_features/ppermute | solution.py:27
  14.1 0.1 pad_add_fusion.info
  14.2 1.3 %collective-permute-done.3.refs_4_ = bf16[128,256]{1,0:T(8,128)(2,1)S(1)} collective-permute-done((bf16[128,256]{1,0:T(8,128)(2,1)S(1)}, bf16[128,256]{1,0:T(8,128)(2,1)S(1)}, u32[]{:S(2)}, u32[]{:S(2)}) %collective-permute-start.3) | collective-permute-done | bytes 65568 | tf_op jit(solution)/shard_map/gather_features/ppermute | solution.py:27
  15.5 1.5 %collective-permute-done.5.refs_6_ = bf16[128,256]{1,0:T(8,128)(2,1)S(1)} collective-permute-done((bf16[128,256]{1,0:T(8,128)(2,1)S(1)}, bf16[128,256]{1,0:T(8,128)(2,1)S(1)}, u32[]{:S(2)}, u32[]{:S(2)}) %collective-permute-start.5) | collective-permute-done | bytes 65568 | tf_op jit(solution)/shard_map/gather_features/ppermute | solution.py:27
  17.0 0.0 collective-permute-done.1.refs_2_
  17.0 0.0 copy-done
  17.0 0.0 copy-done.1
  17.0 0.8 %forward_blocks.1 = (bf16[256,256]{1,0:T(8,128)(2,1)S(1)}, bf16[256,256]{1,0:T(8,128)(2,1)S(1)}) custom-call(s32[13]{0:T(128)S(1)} %pad_add_fusion.info, bf16[6,128,128]{2,1,0:T(8,128)(2,1)S(1)} %bitcast.14, bf16[128,256]{1,0:T(8,128)(2,1)S(1)} %bitcast.20, bf16[128,256]{1,0:T(8,128)(2,1)S(1)} %collective-permute-done.refs_1_, ...), custom_call_target="tpu_custom_call" | custom-call | tf_op jit(solution)/shard_map/forward_blocks/pallas_call | solution.py:132
  17.8 0.0 copy-start.2
  17.8 0.1 collective-permute-start.6
  17.9 1.3 %collective-permute-done.6.near = bf16[256,256]{1,0:T(8,128)(2,1)S(1)} collective-permute-done((bf16[256,256]{1,0:T(8,128)(2,1)S(1)}, bf16[256,256]{1,0:T(8,128)(2,1)S(1)}, u32[]{:S(2)}, u32[]{:S(2)}) %collective-permute-start.6) | collective-permute-done | bytes 131104 | tf_op jit(solution)/shard_map/sum_rows/ppermute | solution.py:27
  19.3 0.0 copy-start.3
  19.3 1.6 %collective-permute-start.7 = (bf16[128,256]{1,0:T(8,128)(2,1)S(1)}, bf16[128,256]{1,0:T(8,128)(2,1)S(1)}, u32[]{:S(2)}, u32[]{:S(2)}) collective-permute-start(bf16[128,256]{1,0:T(8,128)(2,1)S(1)} %add_convert_fusion.7), channel_id=1, source_target_pairs={{0,2},{1,3},{2,0},{3,1},{4,6},{5,7},{6,4},{7,5},{8,10},{9,11},{10,... | collective-permute-start | bytes 196616 | tf_op jit(solution)/shard_map/sum_rows/ppermute | solution.py:27
  20.8 2.8 %collective-permute-done.7.far = bf16[128,256]{1,0:T(8,128)(2,1)S(1)} collective-permute-done((bf16[128,256]{1,0:T(8,128)(2,1)S(1)}, bf16[128,256]{1,0:T(8,128)(2,1)S(1)}, u32[]{:S(2)}, u32[]{:S(2)}) %collective-permute-start.7) | collective-permute-done | bytes 65568 | tf_op jit(solution)/shard_map/sum_rows/ppermute | solution.py:27
  23.6 0.0 copy-done.2
  23.6 0.0 copy-done.3
  23.6 0.8 %dense.1 = (bf16[128,256]{1,0:T(8,128)(2,1)}, bf16[128,256]{1,0:T(8,128)(2,1)S(1)}, bf16[128,256]{1,0:T(8,128)(2,1)S(1)}, bf16[128,256]{1,0:T(8,128)(2,1)S(1)}) custom-call(bf16[256,256]{1,0:T(8,128)(2,1)S(1)} %get-tuple-element.13.mine, bf16[256,256]{1,0:T(8,128)(2,1)S(1)} %collective-permute-done.6.near, bf16[128,256]{1,0:T(8,128)(2,1)S(1)} %collective-permute-done.7.far, ...), custom_call_target="tpu_custom_call" | custom-call | tf_op jit(solution)/shard_map/dense/pallas_call | solution.py:158
  24.4 0.2 convolution_convert_fusion
  24.7 0.1 collective-permute-start.8
  24.8 1.2 %collective-permute-done.8 = bf16[128,256]{1,0:T(8,128)(2,1)S(1)} collective-permute-done((bf16[128,256]{1,0:T(8,128)(2,1)S(1)}, bf16[128,256]{1,0:T(8,128)(2,1)S(1)}, u32[]{:S(2)}, u32[]{:S(2)}) %collective-permute-start.8) | collective-permute-done | bytes 65568 | tf_op jit(solution)/shard_map/sum_weight/ppermute | solution.py:27
  26.0 1.6 %collective-permute-start.9 = (bf16[128,256]{1,0:T(8,128)(2,1)S(1)}, bf16[128,256]{1,0:T(8,128)(2,1)S(1)}, u32[]{:S(2)}, u32[]{:S(2)}) collective-permute-start(bf16[128,256]{1,0:T(8,128)(2,1)S(1)} %add_convert_fusion.6), channel_id=1, source_target_pairs={{0,2},{1,3},{2,0},{3,1},{4,6},{5,7},{6,4},{7,5},{8,10},{9,11},{10,... | collective-permute-start | bytes 196616 | tf_op jit(solution)/shard_map/sum_weight/ppermute | solution.py:27
  27.6 0.5 collective-permute-start.14
  28.1 2.6 %collective-permute-done.9 = bf16[128,256]{1,0:T(8,128)(2,1)S(1)} collective-permute-done((bf16[128,256]{1,0:T(8,128)(2,1)S(1)}, bf16[128,256]{1,0:T(8,128)(2,1)S(1)}, u32[]{:S(2)}, u32[]{:S(2)}) %collective-permute-start.9) | collective-permute-done | bytes 65568 | tf_op jit(solution)/shard_map/sum_weight/ppermute | solution.py:27
  30.8 1.5 %collective-permute-start.10 = (bf16[128,256]{1,0:T(8,128)(2,1)S(1)}, bf16[128,256]{1,0:T(8,128)(2,1)S(1)}, u32[]{:S(2)}, u32[]{:S(2)}) collective-permute-start(bf16[128,256]{1,0:T(8,128)(2,1)S(1)} %add_convert_fusion.5), channel_id=1, source_target_pairs={{0,4},{4,0},{8,12},{12,8},{16,20},{20,16},{24,28},{28,24},{1,5},{5... | collective-permute-start | bytes 196616 | tf_op jit(solution)/shard_map/sum_weight/ppermute | solution.py:27
  32.2 0.0 collective-permute-start.15
  32.2 0.0 collective-permute-done.14.refs_1_
  32.2 0.5 collective-permute-start.16
  32.8 2.4 %collective-permute-done.10 = bf16[128,256]{1,0:T(8,128)(2,1)S(1)} collective-permute-done((bf16[128,256]{1,0:T(8,128)(2,1)S(1)}, bf16[128,256]{1,0:T(8,128)(2,1)S(1)}, u32[]{:S(2)}, u32[]{:S(2)}) %collective-permute-start.10) | collective-permute-done | bytes 65568 | tf_op jit(solution)/shard_map/sum_weight/ppermute | solution.py:27
  35.1 1.1 %collective-permute-start.11 = (bf16[128,256]{1,0:T(8,128)(2,1)S(1)}, bf16[128,256]{1,0:T(8,128)(2,1)S(1)}, u32[]{:S(2)}, u32[]{:S(2)}) collective-permute-start(bf16[128,256]{1,0:T(8,128)(2,1)S(1)} %add_convert_fusion.4), channel_id=1, source_target_pairs={{0,8},{4,12},{8,0},{12,4},{16,24},{20,28},{24,16},{28,20},{1,9},{5... | collective-permute-start | bytes 196616 | tf_op jit(solution)/shard_map/sum_weight/ppermute | solution.py:27
  36.2 0.0 collective-permute-done.15.refs_2_
  36.2 0.0 collective-permute-done.16.refs_3_
  36.2 0.9 %backward_blocks.1 = (bf16[256,256]{1,0:T(8,128)(2,1)S(1)}, bf16[256,256]{1,0:T(8,128)(2,1)S(1)}, bf16[256,256]{1,0:T(8,128)(2,1)S(1)}, bf16[256,256]{1,0:T(8,128)(2,1)S(1)}) custom-call(s32[13]{0:T(128)S(1)} %pad_add_fusion.info, bf16[6,128,128]{2,1,0:T(8,128)(2,1)S(1)} %bitcast.15, bf16[128,256]{1,0:T(8,128)(2,1)S(1)} %get-tuple-element.18.refs_0_, ...), custom_call_target="tpu_custom_call" | custom-call | tf_op jit(solution)/shard_map/backward_blocks/pallas_call | solution.py:174
  37.1 0.5 collective-permute-start.18
  37.6 1.6 %collective-permute-start.17 = (bf16[256,256]{1,0:T(8,128)(2,1)S(1)}, bf16[256,256]{1,0:T(8,128)(2,1)S(1)}, u32[]{:S(2)}, u32[]{:S(2)}) collective-permute-start(bf16[256,256]{1,0:T(8,128)(2,1)S(1)} %get-tuple-element.20), channel_id=1, source_target_pairs={{0,4},{4,0},{8,12},{12,8},{16,20},{20,16},{24,28},{28,24},{1,5},{5... | collective-permute-start | bytes 393224 | tf_op jit(solution)/shard_map/sum_columns/ppermute | solution.py:27
  39.2 0.2 collective-permute-done.11
  39.5 3.9 %collective-permute-start.12 = (bf16[128,256]{1,0:T(8,128)(2,1)S(1)}, bf16[128,256]{1,0:T(8,128)(2,1)S(1)}, u32[]{:S(2)}, u32[]{:S(2)}) collective-permute-start(bf16[128,256]{1,0:T(8,128)(2,1)S(1)} %add_convert_fusion.3), channel_id=1, source_target_pairs={{0,16},{4,20},{8,24},{12,28},{16,0},{20,4},{24,8},{28,12},{1,17},{... | collective-permute-start | bytes 196616 | tf_op jit(solution)/shard_map/sum_weight/ppermute | solution.py:27
  43.4 0.0 collective-permute-done.18
  43.4 2.9 %collective-permute-start.19 = (bf16[128,256]{1,0:T(8,128)(2,1)S(1)}, bf16[128,256]{1,0:T(8,128)(2,1)S(1)}, u32[]{:S(2)}, u32[]{:S(2)}) collective-permute-start(bf16[128,256]{1,0:T(8,128)(2,1)S(1)} %get-tuple-element.23), channel_id=1, source_target_pairs={{0,16},{4,20},{8,24},{12,28},{16,0},{20,4},{24,8},{28,12},{1,17},{... | collective-permute-start | bytes 196616 | tf_op jit(solution)/shard_map/sum_columns/ppermute | solution.py:27
  46.3 0.1 collective-permute-start.20
  46.4 0.0 collective-permute-done.17
  46.4 0.6 %collective-permute-start.21 = (bf16[128,256]{1,0:T(8,128)(2,1)S(1)}, bf16[128,256]{1,0:T(8,128)(2,1)S(1)}, u32[]{:S(2)}, u32[]{:S(2)}) collective-permute-start(bf16[128,256]{1,0:T(8,128)(2,1)S(1)} %add_convert_fusion), channel_id=1, source_target_pairs={{0,8},{4,12},{8,0},{12,4},{16,24},{20,28},{24,16},{28,20},{1,9},{5... | collective-permute-start | bytes 196616 | tf_op jit(solution)/shard_map/sum_columns/ppermute | solution.py:27
  47.0 0.2 collective-permute-done.12
  47.3 0.1 collective-permute-start.13
  47.4 2.0 %collective-permute-done.19 = bf16[128,256]{1,0:T(8,128)(2,1)S(1)} collective-permute-done((bf16[128,256]{1,0:T(8,128)(2,1)S(1)}, bf16[128,256]{1,0:T(8,128)(2,1)S(1)}, u32[]{:S(2)}, u32[]{:S(2)}) %collective-permute-start.19) | collective-permute-done | bytes 65568 | tf_op jit(solution)/shard_map/sum_columns/ppermute | solution.py:27
  49.3 3.0 %collective-permute-done.20 = bf16[128,256]{1,0:T(8,128)(2,1)S(1)} collective-permute-done((bf16[128,256]{1,0:T(8,128)(2,1)S(1)}, bf16[128,256]{1,0:T(8,128)(2,1)S(1)}, u32[]{:S(2)}, u32[]{:S(2)}) %collective-permute-start.20) | collective-permute-done | bytes 65568 | tf_op jit(solution)/shard_map/sum_columns/ppermute | solution.py:27
  52.4 0.0 collective-permute-done.21
  52.4 0.7 %add_bitcast_fusion = f32[1,128,256]{2,1,0:T(8,128)} fusion(bf16[128,256]{1,0:T(8,128)(2,1)S(1)} %collective-permute-done.21, bf16[128,256]{1,0:T(8,128)(2,1)S(1)} %collective-permute-done.20, bf16[128,256]{1,0:T(8,128)(2,1)S(1)} %collective-permute-done.19, bf16[256,256]{1,0:T(8,128)(2,1)S(1)} %collective-permute-done.17, ...), kind=kLoop, calls=%fused_computation.3 | loop fusion | flops 294912 | bytes 458752 | tf_op jit(solution)/shard_map/broadcast_in_dim | solution.py:214
  53.1 0.0 collective-permute-done.13
  53.1 0.7 %maximum_select_fusion = f32[256,256]{1,0:T(8,128)} fusion(f32[128,256]{1,0:T(8,128)S(1)} %collective-permute-done.13, f32[128,256]{1,0:T(8,128)S(1)} %convert_add_fusion, pred[]{:T(512)S(6)} %eq.3), kind=kLoop, calls=%fused_computation.1 | loop fusion | flops 196608 | bytes 524289 | tf_op jit(solution)/shard_map/sum_weight/jit(_where)/select_n | solution.py:211
  (10 shorter events, 0.2 us)
Async XLA Ops:
  0.6 16.4 %copy-start = (bf16[1,1,6,128,128]{4,3,2,1,0:T(8,128)(2,1)S(1)}, bf16[1,1,6,128,128]{4,3,2,1,0:T(8,128)(2,1)}, u32[]{:S(2)}) copy-start(bf16[1,1,6,128,128]{4,3,2,1,0:T(8,128)(2,1)} %param.13) | copy-start | bytes 589828
  0.6 5.7 %collective-permute-start = (bf16[128,256]{1,0:T(8,128)(2,1)}, bf16[128,256]{1,0:T(8,128)(2,1)S(1)}, u32[]{:S(2)}, u32[]{:S(2)}) collective-permute-start(bf16[128,256]{1,0:T(8,128)(2,1)} %bitcast.16), channel_id=1, source_target_pairs={{0,8},{4,12},{8,0},{12,4},{16,24},{20,28},{24,16},{28,20},{1,9},{5... | collective-permute-start | bytes 196616 | tf_op jit(solution)/shard_map/gather_features/ppermute | solution.py:27
  3.7 7.5 %collective-permute-start.2 = (bf16[128,256]{1,0:T(8,128)(2,1)}, bf16[128,256]{1,0:T(8,128)(2,1)S(1)}, u32[]{:S(2)}, u32[]{:S(2)}) collective-permute-start(bf16[128,256]{1,0:T(8,128)(2,1)} %bitcast.17), channel_id=1, source_target_pairs={{0,16},{4,20},{8,24},{12,28},{16,0},{20,4},{24,8},{28,12},{1,17},{... | collective-permute-start | bytes 196616 | tf_op jit(solution)/shard_map/gather_features/ppermute | solution.py:27
  6.3 6.4 %collective-permute-start.4 = (bf16[128,256]{1,0:T(8,128)(2,1)}, bf16[128,256]{1,0:T(8,128)(2,1)S(1)}, u32[]{:S(2)}, u32[]{:S(2)}) collective-permute-start(bf16[128,256]{1,0:T(8,128)(2,1)} %bitcast.18), channel_id=1, source_target_pairs={{0,24},{4,28},{8,16},{12,20},{16,8},{20,12},{24,0},{28,4},{1,25},{... | collective-permute-start | bytes 196616 | tf_op jit(solution)/shard_map/gather_features/ppermute | solution.py:27
  6.3 2.8 %copy-start.4 = (s32[1,1,6]{2,1,0:T(1,128)S(1)}, s32[1,1,6]{2,1,0:T(1,128)}, u32[]{:S(2)}) copy-start(s32[1,1,6]{2,1,0:T(1,128)} %param.11) | copy-start | bytes 76
  6.3 2.8 %copy-start.5 = (s32[1,1,6]{2,1,0:T(1,128)S(1)}, s32[1,1,6]{2,1,0:T(1,128)}, u32[]{:S(2)}) copy-start(s32[1,1,6]{2,1,0:T(1,128)} %param.10) | copy-start | bytes 76
  6.3 10.7 %copy-start.1 = (bf16[1,128,256]{2,1,0:T(8,128)(2,1)S(1)}, bf16[1,128,256]{2,1,0:T(8,128)(2,1)}, u32[]{:S(2)}) copy-start(bf16[1,128,256]{2,1,0:T(8,128)(2,1)} %param.7) | copy-start | bytes 196612
  7.3 9.7 %collective-permute-start.1 = (bf16[256,256]{1,0:T(8,128)(2,1)S(1)}, bf16[256,256]{1,0:T(8,128)(2,1)S(1)}, u32[]{:S(2)}, u32[]{:S(2)}) collective-permute-start(bf16[256,256]{1,0:T(8,128)(2,1)S(1)} %pad_maximum_fusion), channel_id=1, source_target_pairs={{0,4},{4,0},{8,12},{12,8},{16,20},{20,16},{24,28},{28,24},{1,5},{5... | collective-permute-start | bytes 393224 | tf_op jit(solution)/shard_map/gather_features/ppermute | solution.py:27
  11.2 4.3 %collective-permute-start.3 = (bf16[128,256]{1,0:T(8,128)(2,1)S(1)}, bf16[128,256]{1,0:T(8,128)(2,1)S(1)}, u32[]{:S(2)}, u32[]{:S(2)}) collective-permute-start(bf16[128,256]{1,0:T(8,128)(2,1)S(1)} %collective-permute-done.2.refs_3_), channel_id=1, source_target_pairs={{0,4},{4,0},{8,12},{12,8},{16,20},{20,16},{24,28},{28,24},{1,5},{5... | collective-permute-start | bytes 196616 | tf_op jit(solution)/shard_map/gather_features/ppermute | solution.py:27
  12.7 4.3 %collective-permute-start.5 = (bf16[128,256]{1,0:T(8,128)(2,1)S(1)}, bf16[128,256]{1,0:T(8,128)(2,1)S(1)}, u32[]{:S(2)}, u32[]{:S(2)}) collective-permute-start(bf16[128,256]{1,0:T(8,128)(2,1)S(1)} %collective-permute-done.4.refs_5_), channel_id=1, source_target_pairs={{0,4},{4,0},{8,12},{12,8},{16,20},{20,16},{24,28},{28,24},{1,5},{5... | collective-permute-start | bytes 196616 | tf_op jit(solution)/shard_map/gather_features/ppermute | solution.py:27
  17.8 5.8 %copy-start.2 = (bf16[256,256]{1,0:T(8,128)(2,1)S(1)}, bf16[256,256]{1,0:T(8,128)(2,1)}, u32[]{:S(2)}) copy-start(bf16[256,256]{1,0:T(8,128)(2,1)} %weight.1) | copy-start | bytes 393220
  17.8 1.4 %collective-permute-start.6 = (bf16[256,256]{1,0:T(8,128)(2,1)S(1)}, bf16[256,256]{1,0:T(8,128)(2,1)S(1)}, u32[]{:S(2)}, u32[]{:S(2)}) collective-permute-start(bf16[256,256]{1,0:T(8,128)(2,1)S(1)} %get-tuple-element.14), channel_id=1, source_target_pairs={{0,1},{1,0},{2,3},{3,2},{4,5},{5,4},{6,7},{7,6},{8,9},{9,8},{10,11... | collective-permute-start | bytes 393224 | tf_op jit(solution)/shard_map/sum_rows/ppermute | solution.py:27
  19.3 4.4 %copy-start.3 = (bf16[1,128,256]{2,1,0:T(8,128)(2,1)S(1)}, bf16[1,128,256]{2,1,0:T(8,128)(2,1)}, u32[]{:S(2)}) copy-start(bf16[1,128,256]{2,1,0:T(8,128)(2,1)} %param.9) | copy-start | bytes 196612
  19.3 4.3 %collective-permute-start.7 = (bf16[128,256]{1,0:T(8,128)(2,1)S(1)}, bf16[128,256]{1,0:T(8,128)(2,1)S(1)}, u32[]{:S(2)}, u32[]{:S(2)}) collective-permute-start(bf16[128,256]{1,0:T(8,128)(2,1)S(1)} %add_convert_fusion.7), channel_id=1, source_target_pairs={{0,2},{1,3},{2,0},{3,1},{4,6},{5,7},{6,4},{7,5},{8,10},{9,11},{10,... | collective-permute-start | bytes 196616 | tf_op jit(solution)/shard_map/sum_rows/ppermute | solution.py:27
  24.7 1.3 %collective-permute-start.8 = (bf16[128,256]{1,0:T(8,128)(2,1)S(1)}, bf16[128,256]{1,0:T(8,128)(2,1)S(1)}, u32[]{:S(2)}, u32[]{:S(2)}) collective-permute-start(bf16[128,256]{1,0:T(8,128)(2,1)S(1)} %broadcast_select_fusion), channel_id=1, source_target_pairs={{0,1},{1,0},{2,3},{3,2},{4,5},{5,4},{6,7},{7,6},{8,9},{9,8},{10,11... | collective-permute-start | bytes 196616 | tf_op jit(solution)/shard_map/sum_weight/ppermute | solution.py:27
  26.0 4.7 %collective-permute-start.9 = (bf16[128,256]{1,0:T(8,128)(2,1)S(1)}, bf16[128,256]{1,0:T(8,128)(2,1)S(1)}, u32[]{:S(2)}, u32[]{:S(2)}) collective-permute-start(bf16[128,256]{1,0:T(8,128)(2,1)S(1)} %add_convert_fusion.6), channel_id=1, source_target_pairs={{0,2},{1,3},{2,0},{3,1},{4,6},{5,7},{6,4},{7,5},{8,10},{9,11},{10,... | collective-permute-start | bytes 196616 | tf_op jit(solution)/shard_map/sum_weight/ppermute | solution.py:27
  27.6 4.7 %collective-permute-start.14 = (bf16[128,256]{1,0:T(8,128)(2,1)S(1)}, bf16[128,256]{1,0:T(8,128)(2,1)S(1)}, u32[]{:S(2)}, u32[]{:S(2)}) collective-permute-start(bf16[128,256]{1,0:T(8,128)(2,1)S(1)} %get-tuple-element.18.refs_0_), channel_id=1, source_target_pairs={{0,2},{1,3},{2,0},{3,1},{4,6},{5,7},{6,4},{7,5},{8,10},{9,11},{10,... | collective-permute-start | bytes 196616 | tf_op jit(solution)/shard_map/gather_grad_hidden/ppermute | solution.py:27
  30.8 4.3 %collective-permute-start.10 = (bf16[128,256]{1,0:T(8,128)(2,1)S(1)}, bf16[128,256]{1,0:T(8,128)(2,1)S(1)}, u32[]{:S(2)}, u32[]{:S(2)}) collective-permute-start(bf16[128,256]{1,0:T(8,128)(2,1)S(1)} %add_convert_fusion.5), channel_id=1, source_target_pairs={{0,4},{4,0},{8,12},{12,8},{16,20},{20,16},{24,28},{28,24},{1,5},{5... | collective-permute-start | bytes 196616 | tf_op jit(solution)/shard_map/sum_weight/ppermute | solution.py:27
  32.2 4.0 %collective-permute-start.15 = (bf16[128,256]{1,0:T(8,128)(2,1)S(1)}, bf16[128,256]{1,0:T(8,128)(2,1)S(1)}, u32[]{:S(2)}, u32[]{:S(2)}) collective-permute-start(bf16[128,256]{1,0:T(8,128)(2,1)S(1)} %get-tuple-element.18.refs_0_), channel_id=1, source_target_pairs={{0,1},{1,0},{2,3},{3,2},{4,5},{5,4},{6,7},{7,6},{8,9},{9,8},{10,11... | collective-permute-start | bytes 196616 | tf_op jit(solution)/shard_map/gather_grad_hidden/ppermute | solution.py:27
  32.2 4.0 %collective-permute-start.16 = (bf16[128,256]{1,0:T(8,128)(2,1)S(1)}, bf16[128,256]{1,0:T(8,128)(2,1)S(1)}, u32[]{:S(2)}, u32[]{:S(2)}) collective-permute-start(bf16[128,256]{1,0:T(8,128)(2,1)S(1)} %collective-permute-done.14.refs_1_), channel_id=1, source_target_pairs={{0,1},{1,0},{2,3},{3,2},{4,5},{5,4},{6,7},{7,6},{8,9},{9,8},{10,11... | collective-permute-start | bytes 196616 | tf_op jit(solution)/shard_map/gather_grad_hidden/ppermute | solution.py:27
  35.1 4.3 %collective-permute-start.11 = (bf16[128,256]{1,0:T(8,128)(2,1)S(1)}, bf16[128,256]{1,0:T(8,128)(2,1)S(1)}, u32[]{:S(2)}, u32[]{:S(2)}) collective-permute-start(bf16[128,256]{1,0:T(8,128)(2,1)S(1)} %add_convert_fusion.4), channel_id=1, source_target_pairs={{0,8},{4,12},{8,0},{12,4},{16,24},{20,28},{24,16},{28,20},{1,9},{5... | collective-permute-start | bytes 196616 | tf_op jit(solution)/shard_map/sum_weight/ppermute | solution.py:27
  37.1 6.2 %collective-permute-start.18 = (bf16[256,256]{1,0:T(8,128)(2,1)S(1)}, bf16[256,256]{1,0:T(8,128)(2,1)S(1)}, u32[]{:S(2)}, u32[]{:S(2)}) collective-permute-start(bf16[256,256]{1,0:T(8,128)(2,1)S(1)} %get-tuple-element.22), channel_id=1, source_target_pairs={{0,4},{4,0},{8,12},{12,8},{16,20},{20,16},{24,28},{28,24},{1,5},{5... | collective-permute-start | bytes 393224 | tf_op jit(solution)/shard_map/sum_columns/ppermute | solution.py:27
  37.6 8.8 %collective-permute-start.17 = (bf16[256,256]{1,0:T(8,128)(2,1)S(1)}, bf16[256,256]{1,0:T(8,128)(2,1)S(1)}, u32[]{:S(2)}, u32[]{:S(2)}) collective-permute-start(bf16[256,256]{1,0:T(8,128)(2,1)S(1)} %get-tuple-element.20), channel_id=1, source_target_pairs={{0,4},{4,0},{8,12},{12,8},{16,20},{20,16},{24,28},{28,24},{1,5},{5... | collective-permute-start | bytes 393224 | tf_op jit(solution)/shard_map/sum_columns/ppermute | solution.py:27
  39.5 7.8 %collective-permute-start.12 = (bf16[128,256]{1,0:T(8,128)(2,1)S(1)}, bf16[128,256]{1,0:T(8,128)(2,1)S(1)}, u32[]{:S(2)}, u32[]{:S(2)}) collective-permute-start(bf16[128,256]{1,0:T(8,128)(2,1)S(1)} %add_convert_fusion.3), channel_id=1, source_target_pairs={{0,16},{4,20},{8,24},{12,28},{16,0},{20,4},{24,8},{28,12},{1,17},{... | collective-permute-start | bytes 196616 | tf_op jit(solution)/shard_map/sum_weight/ppermute | solution.py:27
  43.4 5.9 %collective-permute-start.19 = (bf16[128,256]{1,0:T(8,128)(2,1)S(1)}, bf16[128,256]{1,0:T(8,128)(2,1)S(1)}, u32[]{:S(2)}, u32[]{:S(2)}) collective-permute-start(bf16[128,256]{1,0:T(8,128)(2,1)S(1)} %get-tuple-element.23), channel_id=1, source_target_pairs={{0,16},{4,20},{8,24},{12,28},{16,0},{20,4},{24,8},{28,12},{1,17},{... | collective-permute-start | bytes 196616 | tf_op jit(solution)/shard_map/sum_columns/ppermute | solution.py:27
  46.3 6.1 %collective-permute-start.20 = (bf16[128,256]{1,0:T(8,128)(2,1)S(1)}, bf16[128,256]{1,0:T(8,128)(2,1)S(1)}, u32[]{:S(2)}, u32[]{:S(2)}) collective-permute-start(bf16[128,256]{1,0:T(8,128)(2,1)S(1)} %get-tuple-element.24), channel_id=1, source_target_pairs={{0,24},{4,28},{8,16},{12,20},{16,8},{20,12},{24,0},{28,4},{1,25},{... | collective-permute-start | bytes 196616 | tf_op jit(solution)/shard_map/sum_columns/ppermute | solution.py:27
  46.4 6.0 %collective-permute-start.21 = (bf16[128,256]{1,0:T(8,128)(2,1)S(1)}, bf16[128,256]{1,0:T(8,128)(2,1)S(1)}, u32[]{:S(2)}, u32[]{:S(2)}) collective-permute-start(bf16[128,256]{1,0:T(8,128)(2,1)S(1)} %add_convert_fusion), channel_id=1, source_target_pairs={{0,8},{4,12},{8,0},{12,4},{16,24},{20,28},{24,16},{28,20},{1,9},{5... | collective-permute-start | bytes 196616 | tf_op jit(solution)/shard_map/sum_columns/ppermute | solution.py:27
  47.3 5.8 %collective-permute-start.13 = (f32[128,256]{1,0:T(8,128)S(1)}, f32[128,256]{1,0:T(8,128)S(1)}, u32[]{:S(2)}, u32[]{:S(2)}) collective-permute-start(f32[128,256]{1,0:T(8,128)S(1)} %convert_add_fusion), channel_id=1, source_target_pairs={{0,1},{1,0},{2,3},{3,2},{4,5},{5,4},{6,7},{7,6},{8,9},{9,8},{10,11... | collective-permute-start | bytes 393224 | tf_op jit(solution)/shard_map/sum_weight/ppermute | solution.py:27

commit v2 on v1

v2 whole, which is shorter than its diff:
```python
import functools

import jax
import jax.numpy as jnp
from jax import lax
from jax.experimental import pallas as pl
from jax.experimental.pallas import tpu as pltpu
from jax.sharding import PartitionSpec as P

VMEM = pl.BlockSpec(memory_space=pltpu.VMEM)
SMEM = pl.BlockSpec(memory_space=pltpu.SMEM)
FULL = (((1,), (0,)), ((), ()))
LEFT_T = (((0,), (0,)), ((), ()))
RIGHT_T = (((1,), (1,)), ((), ()))


def f32(value):
    return value.astype(jnp.float32)


def bf16(value):
    return value.astype(jnp.bfloat16)


def swap(value, axis, mask):
    size = lax.axis_size(axis)
    return lax.ppermute(value, axis, [(i, i ^ mask) for i in range(size)])


def bits_of(axis):
    return [1 << b for b in range(lax.axis_size(axis).bit_length() - 1)]


def after(value, *deps):
    return lax.optimization_barrier((value, *deps))[0]


class Line:
    def __init__(self):
        self.last = None

    def __call__(self, value):
        self.last = value if self.last is None else after(value, self.last)
        return self.last


def params(nbytes):
    return pltpu.CompilerParams(vmem_limit_bytes=nbytes)


def slot_products(transposed, info, values, source, total):
    slots = values.shape[0]
    count = info[2, 0]
    dims = LEFT_T if transposed else FULL

    def place(s):
        row, col = info[0, s], info[1, s]
        return (row, col) if transposed else (col, row)

    def product(s):
        return lax.dot_general(
            values[s], source[place(s)[0]], dims, preferred_element_type=jnp.float32
        )

    total[...] = jnp.zeros_like(total)
    if slots <= 8:
        products = [product(s) for s in range(slots)]
        for s in range(slots):
            total[place(s)[1]] += jnp.where(s < count, products[s], 0.0)
    else:

        def one(s, _):
            total[place(s)[1]] += product(s)
            return 0

        lax.fori_loop(0, count, one, 0)


def info_kernel(rows, cols, counts, info):
    slots = rows.shape[1]
    info[...] = jnp.zeros_like(info)
    info[0:1, pl.ds(0, slots)] = rows[...] ^ lax.axis_index("gc")
    info[1:2, pl.ds(0, slots)] = cols[...] ^ lax.axis_index("gr")
    info[2:3, pl.ds(0, 1)] = counts[...]


def forward_kernel(layout, send_masks, keep_masks, info, values, *refs):
    pieces, (send, keep, source, total) = refs[: len(layout)], refs[len(layout):]
    side = values.shape[1]
    for masks, piece in zip(layout, pieces):
        for n, m in enumerate(masks):
            source[m] = piece[pl.ds(n * side, side), :]
    slot_products(False, info, values, source, total)
    for n, m in enumerate(send_masks):
        send[pl.ds(n * side, side), :] = bf16(total[m])
    for n, m in enumerate(keep_masks):
        keep[pl.ds(n * side, side), :] = bf16(total[m])


def backward_kernel(layout, out_layout, info, values, *refs):
    pieces, rest = refs[: len(layout)], refs[len(layout):]
    outs, (source, total) = rest[: len(out_layout)], rest[len(out_layout):]
    side = values.shape[1]
    for masks, piece in zip(layout, pieces):
        for n, m in enumerate(masks):
            source[m] = piece[pl.ds(n * side, side), :]
    slot_products(True, info, values, source, total)
    for masks, out in zip(out_layout, outs):
        for n, m in enumerate(masks):
            out[pl.ds(n * side, side), :] = bf16(total[m])


def dense_kernel(bit, mine, got, weight, *refs):
    *grads, activated, message, kept, total = refs
    side, half = activated.shape[0], kept.shape[0]
    blocks = mine.shape[0] // side
    w = weight[...]
    summed = [
        f32(mine[pl.ds(e * side, side), :]) + f32(got[pl.ds((e ^ bit) * side, side), :])
        for e in range(blocks)
    ]
    hidden = bf16(jnp.concatenate(summed))
    pre = lax.dot_general(hidden, w, FULL, preferred_element_type=jnp.float32)
    s = 1.0 / (1.0 + jnp.exp(-pre))
    activated[...] = bf16(pre[:side] * s[:side])
    grad_out = jnp.concatenate([f32(g[...]) for g in grads])
    grad_pre = bf16(grad_out * s * (1.0 + pre * (1.0 - s)))
    message[pl.ds(0, blocks * side), :] = bf16(
        lax.dot_general(grad_pre, w, RIGHT_T, preferred_element_type=jnp.float32)
    )
    total[...] = lax.dot_general(hidden, grad_pre, LEFT_T, preferred_element_type=jnp.float32)
    place = lax.axis_index("gc") & 1
    kept[...] = total[pl.ds(pl.multiple_of(place * half, half), half), :]
    message[pl.ds(blocks * side, half), :] = bf16(
        total[pl.ds(pl.multiple_of((1 - place) * half, half), half), :]
    )


def finish_kernel(mine, other, *refs):
    (kept, part, *terms), (grad_features, grad_weight) = refs[:-2], refs[-2:]
    side = grad_features.shape[0]
    parts = [f32(v[pl.ds(side, side), :]) for v in (kept, part)] + [f32(t[...]) for t in terms]
    grad_features[...] = functools.reduce(lambda a, b: a + b, parts)
    half = mine.shape[0]
    place = lax.axis_index("gc") & 1
    grad_weight[pl.ds(pl.multiple_of(place * half, half), half), :] = f32(mine[...])
    grad_weight[pl.ds(pl.multiple_of((1 - place) * half, half), half), :] = f32(other[...])


def per_device(features, weight, grad_out, block_rows, block_cols, block_counts, block_values):
    side, width = features.shape[1:]
    gr_size, gc_size = lax.axis_size("gr"), lax.axis_size("gc")
    outer = [m for m in range(0, gr_size, 2)]
    far_first = sorted(outer[2:]) + [2]
    block = jax.ShapeDtypeStruct((side, width), jnp.bfloat16)

    def stacked(n):
        return jax.ShapeDtypeStruct((n * side, width), jnp.bfloat16)

    limit = 48 * 2**20
    with jax.named_scope("gather_features"):
        x = features[0]
        moved = {m: swap(x, "gr", m) for m in far_first + [1]}
        arrival = Line()
        held = {}
        for m in far_first[:1] + [2] + far_first[1:-1] + [1]:
            held[m] = arrival(moved[m])
            if m > 1:
                moved[m + 1] = swap(held[m], "gr", 1)
        values = block_values[0, 0]
        info = pl.pallas_call(
            info_kernel,
            out_shape=jax.ShapeDtypeStruct((8, 128 * pl.cdiv(values.shape[0], 128)), jnp.int32),
            in_specs=[VMEM] * 3,
            out_specs=VMEM,
            compiler_params=params(limit),
            cost_estimate=pl.CostEstimate(flops=5 * 10**9, bytes_accessed=0, transcendentals=0),
        )(after(block_rows[0], held[2]), block_cols[0], block_counts)
        grads = {0: after(grad_out[0], held[1])}
        for bit in bits_of("gc")[1:]:
            grads.update({m | bit: swap(v, "gc", bit) for m, v in list(grads.items())})
        grads = {m: arrival(v) for m, v in grads.items()}
        for m in (far_first[:1] + [2] + far_first[1:-1])[::-1]:
            held[m + 1] = arrival(moved[m + 1])
        held[0] = x
    layout = [(m,) for m in held]
    pieces = list(held.values())
    pieces[0] = after(pieces[0], *grads.values())

    with jax.named_scope("forward_blocks"):
        send_masks = [m for m in range(gc_size) if m & 1]
        keep_masks = [m for m in range(gc_size) if not m & 1]
        send, keep = pl.pallas_call(
            functools.partial(forward_kernel, layout, send_masks, keep_masks),
            out_shape=[stacked(len(send_masks)), stacked(len(keep_masks))],
            in_specs=[SMEM] + [VMEM] * (1 + len(pieces)),
            out_specs=[VMEM, VMEM],
            scratch_shapes=[
                pltpu.VMEM((gr_size, side, width), jnp.bfloat16),
                pltpu.VMEM((gc_size, side, width), jnp.float32),
            ],
            compiler_params=params(limit),
        )(info, values, *pieces)

    with jax.named_scope("sum_rows"):
        near = swap(send, "gc", 1)
        mine = bf16(f32(keep) + f32(near))
        *bits, last = bits_of("gc")[1:]
        for bit in bits:
            order = jnp.arange(len(keep_masks)) ^ (bit >> 1)
            got = swap(mine, "gc", bit).reshape(-1, side, width)[order].reshape(mine.shape)
            mine = bf16(f32(mine) + f32(got))
        got = swap(mine, "gc", last)

    half = width // 2
    with jax.named_scope("dense"):
        activated, message, kept = pl.pallas_call(
            functools.partial(dense_kernel, last >> 1),
            out_shape=[
                block,
                jax.ShapeDtypeStruct((mine.shape[0] + half, width), jnp.bfloat16),
                jax.ShapeDtypeStruct((half, width), jnp.float32),
            ],
            in_specs=[VMEM] * (3 + len(grads)),
            out_specs=[VMEM] * 3,
            scratch_shapes=[pltpu.VMEM((width, width), jnp.float32)],
            compiler_params=params(limit),
        )(mine, got, weight, *[grads[m] for m in keep_masks])

    with jax.named_scope("swap_cores"):
        answer = swap(message, "gc", 1)
        running = kept + f32(answer[mine.shape[0]:])
    stages = [("gr", bit) for bit in bits_of("gr")[:0:-1] + [1]]
    sent, got, order = [], [], Line()

    def launch(running):
        with jax.named_scope("sum_weight"):
            sent.append(bf16(running))
            got.append(swap(sent[-1], *stages[len(sent) - 1]))

    def advance():
        if len(sent) > len(stages):
            return
        with jax.named_scope("sum_weight"):
            running = f32(sent[-1]) + f32(order(got[-1]))
            if len(sent) < len(stages):
                launch(running)
            else:
                sent.append(bf16(running))
                got.append(swap(sent[-1], "gc", 1))

    launch(running)

    with jax.named_scope("backward_blocks"):
        kept_masks = [(m,) for m in far_first[:-1]] + [(2, 0)]
        out_layout = [tuple(m + 1 for m in masks) for masks in kept_masks] + kept_masks
        outs = pl.pallas_call(
            functools.partial(backward_kernel, [keep_masks, send_masks], out_layout),
            out_shape=[stacked(len(masks)) for masks in out_layout],
            in_specs=[SMEM] + [VMEM] * 3,
            out_specs=[VMEM] * len(out_layout),
            scratch_shapes=[
                pltpu.VMEM((gc_size, side, width), jnp.bfloat16),
                pltpu.VMEM((gr_size, side, width), jnp.float32),
            ],
            compiler_params=params(limit),
        )(info, values, message, answer)
        sends, keeps = outs[: len(kept_masks)], outs[len(kept_masks):]

    with jax.named_scope("sum_columns"):
        arrived = [swap(v, "gr", 1) for v in sends]
        order(keeps[0])
        advance()
        terms = []
        for masks, kept, part in zip(kept_masks[:-1], keeps, arrived):
            total = bf16(f32(kept) + f32(order(part)))
            terms.append(swap(total, "gr", masks[0]))
        advance()
        own = (keeps[-1], order(arrived[-1]))
        total = bf16(f32(own[0][:side]) + f32(own[1][:side]))
        terms.append(swap(total, "gr", 2))
    while len(sent) <= len(stages):
        advance()
    terms = [order(term) for term in terms]
    running, other = sent[-1], order(got[-1])

    grad_features, grad_weight = pl.pallas_call(
        finish_kernel,
        out_shape=[
            jax.ShapeDtypeStruct((side, width), jnp.float32),
            jax.ShapeDtypeStruct((width, width), jnp.float32),
        ],
        in_specs=[VMEM] * (4 + len(terms)),
        out_specs=[VMEM] * 2,
        compiler_params=params(limit),
    )(running, other, *own, *terms)
    return activated[None], grad_weight, grad_features[None]


def solution(mesh):
    placed = (
        P("gc", "gr", None),
        P(),
        P("gr", "gc", None),
        P("gr", "gc", None),
        P("gr", "gc", None),
        P("gr", "gc"),
        P("gr", "gc", None, None, None),
    )
    return jax.shard_map(
        per_device,
        mesh=mesh,
        in_specs=placed,
        out_specs=(P("gr", "gc", None), P(), P("gc", "gr", None)),
        check_vma=False,
    )
```

time: 53.3 us -> 48.5 us (0.910); the launches traced: 53.8 us -> 48.3 us
  starting transfers between devices: 26.9 us -> 23.8 us
  other arithmetic: 2.61 us -> 0.16 us
  Pallas kernels: 2.5 us -> 3.53 us
  waiting for transfers between devices: 20.1 us -> 19.4 us
    ppermute x22 -> x21, starting transfers between devices: 26.9 us -> 23.8 us  [swap(): return lax.ppermute(value, axis, [(i, i ^ mask) for i in range(size)])]
    concatenate x2 -> x0, other arithmetic: 1 us -> none  [the longest x1 0.93 us: per_device(): near = swap(jnp.concatenate([x, direct[2]], axis=0), 'gr', 1)]
    pallas_call x2 -> x4, Pallas kernels: 1.7 us -> 2.61 us  [the longest x1 0.95 us: per_device(): pl.pallas_call(functools.partial(backward_kernel, [keep_masks, send_masks...]
    select_n x2 -> x0, other arithmetic: 0.74 us -> none  [the longest x1 0.72 us: per_device(): jnp.where(upper, jnp.concatenate([running, other]), jnp.concatenate([othe...]
    broadcast_in_dim x1 -> x0, other arithmetic: 0.7 us -> none  [per_device(): return (activated[None], grad_weight, grad_features[None])]
    ppermute x22 -> x21, waiting for transfers between devices: 20.1 us -> 19.4 us  [swap(): return lax.ppermute(value, axis, [(i, i ^ mask) for i in range(size)])]
  transfers between devices with their start and end apart: 22 -> 21, of which waited for: 12 -> 12; matrix products, arithmetic and copies ran while one was open for 3% -> 0% of each run, Pallas kernels for 2% -> 2%
where the time goes in v2:
time: 48.5 us; the launch traced here: 48.3 us
  starting transfers between devices  23.8 us (49%)
  waiting for transfers between devices  19.4 us (40%)
  Pallas kernels  3.53 us (7%)
  between operations  1.4 us (3%)
    ppermute x21, starting transfers between devices, swap(): return lax.ppermute(value, axis, [(i, i ^ mask) for i in range(size)])  23.8 us
    ppermute x21, waiting for transfers between devices, swap(): return lax.ppermute(value, axis, [(i, i ^ mask) for i in range(size)])  19.4 us
  transfers between devices with their start and end apart: 21, of which 12 were waited for; matrix products, arithmetic and copies ran while one was open for 0% of the time, Pallas kernels for 2%

profile of v2, /device:TPU:0, one launch (start us, length us, event | category | flops | bytes accessed | tf_op | source)
XLA Modules:
  0.0 48.3 jit_solution(15237115278902953482)
XLA Ops:
  0.6 4.1 %collective-permute-start.1 = (bf16[128,256]{1,0:T(8,128)(2,1)}, bf16[128,256]{1,0:T(8,128)(2,1)S(1)}, u32[]{:S(2)}, u32[]{:S(2)}) collective-permute-start(bf16[128,256]{1,0:T(8,128)(2,1)} %bitcast.9), channel_id=1, source_target_pairs={{0,16},{4,20},{8,24},{12,28},{16,0},{20,4},{24,8},{28,12},{1,17},{... | collective-permute-start | bytes 196616 | tf_op jit(solution)/shard_map/gather_features/ppermute | solution.py:27
  4.7 1.6 %collective-permute-start = (bf16[128,256]{1,0:T(8,128)(2,1)}, bf16[128,256]{1,0:T(8,128)(2,1)S(1)}, u32[]{:S(2)}, u32[]{:S(2)}) collective-permute-start(bf16[128,256]{1,0:T(8,128)(2,1)} %bitcast.10), channel_id=1, source_target_pairs={{0,8},{4,12},{8,0},{12,4},{16,24},{20,28},{24,16},{28,20},{1,9},{5... | collective-permute-start | bytes 196616 | tf_op jit(solution)/shard_map/gather_features/ppermute | solution.py:27
  6.3 0.0 collective-permute-start.3
  6.3 1.7 %collective-permute-start.2 = (bf16[128,256]{1,0:T(8,128)(2,1)}, bf16[128,256]{1,0:T(8,128)(2,1)S(1)}, u32[]{:S(2)}, u32[]{:S(2)}) collective-permute-start(bf16[128,256]{1,0:T(8,128)(2,1)} %bitcast.12), channel_id=1, source_target_pairs={{0,4},{4,0},{8,12},{12,8},{16,20},{20,16},{24,28},{28,24},{1,5},{5... | collective-permute-start | bytes 196616 | tf_op jit(solution)/shard_map/gather_features/ppermute | solution.py:27
  8.7 0.0 collective-permute-done.1.refs_0_
  8.7 0.5 %collective-permute-done.refs_1_ = bf16[128,256]{1,0:T(8,128)(2,1)S(1)} collective-permute-done((bf16[128,256]{1,0:T(8,128)(2,1)}, bf16[128,256]{1,0:T(8,128)(2,1)S(1)}, u32[]{:S(2)}, u32[]{:S(2)}) %collective-permute-start) | collective-permute-done | bytes 65568 | tf_op jit(solution)/shard_map/gather_features/ppermute | solution.py:27
  9.2 1.5 %collective-permute-start.6 = (bf16[128,256]{1,0:T(8,128)(2,1)S(1)}, bf16[128,256]{1,0:T(8,128)(2,1)S(1)}, u32[]{:S(2)}, u32[]{:S(2)}) collective-permute-start(bf16[128,256]{1,0:T(8,128)(2,1)S(1)} %collective-permute-done.refs_1_), channel_id=1, source_target_pairs={{0,4},{4,0},{8,12},{12,8},{16,20},{20,16},{24,28},{28,24},{1,5},{5... | collective-permute-start | bytes 196616 | tf_op jit(solution)/shard_map/gather_features/ppermute | solution.py:27
  10.7 1.9 %collective-permute-done.3.refs_2_ = bf16[128,256]{1,0:T(8,128)(2,1)S(1)} collective-permute-done((bf16[128,256]{1,0:T(8,128)(2,1)}, bf16[128,256]{1,0:T(8,128)(2,1)S(1)}, u32[]{:S(2)}, u32[]{:S(2)}) %collective-permute-start.3) | collective-permute-done | bytes 65568 | tf_op jit(solution)/shard_map/gather_features/ppermute | solution.py:27
  12.6 1.5 %collective-permute-start.5 = (bf16[128,256]{1,0:T(8,128)(2,1)S(1)}, bf16[128,256]{1,0:T(8,128)(2,1)S(1)}, u32[]{:S(2)}, u32[]{:S(2)}) collective-permute-start(bf16[128,256]{1,0:T(8,128)(2,1)S(1)} %collective-permute-done.3.refs_2_), channel_id=1, source_target_pairs={{0,4},{4,0},{8,12},{12,8},{16,20},{20,16},{24,28},{28,24},{1,5},{5... | collective-permute-start | bytes 196616 | tf_op jit(solution)/shard_map/gather_features/ppermute | solution.py:27
  14.1 0.0 collective-permute-done.2.refs_3_
  14.1 0.0 copy-start.4
  14.1 0.0 copy-start.5
  14.1 1.5 %collective-permute-start.4 = (bf16[128,256]{1,0:T(8,128)(2,1)}, bf16[128,256]{1,0:T(8,128)(2,1)S(1)}, u32[]{:S(2)}, u32[]{:S(2)}) collective-permute-start(bf16[128,256]{1,0:T(8,128)(2,1)} %bitcast.14), channel_id=1, source_target_pairs={{0,2},{1,3},{2,0},{3,1},{4,6},{5,7},{6,4},{7,5},{8,10},{9,11},{10,... | collective-permute-start | bytes 196616 | tf_op jit(solution)/shard_map/gather_features/ppermute | solution.py:27
  15.6 0.5 %collective-permute-start.7 = (bf16[128,256]{1,0:T(8,128)(2,1)S(1)}, bf16[128,256]{1,0:T(8,128)(2,1)S(1)}, u32[]{:S(2)}, u32[]{:S(2)}) collective-permute-start(bf16[128,256]{1,0:T(8,128)(2,1)S(1)} %collective-permute-done.1.refs_0_), channel_id=1, source_target_pairs={{0,4},{4,0},{8,12},{12,8},{16,20},{20,16},{24,28},{28,24},{1,5},{5... | collective-permute-start | bytes 196616 | tf_op jit(solution)/shard_map/gather_features/ppermute | solution.py:27
  16.1 0.0 copy-done.4
  16.1 0.0 copy-done.5
  16.1 0.0 copy-start
  16.1 0.0 copy-start.2
  16.1 2.4 %collective-permute-done.4.refs_1_ = bf16[128,256]{1,0:T(8,128)(2,1)S(1)} collective-permute-done((bf16[128,256]{1,0:T(8,128)(2,1)}, bf16[128,256]{1,0:T(8,128)(2,1)S(1)}, u32[]{:S(2)}, u32[]{:S(2)}) %collective-permute-start.4) | collective-permute-done | bytes 65568 | tf_op jit(solution)/shard_map/gather_features/ppermute | solution.py:27
  18.6 0.0 collective-permute-done.5.refs_4_
  18.6 0.0 collective-permute-done.6.refs_5_
  18.6 1.3 %collective-permute-done.7.refs_6_ = bf16[128,256]{1,0:T(8,128)(2,1)S(1)} collective-permute-done((bf16[128,256]{1,0:T(8,128)(2,1)S(1)}, bf16[128,256]{1,0:T(8,128)(2,1)S(1)}, u32[]{:S(2)}, u32[]{:S(2)}) %collective-permute-start.7) | collective-permute-done | bytes 65568 | tf_op jit(solution)/shard_map/gather_features/ppermute | solution.py:27
  19.9 0.0 copy-done
  19.9 0.0 copy-done.2
  19.9 0.9 %forward_blocks.1 = (bf16[256,256]{1,0:T(8,128)(2,1)S(1)}, bf16[256,256]{1,0:T(8,128)(2,1)S(1)}) custom-call(s32[8,128]{1,0:T(8,128)S(1)} %gather_features.1.info, bf16[6,128,128]{2,1,0:T(8,128)(2,1)S(1)} %bitcast.7, bf16[128,256]{1,0:T(8,128)(2,1)S(1)} %collective-permute-done.1.refs_0_, bf16[128,256]{1,0:T(8,128)(2,1)S(1)} %collective-permute-done.refs_1_, ...), custom_call_target="tpu_custom_call" | custom-call | tf_op jit(solution)/shard_map/forward_blocks/pallas_call | solution.py:193
  20.8 0.1 collective-permute-start.8
  20.9 1.3 %collective-permute-done.8 = bf16[256,256]{1,0:T(8,128)(2,1)S(1)} collective-permute-done((bf16[256,256]{1,0:T(8,128)(2,1)S(1)}, bf16[256,256]{1,0:T(8,128)(2,1)S(1)}, u32[]{:S(2)}, u32[]{:S(2)}) %collective-permute-start.8) | collective-permute-done | bytes 131104 | tf_op jit(solution)/shard_map/sum_rows/ppermute | solution.py:27
  22.2 0.0 copy-start.1
  22.2 0.0 copy-start.3
  22.3 0.6 %collective-permute-start.9 = (bf16[256,256]{1,0:T(8,128)(2,1)S(1)}, bf16[256,256]{1,0:T(8,128)(2,1)S(1)}, u32[]{:S(2)}, u32[]{:S(2)}) collective-permute-start(bf16[256,256]{1,0:T(8,128)(2,1)S(1)} %add_convert_fusion.mine), channel_id=1, source_target_pairs={{0,2},{1,3},{2,0},{3,1},{4,6},{5,7},{6,4},{7,5},{8,10},{9,11},{10,... | collective-permute-start | bytes 393224 | tf_op jit(solution)/shard_map/sum_rows/ppermute | solution.py:27
  22.9 5.0 %collective-permute-done.9.got = bf16[256,256]{1,0:T(8,128)(2,1)S(1)} collective-permute-done((bf16[256,256]{1,0:T(8,128)(2,1)S(1)}, bf16[256,256]{1,0:T(8,128)(2,1)S(1)}, u32[]{:S(2)}, u32[]{:S(2)}) %collective-permute-start.9) | collective-permute-done | bytes 131104 | tf_op jit(solution)/shard_map/sum_rows/ppermute | solution.py:27
  27.9 0.0 copy-done.1
  27.9 0.0 copy-done.3
  27.9 0.8 %dense.1 = (bf16[128,256]{1,0:T(8,128)(2,1)}, bf16[384,256]{1,0:T(8,128)(2,1)S(1)}, f32[128,256]{1,0:T(8,128)S(1)}) custom-call(bf16[256,256]{1,0:T(8,128)(2,1)S(1)} %add_convert_fusion.mine, bf16[256,256]{1,0:T(8,128)(2,1)S(1)} %collective-permute-done.9.got, bf16[256,256]{1,0:T(8,128)(2,1)S(1)} %copy-done.1, bf16[128,256]{1,0:T(8,128)(2,1)S(1)} %bitcast.15, ...), custom_call_target="tpu_custom_call" | custom-call | tf_op jit(solution)/shard_map/dense/pallas_call | solution.py:217
  28.7 0.0 collective-permute-start.10
  28.7 1.4 %collective-permute-done.10.refs_1_ = bf16[384,256]{1,0:T(8,128)(2,1)S(1)} collective-permute-done((bf16[384,256]{1,0:T(8,128)(2,1)S(1)}, bf16[384,256]{1,0:T(8,128)(2,1)S(1)}, u32[]{:S(2)}, u32[]{:S(2)}) %collective-permute-start.10) | collective-permute-done | bytes 196640 | tf_op jit(solution)/shard_map/swap_cores/ppermute | solution.py:27
  30.2 1.4 %collective-permute-start.11 = (bf16[128,256]{1,0:T(8,128)(2,1)S(1)}, bf16[128,256]{1,0:T(8,128)(2,1)S(1)}, u32[]{:S(2)}, u32[]{:S(2)}) collective-permute-start(bf16[128,256]{1,0:T(8,128)(2,1)S(1)} %add_convert_fusion.7), channel_id=1, source_target_pairs={{0,16},{4,20},{8,24},{12,28},{16,0},{20,4},{24,8},{28,12},{1,17},{... | collective-permute-start | bytes 196616 | tf_op jit(solution)/shard_map/sum_weight/ppermute | solution.py:27
  31.6 0.9 %backward_blocks.1 = (bf16[128,256]{1,0:T(8,128)(2,1)S(1)}, bf16[128,256]{1,0:T(8,128)(2,1)S(1)}, bf16[256,256]{1,0:T(8,128)(2,1)S(1)}, bf16[128,256]{1,0:T(8,12...) custom-call(s32[8,128]{1,0:T(8,128)S(1)} %gather_features.1.info, ...), custom_call_target="tpu_custom_call" | custom-call | tf_op jit(solution)/shard_map/backward_blocks/pallas_call | solution.py:257
  32.5 0.6 %collective-permute-start.13 = (bf16[128,256]{1,0:T(8,128)(2,1)S(1)}, bf16[128,256]{1,0:T(8,128)(2,1)S(1)}, u32[]{:S(2)}, u32[]{:S(2)}) collective-permute-start(bf16[128,256]{1,0:T(8,128)(2,1)S(1)} %get-tuple-element.55), channel_id=1, source_target_pairs={{0,4},{4,0},{8,12},{12,8},{16,20},{20,16},{24,28},{28,24},{1,5},{5... | collective-permute-start | bytes 196616 | tf_op jit(solution)/shard_map/sum_columns/ppermute | solution.py:27
  33.1 1.5 %collective-permute-start.14 = (bf16[128,256]{1,0:T(8,128)(2,1)S(1)}, bf16[128,256]{1,0:T(8,128)(2,1)S(1)}, u32[]{:S(2)}, u32[]{:S(2)}) collective-permute-start(bf16[128,256]{1,0:T(8,128)(2,1)S(1)} %get-tuple-element.56), channel_id=1, source_target_pairs={{0,4},{4,0},{8,12},{12,8},{16,20},{20,16},{24,28},{28,24},{1,5},{5... | collective-permute-start | bytes 196616 | tf_op jit(solution)/shard_map/sum_columns/ppermute | solution.py:27
  34.6 0.5 %collective-permute-start.16 = (bf16[256,256]{1,0:T(8,128)(2,1)S(1)}, bf16[256,256]{1,0:T(8,128)(2,1)S(1)}, u32[]{:S(2)}, u32[]{:S(2)}) collective-permute-start(bf16[256,256]{1,0:T(8,128)(2,1)S(1)} %get-tuple-element.60), channel_id=1, source_target_pairs={{0,4},{4,0},{8,12},{12,8},{16,20},{20,16},{24,28},{28,24},{1,5},{5... | collective-permute-start | bytes 393224 | tf_op jit(solution)/shard_map/sum_columns/ppermute | solution.py:27
  35.1 0.7 %collective-permute-done.11 = bf16[128,256]{1,0:T(8,128)(2,1)S(1)} collective-permute-done((bf16[128,256]{1,0:T(8,128)(2,1)S(1)}, bf16[128,256]{1,0:T(8,128)(2,1)S(1)}, u32[]{:S(2)}, u32[]{:S(2)}) %collective-permute-start.11) | collective-permute-done | bytes 65568 | tf_op jit(solution)/shard_map/sum_weight/ppermute | solution.py:27
  35.9 1.4 %collective-permute-start.12 = (bf16[128,256]{1,0:T(8,128)(2,1)S(1)}, bf16[128,256]{1,0:T(8,128)(2,1)S(1)}, u32[]{:S(2)}, u32[]{:S(2)}) collective-permute-start(bf16[128,256]{1,0:T(8,128)(2,1)S(1)} %add_convert_fusion.6), channel_id=1, source_target_pairs={{0,8},{4,12},{8,0},{12,4},{16,24},{20,28},{24,16},{28,20},{1,9},{5... | collective-permute-start | bytes 196616 | tf_op jit(solution)/shard_map/sum_columns/sum_weight/sum_weight/ppermute | solution.py:27
  37.2 1.7 %collective-permute-done.14 = bf16[128,256]{1,0:T(8,128)(2,1)S(1)} collective-permute-done((bf16[128,256]{1,0:T(8,128)(2,1)S(1)}, bf16[128,256]{1,0:T(8,128)(2,1)S(1)}, u32[]{:S(2)}, u32[]{:S(2)}) %collective-permute-start.14) | collective-permute-done | bytes 65568 | tf_op jit(solution)/shard_map/sum_columns/ppermute | solution.py:27
  39.0 0.0 collective-permute-done.13
  39.0 0.7 %collective-permute-start.19 = (bf16[128,256]{1,0:T(8,128)(2,1)S(1)}, bf16[128,256]{1,0:T(8,128)(2,1)S(1)}, u32[]{:S(2)}, u32[]{:S(2)}) collective-permute-start(bf16[128,256]{1,0:T(8,128)(2,1)S(1)} %add_convert_fusion.2), channel_id=1, source_target_pairs={{0,24},{4,28},{8,16},{12,20},{16,8},{20,12},{24,0},{28,4},{1,25},{... | collective-permute-start | bytes 196616 | tf_op jit(solution)/shard_map/sum_columns/ppermute | solution.py:27
  39.7 2.0 %collective-permute-start.20 = (bf16[128,256]{1,0:T(8,128)(2,1)S(1)}, bf16[128,256]{1,0:T(8,128)(2,1)S(1)}, u32[]{:S(2)}, u32[]{:S(2)}) collective-permute-start(bf16[128,256]{1,0:T(8,128)(2,1)S(1)} %add_convert_fusion.1), channel_id=1, source_target_pairs={{0,16},{4,20},{8,24},{12,28},{16,0},{20,4},{24,8},{28,12},{1,17},{... | collective-permute-start | bytes 196616 | tf_op jit(solution)/shard_map/sum_columns/ppermute | solution.py:27
  41.7 0.0 collective-permute-done.12
  41.8 1.4 %collective-permute-start.15 = (bf16[128,256]{1,0:T(8,128)(2,1)S(1)}, bf16[128,256]{1,0:T(8,128)(2,1)S(1)}, u32[]{:S(2)}, u32[]{:S(2)}) collective-permute-start(bf16[128,256]{1,0:T(8,128)(2,1)S(1)} %add_convert_fusion.5), channel_id=1, source_target_pairs={{0,4},{4,0},{8,12},{12,8},{16,20},{20,16},{24,28},{28,24},{1,5},{5... | collective-permute-start | bytes 196616 | tf_op jit(solution)/shard_map/sum_columns/sum_weight/sum_weight/ppermute | solution.py:27
  43.2 0.0 collective-permute-done.16.refs_1_
  43.2 1.1 %collective-permute-start.18 = (bf16[128,256]{1,0:T(8,128)(2,1)S(1)}, bf16[128,256]{1,0:T(8,128)(2,1)S(1)}, u32[]{:S(2)}, u32[]{:S(2)}) collective-permute-start(bf16[128,256]{1,0:T(8,128)(2,1)S(1)} %add_convert_fusion.3), channel_id=1, source_target_pairs={{0,8},{4,12},{8,0},{12,4},{16,24},{20,28},{24,16},{28,20},{1,9},{5... | collective-permute-start | bytes 196616 | tf_op jit(solution)/shard_map/sum_columns/ppermute | solution.py:27
  44.3 1.8 %collective-permute-done.15 = bf16[128,256]{1,0:T(8,128)(2,1)S(1)} collective-permute-done((bf16[128,256]{1,0:T(8,128)(2,1)S(1)}, bf16[128,256]{1,0:T(8,128)(2,1)S(1)}, u32[]{:S(2)}, u32[]{:S(2)}) %collective-permute-start.15) | collective-permute-done | bytes 65568 | tf_op jit(solution)/shard_map/sum_columns/sum_weight/sum_weight/ppermute | solution.py:27
  46.1 0.1 collective-permute-start.17
  46.2 0.2 collective-permute-done.20.refs_2_
  46.4 0.0 collective-permute-done.19.refs_3_
  46.4 1.2 %collective-permute-done.18.refs_4_ = bf16[128,256]{1,0:T(8,128)(2,1)S(1)} collective-permute-done((bf16[128,256]{1,0:T(8,128)(2,1)S(1)}, bf16[128,256]{1,0:T(8,128)(2,1)S(1)}, u32[]{:S(2)}, u32[]{:S(2)}) %collective-permute-start.18) | collective-permute-done | bytes 65568 | tf_op jit(solution)/shard_map/sum_columns/ppermute | solution.py:27
  47.5 0.0 collective-permute-done.17.other
  47.5 0.8 %shard_map.94 = (f32[128,256]{1,0:T(8,128)}, f32[256,256]{1,0:T(8,128)}) custom-call(bf16[128,256]{1,0:T(8,128)(2,1)S(1)} %add_convert_fusion.4.mine, bf16[128,256]{1,0:T(8,128)(2,1)S(1)} %collective-permute-done.17.other, bf16[256,256]{1,0:T(8,128)(2,1)S(1)} %get-tuple-element.63.refs_0_, bf16[256,256]{1,0:T(8,128)(2,1)S(1)} %collective-permute-done.16.refs_1_, ...), custom_call_target="tpu_custom_call" | custom-call | tf_op jit(solution)/shard_map/pallas_call | solution.py:287
  (9 shorter events, 0.2 us)
Async XLA Ops:
  0.6 8.1 %collective-permute-start.1 = (bf16[128,256]{1,0:T(8,128)(2,1)}, bf16[128,256]{1,0:T(8,128)(2,1)S(1)}, u32[]{:S(2)}, u32[]{:S(2)}) collective-permute-start(bf16[128,256]{1,0:T(8,128)(2,1)} %bitcast.9), channel_id=1, source_target_pairs={{0,16},{4,20},{8,24},{12,28},{16,0},{20,4},{24,8},{28,12},{1,17},{... | collective-permute-start | bytes 196616 | tf_op jit(solution)/shard_map/gather_features/ppermute | solution.py:27
  4.7 4.5 %collective-permute-start = (bf16[128,256]{1,0:T(8,128)(2,1)}, bf16[128,256]{1,0:T(8,128)(2,1)S(1)}, u32[]{:S(2)}, u32[]{:S(2)}) collective-permute-start(bf16[128,256]{1,0:T(8,128)(2,1)} %bitcast.10), channel_id=1, source_target_pairs={{0,8},{4,12},{8,0},{12,4},{16,24},{20,28},{24,16},{28,20},{1,9},{5... | collective-permute-start | bytes 196616 | tf_op jit(solution)/shard_map/gather_features/ppermute | solution.py:27
  6.3 6.3 %collective-permute-start.3 = (bf16[128,256]{1,0:T(8,128)(2,1)}, bf16[128,256]{1,0:T(8,128)(2,1)S(1)}, u32[]{:S(2)}, u32[]{:S(2)}) collective-permute-start(bf16[128,256]{1,0:T(8,128)(2,1)} %bitcast.11), channel_id=1, source_target_pairs={{0,24},{4,28},{8,16},{12,20},{16,8},{20,12},{24,0},{28,4},{1,25},{... | collective-permute-start | bytes 196616 | tf_op jit(solution)/shard_map/gather_features/ppermute | solution.py:27
  6.3 7.8 %collective-permute-start.2 = (bf16[128,256]{1,0:T(8,128)(2,1)}, bf16[128,256]{1,0:T(8,128)(2,1)S(1)}, u32[]{:S(2)}, u32[]{:S(2)}) collective-permute-start(bf16[128,256]{1,0:T(8,128)(2,1)} %bitcast.12), channel_id=1, source_target_pairs={{0,4},{4,0},{8,12},{12,8},{16,20},{20,16},{24,28},{28,24},{1,5},{5... | collective-permute-start | bytes 196616 | tf_op jit(solution)/shard_map/gather_features/ppermute | solution.py:27
  9.2 9.4 %collective-permute-start.6 = (bf16[128,256]{1,0:T(8,128)(2,1)S(1)}, bf16[128,256]{1,0:T(8,128)(2,1)S(1)}, u32[]{:S(2)}, u32[]{:S(2)}) collective-permute-start(bf16[128,256]{1,0:T(8,128)(2,1)S(1)} %collective-permute-done.refs_1_), channel_id=1, source_target_pairs={{0,4},{4,0},{8,12},{12,8},{16,20},{20,16},{24,28},{28,24},{1,5},{5... | collective-permute-start | bytes 196616 | tf_op jit(solution)/shard_map/gather_features/ppermute | solution.py:27
  12.6 6.0 %collective-permute-start.5 = (bf16[128,256]{1,0:T(8,128)(2,1)S(1)}, bf16[128,256]{1,0:T(8,128)(2,1)S(1)}, u32[]{:S(2)}, u32[]{:S(2)}) collective-permute-start(bf16[128,256]{1,0:T(8,128)(2,1)S(1)} %collective-permute-done.3.refs_2_), channel_id=1, source_target_pairs={{0,4},{4,0},{8,12},{12,8},{16,20},{20,16},{24,28},{28,24},{1,5},{5... | collective-permute-start | bytes 196616 | tf_op jit(solution)/shard_map/gather_features/ppermute | solution.py:27
  14.1 2.0 %copy-start.4 = (s32[1,1,6]{2,1,0:T(1,128)S(1)}, s32[1,1,6]{2,1,0:T(1,128)}, u32[]{:S(2)}) copy-start(s32[1,1,6]{2,1,0:T(1,128)} %param.10) | copy-start | bytes 76
  14.1 2.0 %copy-start.5 = (s32[1,1,6]{2,1,0:T(1,128)S(1)}, s32[1,1,6]{2,1,0:T(1,128)}, u32[]{:S(2)}) copy-start(s32[1,1,6]{2,1,0:T(1,128)} %param.11) | copy-start | bytes 76
  14.1 4.5 %collective-permute-start.4 = (bf16[128,256]{1,0:T(8,128)(2,1)}, bf16[128,256]{1,0:T(8,128)(2,1)S(1)}, u32[]{:S(2)}, u32[]{:S(2)}) collective-permute-start(bf16[128,256]{1,0:T(8,128)(2,1)} %bitcast.14), channel_id=1, source_target_pairs={{0,2},{1,3},{2,0},{3,1},{4,6},{5,7},{6,4},{7,5},{8,10},{9,11},{10,... | collective-permute-start | bytes 196616 | tf_op jit(solution)/shard_map/gather_features/ppermute | solution.py:27
  15.6 4.3 %collective-permute-start.7 = (bf16[128,256]{1,0:T(8,128)(2,1)S(1)}, bf16[128,256]{1,0:T(8,128)(2,1)S(1)}, u32[]{:S(2)}, u32[]{:S(2)}) collective-permute-start(bf16[128,256]{1,0:T(8,128)(2,1)S(1)} %collective-permute-done.1.refs_0_), channel_id=1, source_target_pairs={{0,4},{4,0},{8,12},{12,8},{16,20},{20,16},{24,28},{28,24},{1,5},{5... | collective-permute-start | bytes 196616 | tf_op jit(solution)/shard_map/gather_features/ppermute | solution.py:27
  16.1 3.8 %copy-start = (bf16[1,1,6,128,128]{4,3,2,1,0:T(8,128)(2,1)S(1)}, bf16[1,1,6,128,128]{4,3,2,1,0:T(8,128)(2,1)}, u32[]{:S(2)}) copy-start(bf16[1,1,6,128,128]{4,3,2,1,0:T(8,128)(2,1)} %param.13) | copy-start | bytes 589828
  16.1 3.8 %copy-start.2 = (bf16[1,128,256]{2,1,0:T(8,128)(2,1)S(1)}, bf16[1,128,256]{2,1,0:T(8,128)(2,1)}, u32[]{:S(2)}) copy-start(bf16[1,128,256]{2,1,0:T(8,128)(2,1)} %param.7) | copy-start | bytes 196612
  20.8 1.4 %collective-permute-start.8 = (bf16[256,256]{1,0:T(8,128)(2,1)S(1)}, bf16[256,256]{1,0:T(8,128)(2,1)S(1)}, u32[]{:S(2)}, u32[]{:S(2)}) collective-permute-start(bf16[256,256]{1,0:T(8,128)(2,1)S(1)} %get-tuple-element.49), channel_id=1, source_target_pairs={{0,1},{1,0},{2,3},{3,2},{4,5},{5,4},{6,7},{7,6},{8,9},{9,8},{10,11... | collective-permute-start | bytes 393224 | tf_op jit(solution)/shard_map/sum_rows/ppermute | solution.py:27
  22.2 5.7 %copy-start.1 = (bf16[256,256]{1,0:T(8,128)(2,1)S(1)}, bf16[256,256]{1,0:T(8,128)(2,1)}, u32[]{:S(2)}) copy-start(bf16[256,256]{1,0:T(8,128)(2,1)} %weight.1) | copy-start | bytes 393220
  22.2 5.7 %copy-start.3 = (bf16[1,128,256]{2,1,0:T(8,128)(2,1)S(1)}, bf16[1,128,256]{2,1,0:T(8,128)(2,1)}, u32[]{:S(2)}) copy-start(bf16[1,128,256]{2,1,0:T(8,128)(2,1)} %param.9) | copy-start | bytes 196612
  22.3 5.6 %collective-permute-start.9 = (bf16[256,256]{1,0:T(8,128)(2,1)S(1)}, bf16[256,256]{1,0:T(8,128)(2,1)S(1)}, u32[]{:S(2)}, u32[]{:S(2)}) collective-permute-start(bf16[256,256]{1,0:T(8,128)(2,1)S(1)} %add_convert_fusion.mine), channel_id=1, source_target_pairs={{0,2},{1,3},{2,0},{3,1},{4,6},{5,7},{6,4},{7,5},{8,10},{9,11},{10,... | collective-permute-start | bytes 393224 | tf_op jit(solution)/shard_map/sum_rows/ppermute | solution.py:27
  28.7 1.4 %collective-permute-start.10 = (bf16[384,256]{1,0:T(8,128)(2,1)S(1)}, bf16[384,256]{1,0:T(8,128)(2,1)S(1)}, u32[]{:S(2)}, u32[]{:S(2)}) collective-permute-start(bf16[384,256]{1,0:T(8,128)(2,1)S(1)} %get-tuple-element.52.refs_0_), channel_id=1, source_target_pairs={{0,1},{1,0},{2,3},{3,2},{4,5},{5,4},{6,7},{7,6},{8,9},{9,8},{10,11... | collective-permute-start | bytes 589832 | tf_op jit(solution)/shard_map/swap_cores/ppermute | solution.py:27
  30.2 5.6 %collective-permute-start.11 = (bf16[128,256]{1,0:T(8,128)(2,1)S(1)}, bf16[128,256]{1,0:T(8,128)(2,1)S(1)}, u32[]{:S(2)}, u32[]{:S(2)}) collective-permute-start(bf16[128,256]{1,0:T(8,128)(2,1)S(1)} %add_convert_fusion.7), channel_id=1, source_target_pairs={{0,16},{4,20},{8,24},{12,28},{16,0},{20,4},{24,8},{28,12},{1,17},{... | collective-permute-start | bytes 196616 | tf_op jit(solution)/shard_map/sum_weight/ppermute | solution.py:27
  32.5 6.5 %collective-permute-start.13 = (bf16[128,256]{1,0:T(8,128)(2,1)S(1)}, bf16[128,256]{1,0:T(8,128)(2,1)S(1)}, u32[]{:S(2)}, u32[]{:S(2)}) collective-permute-start(bf16[128,256]{1,0:T(8,128)(2,1)S(1)} %get-tuple-element.55), channel_id=1, source_target_pairs={{0,4},{4,0},{8,12},{12,8},{16,20},{20,16},{24,28},{28,24},{1,5},{5... | collective-permute-start | bytes 196616 | tf_op jit(solution)/shard_map/sum_columns/ppermute | solution.py:27
  33.1 5.9 %collective-permute-start.14 = (bf16[128,256]{1,0:T(8,128)(2,1)S(1)}, bf16[128,256]{1,0:T(8,128)(2,1)S(1)}, u32[]{:S(2)}, u32[]{:S(2)}) collective-permute-start(bf16[128,256]{1,0:T(8,128)(2,1)S(1)} %get-tuple-element.56), channel_id=1, source_target_pairs={{0,4},{4,0},{8,12},{12,8},{16,20},{20,16},{24,28},{28,24},{1,5},{5... | collective-permute-start | bytes 196616 | tf_op jit(solution)/shard_map/sum_columns/ppermute | solution.py:27
  34.6 8.6 %collective-permute-start.16 = (bf16[256,256]{1,0:T(8,128)(2,1)S(1)}, bf16[256,256]{1,0:T(8,128)(2,1)S(1)}, u32[]{:S(2)}, u32[]{:S(2)}) collective-permute-start(bf16[256,256]{1,0:T(8,128)(2,1)S(1)} %get-tuple-element.60), channel_id=1, source_target_pairs={{0,4},{4,0},{8,12},{12,8},{16,20},{20,16},{24,28},{28,24},{1,5},{5... | collective-permute-start | bytes 393224 | tf_op jit(solution)/shard_map/sum_columns/ppermute | solution.py:27
  35.9 5.9 %collective-permute-start.12 = (bf16[128,256]{1,0:T(8,128)(2,1)S(1)}, bf16[128,256]{1,0:T(8,128)(2,1)S(1)}, u32[]{:S(2)}, u32[]{:S(2)}) collective-permute-start(bf16[128,256]{1,0:T(8,128)(2,1)S(1)} %add_convert_fusion.6), channel_id=1, source_target_pairs={{0,8},{4,12},{8,0},{12,4},{16,24},{20,28},{24,16},{28,20},{1,9},{5... | collective-permute-start | bytes 196616 | tf_op jit(solution)/shard_map/sum_columns/sum_weight/sum_weight/ppermute | solution.py:27
  39.0 7.3 %collective-permute-start.19 = (bf16[128,256]{1,0:T(8,128)(2,1)S(1)}, bf16[128,256]{1,0:T(8,128)(2,1)S(1)}, u32[]{:S(2)}, u32[]{:S(2)}) collective-permute-start(bf16[128,256]{1,0:T(8,128)(2,1)S(1)} %add_convert_fusion.2), channel_id=1, source_target_pairs={{0,24},{4,28},{8,16},{12,20},{16,8},{20,12},{24,0},{28,4},{1,25},{... | collective-permute-start | bytes 196616 | tf_op jit(solution)/shard_map/sum_columns/ppermute | solution.py:27
  39.7 6.7 %collective-permute-start.20 = (bf16[128,256]{1,0:T(8,128)(2,1)S(1)}, bf16[128,256]{1,0:T(8,128)(2,1)S(1)}, u32[]{:S(2)}, u32[]{:S(2)}) collective-permute-start(bf16[128,256]{1,0:T(8,128)(2,1)S(1)} %add_convert_fusion.1), channel_id=1, source_target_pairs={{0,16},{4,20},{8,24},{12,28},{16,0},{20,4},{24,8},{28,12},{1,17},{... | collective-permute-start | bytes 196616 | tf_op jit(solution)/shard_map/sum_columns/ppermute | solution.py:27
  41.8 4.3 %collective-permute-start.15 = (bf16[128,256]{1,0:T(8,128)(2,1)S(1)}, bf16[128,256]{1,0:T(8,128)(2,1)S(1)}, u32[]{:S(2)}, u32[]{:S(2)}) collective-permute-start(bf16[128,256]{1,0:T(8,128)(2,1)S(1)} %add_convert_fusion.5), channel_id=1, source_target_pairs={{0,4},{4,0},{8,12},{12,8},{16,20},{20,16},{24,28},{28,24},{1,5},{5... | collective-permute-start | bytes 196616 | tf_op jit(solution)/shard_map/sum_columns/sum_weight/sum_weight/ppermute | solution.py:27
  43.2 4.3 %collective-permute-start.18 = (bf16[128,256]{1,0:T(8,128)(2,1)S(1)}, bf16[128,256]{1,0:T(8,128)(2,1)S(1)}, u32[]{:S(2)}, u32[]{:S(2)}) collective-permute-start(bf16[128,256]{1,0:T(8,128)(2,1)S(1)} %add_convert_fusion.3), channel_id=1, source_target_pairs={{0,8},{4,12},{8,0},{12,4},{16,24},{20,28},{24,16},{28,20},{1,9},{5... | collective-permute-start | bytes 196616 | tf_op jit(solution)/shard_map/sum_columns/ppermute | solution.py:27
  46.1 1.4 %collective-permute-start.17 = (bf16[128,256]{1,0:T(8,128)(2,1)S(1)}, bf16[128,256]{1,0:T(8,128)(2,1)S(1)}, u32[]{:S(2)}, u32[]{:S(2)}) collective-permute-start(bf16[128,256]{1,0:T(8,128)(2,1)S(1)} %add_convert_fusion.4.mine), channel_id=1, source_target_pairs={{0,1},{1,0},{2,3},{3,2},{4,5},{5,4},{6,7},{7,6},{8,9},{9,8},{10,11... | collective-permute-start | bytes 196616 | tf_op jit(solution)/shard_map/sum_weight/ppermute | solution.py:27

commit v3 on v2

--- a/solution.py
+++ b/solution.py
@@ -74,6 +74,24 @@
             return 0
 
         lax.fori_loop(0, count, one, 0)
+
+
+def join_kernel(*refs):
+    *parts, out = refs
+    rows = parts[0].shape[0]
+    for n, part in enumerate(parts):
+        out[pl.ds(n * rows, rows), :] = part[...]
+
+
+def join(*parts):
+    shape = (len(parts) * parts[0].shape[0], parts[0].shape[1])
+    return pl.pallas_call(
+        join_kernel,
+        out_shape=jax.ShapeDtypeStruct(shape, parts[0].dtype),
+        in_specs=[VMEM] * len(parts),
+        out_specs=VMEM,
+        compiler_params=params(16 * 2**20),
+    )(*parts)
 
 
 def info_kernel(rows, cols, counts, info):
@@ -160,13 +178,13 @@
     limit = 48 * 2**20
     with jax.named_scope("gather_features"):
         x = features[0]
-        moved = {m: swap(x, "gr", m) for m in far_first + [1]}
-        arrival = Line()
-        held = {}
-        for m in far_first[:1] + [2] + far_first[1:-1] + [1]:
-            held[m] = arrival(moved[m])
-            if m > 1:
-                moved[m + 1] = swap(held[m], "gr", 1)
+        first, *others = far_first[:-1]
+        held = {m: swap(x, "gr", m) for m in [1, first, 2, *others]}
+        held[0] = x
+        grads = {0: after(grad_out[0], held[2])}
+        for bit in bits_of("gc")[1:]:
+            grads.update({m | bit: swap(v, "gc", bit) for m, v in list(grads.items())})
+        held.update({m + 1: swap(held[m], "gr", 1) for m in [first, 2, *others]})
         values = block_values[0, 0]
         info = pl.pallas_call(
             info_kernel,
@@ -175,17 +193,10 @@
             out_specs=VMEM,
             compiler_params=params(limit),
             cost_estimate=pl.CostEstimate(flops=5 * 10**9, bytes_accessed=0, transcendentals=0),
-        )(after(block_rows[0], held[2]), block_cols[0], block_counts)
-        grads = {0: after(grad_out[0], held[1])}
-        for bit in bits_of("gc")[1:]:
-            grads.update({m | bit: swap(v, "gc", bit) for m, v in list(grads.items())})
-        grads = {m: arrival(v) for m, v in grads.items()}
-        for m in (far_first[:1] + [2] + far_first[1:-1])[::-1]:
-            held[m + 1] = arrival(moved[m + 1])
-        held[0] = x
+        )(*[after(v, held[2]) for v in (block_rows[0], block_cols[0], block_counts)])
     layout = [(m,) for m in held]
+    held[0] = after(x, *grads.values())
     pieces = list(held.values())
-    pieces[0] = after(pieces[0], *grads.values())
 
     with jax.named_scope("forward_blocks"):
         send_masks = [m for m in range(gc_size) if m & 1]

time: 48.5 us -> 46.6 us (0.961)
  waiting for transfers between devices: 19.4 us -> 15.7 us
  starting transfers between devices: 23.8 us -> 25.6 us
    ppermute x21, waiting for transfers between devices: 19.4 us -> 15.7 us  [swap(): return lax.ppermute(value, axis, [(i, i ^ mask) for i in range(size)])]
    ppermute x21, starting transfers between devices: 23.8 us -> 25.6 us  [swap(): return lax.ppermute(value, axis, [(i, i ^ mask) for i in range(size)])]
where the time goes in v3:
time: 46.6 us; the launch traced here: 46.5 us
  starting transfers between devices  25.6 us (55%)
  waiting for transfers between devices  15.7 us (34%)
  Pallas kernels  3.53 us (8%)
  between operations  1.44 us (3%)
    ppermute x21, starting transfers between devices, swap(): return lax.ppermute(value, axis, [(i, i ^ mask) for i in range(size)])  25.6 us
    ppermute x21, waiting for transfers between devices, swap(): return lax.ppermute(value, axis, [(i, i ^ mask) for i in range(size)])  15.7 us
    pallas_call x1, Pallas kernels, per_device(): pl.pallas_call(functools.partial(backward_kernel, [keep_masks, send_masks...  0.95 us
  transfers between devices with their start and end apart: 21, of which 12 were waited for; matrix products, arithmetic and copies ran while one was open for 0% of the time, Pallas kernels for 2%

profile of v3, /device:TPU:0, one launch (start us, length us, event | category | flops | bytes accessed | tf_op | source)
XLA Modules:
  0.0 46.5 jit_solution(9804814628107744597)
XLA Ops:
  0.6 3.1 %collective-permute-start = (bf16[128,256]{1,0:T(8,128)(2,1)}, bf16[128,256]{1,0:T(8,128)(2,1)S(1)}, u32[]{:S(2)}, u32[]{:S(2)}) collective-permute-start(bf16[128,256]{1,0:T(8,128)(2,1)} %bitcast.9), channel_id=1, source_target_pairs={{0,8},{4,12},{8,0},{12,4},{16,24},{20,28},{24,16},{28,20},{1,9},{5... | collective-permute-start | bytes 196616 | tf_op jit(solution)/shard_map/gather_features/ppermute | solution.py:27
  3.7 2.5 %collective-permute-start.3 = (bf16[128,256]{1,0:T(8,128)(2,1)}, bf16[128,256]{1,0:T(8,128)(2,1)S(1)}, u32[]{:S(2)}, u32[]{:S(2)}) collective-permute-start(bf16[128,256]{1,0:T(8,128)(2,1)} %bitcast.10), channel_id=1, source_target_pairs={{0,24},{4,28},{8,16},{12,20},{16,8},{20,12},{24,0},{28,4},{1,25},{... | collective-permute-start | bytes 196616 | tf_op jit(solution)/shard_map/gather_features/ppermute | solution.py:27
  6.2 0.1 collective-permute-start.2
  6.3 1.5 %collective-permute-start.1 = (bf16[128,256]{1,0:T(8,128)(2,1)}, bf16[128,256]{1,0:T(8,128)(2,1)S(1)}, u32[]{:S(2)}, u32[]{:S(2)}) collective-permute-start(bf16[128,256]{1,0:T(8,128)(2,1)} %bitcast.12), channel_id=1, source_target_pairs={{0,4},{4,0},{8,12},{12,8},{16,20},{20,16},{24,28},{28,24},{1,5},{5... | collective-permute-start | bytes 196616 | tf_op jit(solution)/shard_map/gather_features/ppermute | solution.py:27
  8.5 0.0 collective-permute-done.refs_2_
  8.5 0.0 copy-start.4
  8.5 0.0 copy-start.5
  8.5 0.0 copy-start
  8.5 0.0 copy-start.2
  8.5 1.6 %collective-permute-start.4 = (bf16[128,256]{1,0:T(8,128)(2,1)}, bf16[128,256]{1,0:T(8,128)(2,1)S(1)}, u32[]{:S(2)}, u32[]{:S(2)}) collective-permute-start(bf16[128,256]{1,0:T(8,128)(2,1)} %bitcast.14), channel_id=1, source_target_pairs={{0,2},{1,3},{2,0},{3,1},{4,6},{5,7},{6,4},{7,5},{8,10},{9,11},{10,... | collective-permute-start | bytes 196616 | tf_op jit(solution)/shard_map/gather_features/ppermute | solution.py:27
  10.1 0.5 %collective-permute-start.6 = (bf16[128,256]{1,0:T(8,128)(2,1)S(1)}, bf16[128,256]{1,0:T(8,128)(2,1)S(1)}, u32[]{:S(2)}, u32[]{:S(2)}) collective-permute-start(bf16[128,256]{1,0:T(8,128)(2,1)S(1)} %collective-permute-done.refs_2_), channel_id=1, source_target_pairs={{0,4},{4,0},{8,12},{12,8},{16,20},{20,16},{24,28},{28,24},{1,5},{5... | collective-permute-start | bytes 196616 | tf_op jit(solution)/shard_map/gather_features/ppermute | solution.py:27
  10.6 0.2 collective-permute-done.3.refs_3_
  10.8 1.5 %collective-permute-start.7 = (bf16[128,256]{1,0:T(8,128)(2,1)S(1)}, bf16[128,256]{1,0:T(8,128)(2,1)S(1)}, u32[]{:S(2)}, u32[]{:S(2)}) collective-permute-start(bf16[128,256]{1,0:T(8,128)(2,1)S(1)} %collective-permute-done.3.refs_3_), channel_id=1, source_target_pairs={{0,4},{4,0},{8,12},{12,8},{16,20},{20,16},{24,28},{28,24},{1,5},{5... | collective-permute-start | bytes 196616 | tf_op jit(solution)/shard_map/gather_features/ppermute | solution.py:27
  12.3 0.6 %collective-permute-done.2.refs_1_ = bf16[128,256]{1,0:T(8,128)(2,1)S(1)} collective-permute-done((bf16[128,256]{1,0:T(8,128)(2,1)}, bf16[128,256]{1,0:T(8,128)(2,1)S(1)}, u32[]{:S(2)}, u32[]{:S(2)}) %collective-permute-start.2) | collective-permute-done | bytes 65568 | tf_op jit(solution)/shard_map/gather_features/ppermute | solution.py:27
  12.9 1.5 %collective-permute-start.5 = (bf16[128,256]{1,0:T(8,128)(2,1)S(1)}, bf16[128,256]{1,0:T(8,128)(2,1)S(1)}, u32[]{:S(2)}, u32[]{:S(2)}) collective-permute-start(bf16[128,256]{1,0:T(8,128)(2,1)S(1)} %collective-permute-done.2.refs_1_), channel_id=1, source_target_pairs={{0,4},{4,0},{8,12},{12,8},{16,20},{20,16},{24,28},{28,24},{1,5},{5... | collective-permute-start | bytes 196616 | tf_op jit(solution)/shard_map/gather_features/ppermute | solution.py:27
  14.4 0.0 copy-done.4
  14.4 0.0 copy-done.5
  14.4 0.0 collective-permute-done.4.refs_1_
  14.4 0.0 collective-permute-done.1.refs_0_
  14.4 0.6 %collective-permute-done.7.refs_7_ = bf16[128,256]{1,0:T(8,128)(2,1)S(1)} collective-permute-done((bf16[128,256]{1,0:T(8,128)(2,1)S(1)}, bf16[128,256]{1,0:T(8,128)(2,1)S(1)}, u32[]{:S(2)}, u32[]{:S(2)}) %collective-permute-start.7) | collective-permute-done | bytes 65568 | tf_op jit(solution)/shard_map/gather_features/ppermute | solution.py:27
  15.1 2.1 %collective-permute-done.5.refs_5_ = bf16[128,256]{1,0:T(8,128)(2,1)S(1)} collective-permute-done((bf16[128,256]{1,0:T(8,128)(2,1)S(1)}, bf16[128,256]{1,0:T(8,128)(2,1)S(1)}, u32[]{:S(2)}, u32[]{:S(2)}) %collective-permute-start.5) | collective-permute-done | bytes 65568 | tf_op jit(solution)/shard_map/gather_features/ppermute | solution.py:27
  17.1 0.0 collective-permute-done.6.refs_6_
  17.1 0.0 copy-done
  17.1 0.0 copy-done.2
  17.1 0.9 %forward_blocks.1 = (bf16[256,256]{1,0:T(8,128)(2,1)S(1)}, bf16[256,256]{1,0:T(8,128)(2,1)S(1)}) custom-call(s32[8,128]{1,0:T(8,128)S(1)} %gather_features.1.info, bf16[6,128,128]{2,1,0:T(8,128)(2,1)S(1)} %bitcast.7, bf16[128,256]{1,0:T(8,128)(2,1)S(1)} %collective-permute-done.1.refs_0_, bf16[128,256]{1,0:T(8,128)(2,1)S(1)} %collective-permute-done.2.refs_1_, ...), custom_call_target="tpu_custom_call" | custom-call | tf_op jit(solution)/shard_map/forward_blocks/pallas_call | solution.py:204
  18.1 0.1 collective-permute-start.8
  18.2 1.3 %collective-permute-done.8 = bf16[256,256]{1,0:T(8,128)(2,1)S(1)} collective-permute-done((bf16[256,256]{1,0:T(8,128)(2,1)S(1)}, bf16[256,256]{1,0:T(8,128)(2,1)S(1)}, u32[]{:S(2)}, u32[]{:S(2)}) %collective-permute-start.8) | collective-permute-done | bytes 131104 | tf_op jit(solution)/shard_map/sum_rows/ppermute | solution.py:27
  19.5 0.0 copy-start.1
  19.5 0.0 copy-start.3
  19.5 1.6 %collective-permute-start.9 = (bf16[256,256]{1,0:T(8,128)(2,1)S(1)}, bf16[256,256]{1,0:T(8,128)(2,1)S(1)}, u32[]{:S(2)}, u32[]{:S(2)}) collective-permute-start(bf16[256,256]{1,0:T(8,128)(2,1)S(1)} %add_convert_fusion.mine), channel_id=1, source_target_pairs={{0,2},{1,3},{2,0},{3,1},{4,6},{5,7},{6,4},{7,5},{8,10},{9,11},{10,... | collective-permute-start | bytes 393224 | tf_op jit(solution)/shard_map/sum_rows/ppermute | solution.py:27
  21.1 4.1 %collective-permute-done.9.got = bf16[256,256]{1,0:T(8,128)(2,1)S(1)} collective-permute-done((bf16[256,256]{1,0:T(8,128)(2,1)S(1)}, bf16[256,256]{1,0:T(8,128)(2,1)S(1)}, u32[]{:S(2)}, u32[]{:S(2)}) %collective-permute-start.9) | collective-permute-done | bytes 131104 | tf_op jit(solution)/shard_map/sum_rows/ppermute | solution.py:27
  25.2 0.0 copy-done.1
  25.2 0.0 copy-done.3
  25.2 0.8 %dense.1 = (bf16[128,256]{1,0:T(8,128)(2,1)}, bf16[384,256]{1,0:T(8,128)(2,1)S(1)}, f32[128,256]{1,0:T(8,128)S(1)}) custom-call(bf16[256,256]{1,0:T(8,128)(2,1)S(1)} %add_convert_fusion.mine, bf16[256,256]{1,0:T(8,128)(2,1)S(1)} %collective-permute-done.9.got, bf16[256,256]{1,0:T(8,128)(2,1)S(1)} %copy-done.1, bf16[128,256]{1,0:T(8,128)(2,1)S(1)} %bitcast.15, ...), custom_call_target="tpu_custom_call" | custom-call | tf_op jit(solution)/shard_map/dense/pallas_call | solution.py:228
  26.0 0.0 collective-permute-start.10
  26.0 1.4 %collective-permute-done.10.refs_1_ = bf16[384,256]{1,0:T(8,128)(2,1)S(1)} collective-permute-done((bf16[384,256]{1,0:T(8,128)(2,1)S(1)}, bf16[384,256]{1,0:T(8,128)(2,1)S(1)}, u32[]{:S(2)}, u32[]{:S(2)}) %collective-permute-start.10) | collective-permute-done | bytes 196640 | tf_op jit(solution)/shard_map/swap_cores/ppermute | solution.py:27
  27.5 2.4 %collective-permute-start.11 = (bf16[128,256]{1,0:T(8,128)(2,1)S(1)}, bf16[128,256]{1,0:T(8,128)(2,1)S(1)}, u32[]{:S(2)}, u32[]{:S(2)}) collective-permute-start(bf16[128,256]{1,0:T(8,128)(2,1)S(1)} %add_convert_fusion.7), channel_id=1, source_target_pairs={{0,16},{4,20},{8,24},{12,28},{16,0},{20,4},{24,8},{28,12},{1,17},{... | collective-permute-start | bytes 196616 | tf_op jit(solution)/shard_map/sum_weight/ppermute | solution.py:27
  29.9 0.9 %backward_blocks.1 = (bf16[128,256]{1,0:T(8,128)(2,1)S(1)}, bf16[128,256]{1,0:T(8,128)(2,1)S(1)}, bf16[256,256]{1,0:T(8,128)(2,1)S(1)}, bf16[128,256]{1,0:T(8,12...) custom-call(s32[8,128]{1,0:T(8,128)S(1)} %gather_features.1.info, ...), custom_call_target="tpu_custom_call" | custom-call | tf_op jit(solution)/shard_map/backward_blocks/pallas_call | solution.py:268
  30.8 0.8 %collective-permute-start.13 = (bf16[128,256]{1,0:T(8,128)(2,1)S(1)}, bf16[128,256]{1,0:T(8,128)(2,1)S(1)}, u32[]{:S(2)}, u32[]{:S(2)}) collective-permute-start(bf16[128,256]{1,0:T(8,128)(2,1)S(1)} %get-tuple-element.43), channel_id=1, source_target_pairs={{0,4},{4,0},{8,12},{12,8},{16,20},{20,16},{24,28},{28,24},{1,5},{5... | collective-permute-start | bytes 196616 | tf_op jit(solution)/shard_map/sum_columns/ppermute | solution.py:27
  31.6 1.3 %collective-permute-start.14 = (bf16[128,256]{1,0:T(8,128)(2,1)S(1)}, bf16[128,256]{1,0:T(8,128)(2,1)S(1)}, u32[]{:S(2)}, u32[]{:S(2)}) collective-permute-start(bf16[128,256]{1,0:T(8,128)(2,1)S(1)} %get-tuple-element.44), channel_id=1, source_target_pairs={{0,4},{4,0},{8,12},{12,8},{16,20},{20,16},{24,28},{28,24},{1,5},{5... | collective-permute-start | bytes 196616 | tf_op jit(solution)/shard_map/sum_columns/ppermute | solution.py:27
  32.9 0.7 %collective-permute-start.16 = (bf16[256,256]{1,0:T(8,128)(2,1)S(1)}, bf16[256,256]{1,0:T(8,128)(2,1)S(1)}, u32[]{:S(2)}, u32[]{:S(2)}) collective-permute-start(bf16[256,256]{1,0:T(8,128)(2,1)S(1)} %get-tuple-element.48), channel_id=1, source_target_pairs={{0,4},{4,0},{8,12},{12,8},{16,20},{20,16},{24,28},{28,24},{1,5},{5... | collective-permute-start | bytes 393224 | tf_op jit(solution)/shard_map/sum_columns/ppermute | solution.py:27
  33.6 0.4 collective-permute-done.11
  34.0 1.2 %collective-permute-start.12 = (bf16[128,256]{1,0:T(8,128)(2,1)S(1)}, bf16[128,256]{1,0:T(8,128)(2,1)S(1)}, u32[]{:S(2)}, u32[]{:S(2)}) collective-permute-start(bf16[128,256]{1,0:T(8,128)(2,1)S(1)} %add_convert_fusion.6), channel_id=1, source_target_pairs={{0,8},{4,12},{8,0},{12,4},{16,24},{20,28},{24,16},{28,20},{1,9},{5... | collective-permute-start | bytes 196616 | tf_op jit(solution)/shard_map/sum_columns/sum_weight/sum_weight/ppermute | solution.py:27
  35.2 2.1 %collective-permute-done.14 = bf16[128,256]{1,0:T(8,128)(2,1)S(1)} collective-permute-done((bf16[128,256]{1,0:T(8,128)(2,1)S(1)}, bf16[128,256]{1,0:T(8,128)(2,1)S(1)}, u32[]{:S(2)}, u32[]{:S(2)}) %collective-permute-start.14) | collective-permute-done | bytes 65568 | tf_op jit(solution)/shard_map/sum_columns/ppermute | solution.py:27
  37.3 0.0 collective-permute-done.13
  37.3 1.2 %collective-permute-start.19 = (bf16[128,256]{1,0:T(8,128)(2,1)S(1)}, bf16[128,256]{1,0:T(8,128)(2,1)S(1)}, u32[]{:S(2)}, u32[]{:S(2)}) collective-permute-start(bf16[128,256]{1,0:T(8,128)(2,1)S(1)} %add_convert_fusion.2), channel_id=1, source_target_pairs={{0,24},{4,28},{8,16},{12,20},{16,8},{20,12},{24,0},{28,4},{1,25},{... | collective-permute-start | bytes 196616 | tf_op jit(solution)/shard_map/sum_columns/ppermute | solution.py:27
  38.5 1.1 %collective-permute-start.20 = (bf16[128,256]{1,0:T(8,128)(2,1)S(1)}, bf16[128,256]{1,0:T(8,128)(2,1)S(1)}, u32[]{:S(2)}, u32[]{:S(2)}) collective-permute-start(bf16[128,256]{1,0:T(8,128)(2,1)S(1)} %add_convert_fusion.1), channel_id=1, source_target_pairs={{0,16},{4,20},{8,24},{12,28},{16,0},{20,4},{24,8},{28,12},{1,17},{... | collective-permute-start | bytes 196616 | tf_op jit(solution)/shard_map/sum_columns/ppermute | solution.py:27
  39.6 0.0 collective-permute-done.12
  39.7 1.4 %collective-permute-start.15 = (bf16[128,256]{1,0:T(8,128)(2,1)S(1)}, bf16[128,256]{1,0:T(8,128)(2,1)S(1)}, u32[]{:S(2)}, u32[]{:S(2)}) collective-permute-start(bf16[128,256]{1,0:T(8,128)(2,1)S(1)} %add_convert_fusion.5), channel_id=1, source_target_pairs={{0,4},{4,0},{8,12},{12,8},{16,20},{20,16},{24,28},{28,24},{1,5},{5... | collective-permute-start | bytes 196616 | tf_op jit(solution)/shard_map/sum_columns/sum_weight/sum_weight/ppermute | solution.py:27
  41.1 0.0 collective-permute-done.16.refs_1_
  41.1 1.5 %collective-permute-start.18 = (bf16[128,256]{1,0:T(8,128)(2,1)S(1)}, bf16[128,256]{1,0:T(8,128)(2,1)S(1)}, u32[]{:S(2)}, u32[]{:S(2)}) collective-permute-start(bf16[128,256]{1,0:T(8,128)(2,1)S(1)} %add_convert_fusion.3), channel_id=1, source_target_pairs={{0,8},{4,12},{8,0},{12,4},{16,24},{20,28},{24,16},{28,20},{1,9},{5... | collective-permute-start | bytes 196616 | tf_op jit(solution)/shard_map/sum_columns/ppermute | solution.py:27
  42.6 1.4 %collective-permute-done.15 = bf16[128,256]{1,0:T(8,128)(2,1)S(1)} collective-permute-done((bf16[128,256]{1,0:T(8,128)(2,1)S(1)}, bf16[128,256]{1,0:T(8,128)(2,1)S(1)}, u32[]{:S(2)}, u32[]{:S(2)}) %collective-permute-start.15) | collective-permute-done | bytes 65568 | tf_op jit(solution)/shard_map/sum_columns/sum_weight/sum_weight/ppermute | solution.py:27
  44.0 0.1 collective-permute-start.17
  44.1 0.9 %collective-permute-done.20.refs_2_ = bf16[128,256]{1,0:T(8,128)(2,1)S(1)} collective-permute-done((bf16[128,256]{1,0:T(8,128)(2,1)S(1)}, bf16[128,256]{1,0:T(8,128)(2,1)S(1)}, u32[]{:S(2)}, u32[]{:S(2)}) %collective-permute-start.20) | collective-permute-done | bytes 65568 | tf_op jit(solution)/shard_map/sum_columns/ppermute | solution.py:27
  45.0 0.0 collective-permute-done.19.refs_3_
  45.0 0.7 %collective-permute-done.18.refs_4_ = bf16[128,256]{1,0:T(8,128)(2,1)S(1)} collective-permute-done((bf16[128,256]{1,0:T(8,128)(2,1)S(1)}, bf16[128,256]{1,0:T(8,128)(2,1)S(1)}, u32[]{:S(2)}, u32[]{:S(2)}) %collective-permute-start.18) | collective-permute-done | bytes 65568 | tf_op jit(solution)/shard_map/sum_columns/ppermute | solution.py:27
  45.7 0.0 collective-permute-done.17.other
  45.7 0.8 %shard_map.94 = (f32[128,256]{1,0:T(8,128)}, f32[256,256]{1,0:T(8,128)}) custom-call(bf16[128,256]{1,0:T(8,128)(2,1)S(1)} %add_convert_fusion.4.mine, bf16[128,256]{1,0:T(8,128)(2,1)S(1)} %collective-permute-done.17.other, bf16[256,256]{1,0:T(8,128)(2,1)S(1)} %get-tuple-element.51.refs_0_, bf16[256,256]{1,0:T(8,128)(2,1)S(1)} %collective-permute-done.16.refs_1_, ...), custom_call_target="tpu_custom_call" | custom-call | tf_op jit(solution)/shard_map/pallas_call | solution.py:298
  (9 shorter events, 0.2 us)
Async XLA Ops:
  0.6 7.9 %collective-permute-start = (bf16[128,256]{1,0:T(8,128)(2,1)}, bf16[128,256]{1,0:T(8,128)(2,1)S(1)}, u32[]{:S(2)}, u32[]{:S(2)}) collective-permute-start(bf16[128,256]{1,0:T(8,128)(2,1)} %bitcast.9), channel_id=1, source_target_pairs={{0,8},{4,12},{8,0},{12,4},{16,24},{20,28},{24,16},{28,20},{1,9},{5... | collective-permute-start | bytes 196616 | tf_op jit(solution)/shard_map/gather_features/ppermute | solution.py:27
  3.7 7.1 %collective-permute-start.3 = (bf16[128,256]{1,0:T(8,128)(2,1)}, bf16[128,256]{1,0:T(8,128)(2,1)S(1)}, u32[]{:S(2)}, u32[]{:S(2)}) collective-permute-start(bf16[128,256]{1,0:T(8,128)(2,1)} %bitcast.10), channel_id=1, source_target_pairs={{0,24},{4,28},{8,16},{12,20},{16,8},{20,12},{24,0},{28,4},{1,25},{... | collective-permute-start | bytes 196616 | tf_op jit(solution)/shard_map/gather_features/ppermute | solution.py:27
  6.2 6.7 %collective-permute-start.2 = (bf16[128,256]{1,0:T(8,128)(2,1)}, bf16[128,256]{1,0:T(8,128)(2,1)S(1)}, u32[]{:S(2)}, u32[]{:S(2)}) collective-permute-start(bf16[128,256]{1,0:T(8,128)(2,1)} %bitcast.11), channel_id=1, source_target_pairs={{0,16},{4,20},{8,24},{12,28},{16,0},{20,4},{24,8},{28,12},{1,17},{... | collective-permute-start | bytes 196616 | tf_op jit(solution)/shard_map/gather_features/ppermute | solution.py:27
  6.3 8.1 %collective-permute-start.1 = (bf16[128,256]{1,0:T(8,128)(2,1)}, bf16[128,256]{1,0:T(8,128)(2,1)S(1)}, u32[]{:S(2)}, u32[]{:S(2)}) collective-permute-start(bf16[128,256]{1,0:T(8,128)(2,1)} %bitcast.12), channel_id=1, source_target_pairs={{0,4},{4,0},{8,12},{12,8},{16,20},{20,16},{24,28},{28,24},{1,5},{5... | collective-permute-start | bytes 196616 | tf_op jit(solution)/shard_map/gather_features/ppermute | solution.py:27
  8.5 5.9 %copy-start.4 = (s32[1,1,6]{2,1,0:T(1,128)S(1)}, s32[1,1,6]{2,1,0:T(1,128)}, u32[]{:S(2)}) copy-start(s32[1,1,6]{2,1,0:T(1,128)} %param.10) | copy-start | bytes 76
  8.5 5.9 %copy-start.5 = (s32[1,1,6]{2,1,0:T(1,128)S(1)}, s32[1,1,6]{2,1,0:T(1,128)}, u32[]{:S(2)}) copy-start(s32[1,1,6]{2,1,0:T(1,128)} %param.11) | copy-start | bytes 76
  8.5 8.6 %copy-start = (bf16[1,1,6,128,128]{4,3,2,1,0:T(8,128)(2,1)S(1)}, bf16[1,1,6,128,128]{4,3,2,1,0:T(8,128)(2,1)}, u32[]{:S(2)}) copy-start(bf16[1,1,6,128,128]{4,3,2,1,0:T(8,128)(2,1)} %param.13) | copy-start | bytes 589828
  8.5 8.6 %copy-start.2 = (bf16[1,128,256]{2,1,0:T(8,128)(2,1)S(1)}, bf16[1,128,256]{2,1,0:T(8,128)(2,1)}, u32[]{:S(2)}) copy-start(bf16[1,128,256]{2,1,0:T(8,128)(2,1)} %param.7) | copy-start | bytes 196612
  8.5 5.9 %collective-permute-start.4 = (bf16[128,256]{1,0:T(8,128)(2,1)}, bf16[128,256]{1,0:T(8,128)(2,1)S(1)}, u32[]{:S(2)}, u32[]{:S(2)}) collective-permute-start(bf16[128,256]{1,0:T(8,128)(2,1)} %bitcast.14), channel_id=1, source_target_pairs={{0,2},{1,3},{2,0},{3,1},{4,6},{5,7},{6,4},{7,5},{8,10},{9,11},{10,... | collective-permute-start | bytes 196616 | tf_op jit(solution)/shard_map/gather_features/ppermute | solution.py:27
  10.1 7.0 %collective-permute-start.6 = (bf16[128,256]{1,0:T(8,128)(2,1)S(1)}, bf16[128,256]{1,0:T(8,128)(2,1)S(1)}, u32[]{:S(2)}, u32[]{:S(2)}) collective-permute-start(bf16[128,256]{1,0:T(8,128)(2,1)S(1)} %collective-permute-done.refs_2_), channel_id=1, source_target_pairs={{0,4},{4,0},{8,12},{12,8},{16,20},{20,16},{24,28},{28,24},{1,5},{5... | collective-permute-start | bytes 196616 | tf_op jit(solution)/shard_map/gather_features/ppermute | solution.py:27
  10.8 4.3 %collective-permute-start.7 = (bf16[128,256]{1,0:T(8,128)(2,1)S(1)}, bf16[128,256]{1,0:T(8,128)(2,1)S(1)}, u32[]{:S(2)}, u32[]{:S(2)}) collective-permute-start(bf16[128,256]{1,0:T(8,128)(2,1)S(1)} %collective-permute-done.3.refs_3_), channel_id=1, source_target_pairs={{0,4},{4,0},{8,12},{12,8},{16,20},{20,16},{24,28},{28,24},{1,5},{5... | collective-permute-start | bytes 196616 | tf_op jit(solution)/shard_map/gather_features/ppermute | solution.py:27
  12.9 4.3 %collective-permute-start.5 = (bf16[128,256]{1,0:T(8,128)(2,1)S(1)}, bf16[128,256]{1,0:T(8,128)(2,1)S(1)}, u32[]{:S(2)}, u32[]{:S(2)}) collective-permute-start(bf16[128,256]{1,0:T(8,128)(2,1)S(1)} %collective-permute-done.2.refs_1_), channel_id=1, source_target_pairs={{0,4},{4,0},{8,12},{12,8},{16,20},{20,16},{24,28},{28,24},{1,5},{5... | collective-permute-start | bytes 196616 | tf_op jit(solution)/shard_map/gather_features/ppermute | solution.py:27
  18.1 1.4 %collective-permute-start.8 = (bf16[256,256]{1,0:T(8,128)(2,1)S(1)}, bf16[256,256]{1,0:T(8,128)(2,1)S(1)}, u32[]{:S(2)}, u32[]{:S(2)}) collective-permute-start(bf16[256,256]{1,0:T(8,128)(2,1)S(1)} %get-tuple-element.37), channel_id=1, source_target_pairs={{0,1},{1,0},{2,3},{3,2},{4,5},{5,4},{6,7},{7,6},{8,9},{9,8},{10,11... | collective-permute-start | bytes 393224 | tf_op jit(solution)/shard_map/sum_rows/ppermute | solution.py:27
  19.5 5.7 %copy-start.1 = (bf16[256,256]{1,0:T(8,128)(2,1)S(1)}, bf16[256,256]{1,0:T(8,128)(2,1)}, u32[]{:S(2)}) copy-start(bf16[256,256]{1,0:T(8,128)(2,1)} %weight.1) | copy-start | bytes 393220
  19.5 5.7 %copy-start.3 = (bf16[1,128,256]{2,1,0:T(8,128)(2,1)S(1)}, bf16[1,128,256]{2,1,0:T(8,128)(2,1)}, u32[]{:S(2)}) copy-start(bf16[1,128,256]{2,1,0:T(8,128)(2,1)} %param.9) | copy-start | bytes 196612
  19.5 5.6 %collective-permute-start.9 = (bf16[256,256]{1,0:T(8,128)(2,1)S(1)}, bf16[256,256]{1,0:T(8,128)(2,1)S(1)}, u32[]{:S(2)}, u32[]{:S(2)}) collective-permute-start(bf16[256,256]{1,0:T(8,128)(2,1)S(1)} %add_convert_fusion.mine), channel_id=1, source_target_pairs={{0,2},{1,3},{2,0},{3,1},{4,6},{5,7},{6,4},{7,5},{8,10},{9,11},{10,... | collective-permute-start | bytes 393224 | tf_op jit(solution)/shard_map/sum_rows/ppermute | solution.py:27
  26.0 1.4 %collective-permute-start.10 = (bf16[384,256]{1,0:T(8,128)(2,1)S(1)}, bf16[384,256]{1,0:T(8,128)(2,1)S(1)}, u32[]{:S(2)}, u32[]{:S(2)}) collective-permute-start(bf16[384,256]{1,0:T(8,128)(2,1)S(1)} %get-tuple-element.40.refs_0_), channel_id=1, source_target_pairs={{0,1},{1,0},{2,3},{3,2},{4,5},{5,4},{6,7},{7,6},{8,9},{9,8},{10,11... | collective-permute-start | bytes 589832 | tf_op jit(solution)/shard_map/swap_cores/ppermute | solution.py:27
  27.5 6.5 %collective-permute-start.11 = (bf16[128,256]{1,0:T(8,128)(2,1)S(1)}, bf16[128,256]{1,0:T(8,128)(2,1)S(1)}, u32[]{:S(2)}, u32[]{:S(2)}) collective-permute-start(bf16[128,256]{1,0:T(8,128)(2,1)S(1)} %add_convert_fusion.7), channel_id=1, source_target_pairs={{0,16},{4,20},{8,24},{12,28},{16,0},{20,4},{24,8},{28,12},{1,17},{... | collective-permute-start | bytes 196616 | tf_op jit(solution)/shard_map/sum_weight/ppermute | solution.py:27
  30.8 6.5 %collective-permute-start.13 = (bf16[128,256]{1,0:T(8,128)(2,1)S(1)}, bf16[128,256]{1,0:T(8,128)(2,1)S(1)}, u32[]{:S(2)}, u32[]{:S(2)}) collective-permute-start(bf16[128,256]{1,0:T(8,128)(2,1)S(1)} %get-tuple-element.43), channel_id=1, source_target_pairs={{0,4},{4,0},{8,12},{12,8},{16,20},{20,16},{24,28},{28,24},{1,5},{5... | collective-permute-start | bytes 196616 | tf_op jit(solution)/shard_map/sum_columns/ppermute | solution.py:27
  31.6 5.7 %collective-permute-start.14 = (bf16[128,256]{1,0:T(8,128)(2,1)S(1)}, bf16[128,256]{1,0:T(8,128)(2,1)S(1)}, u32[]{:S(2)}, u32[]{:S(2)}) collective-permute-start(bf16[128,256]{1,0:T(8,128)(2,1)S(1)} %get-tuple-element.44), channel_id=1, source_target_pairs={{0,4},{4,0},{8,12},{12,8},{16,20},{20,16},{24,28},{28,24},{1,5},{5... | collective-permute-start | bytes 196616 | tf_op jit(solution)/shard_map/sum_columns/ppermute | solution.py:27
  32.9 8.2 %collective-permute-start.16 = (bf16[256,256]{1,0:T(8,128)(2,1)S(1)}, bf16[256,256]{1,0:T(8,128)(2,1)S(1)}, u32[]{:S(2)}, u32[]{:S(2)}) collective-permute-start(bf16[256,256]{1,0:T(8,128)(2,1)S(1)} %get-tuple-element.48), channel_id=1, source_target_pairs={{0,4},{4,0},{8,12},{12,8},{16,20},{20,16},{24,28},{28,24},{1,5},{5... | collective-permute-start | bytes 393224 | tf_op jit(solution)/shard_map/sum_columns/ppermute | solution.py:27
  34.0 5.7 %collective-permute-start.12 = (bf16[128,256]{1,0:T(8,128)(2,1)S(1)}, bf16[128,256]{1,0:T(8,128)(2,1)S(1)}, u32[]{:S(2)}, u32[]{:S(2)}) collective-permute-start(bf16[128,256]{1,0:T(8,128)(2,1)S(1)} %add_convert_fusion.6), channel_id=1, source_target_pairs={{0,8},{4,12},{8,0},{12,4},{16,24},{20,28},{24,16},{28,20},{1,9},{5... | collective-permute-start | bytes 196616 | tf_op jit(solution)/shard_map/sum_columns/sum_weight/sum_weight/ppermute | solution.py:27
  37.3 7.7 %collective-permute-start.19 = (bf16[128,256]{1,0:T(8,128)(2,1)S(1)}, bf16[128,256]{1,0:T(8,128)(2,1)S(1)}, u32[]{:S(2)}, u32[]{:S(2)}) collective-permute-start(bf16[128,256]{1,0:T(8,128)(2,1)S(1)} %add_convert_fusion.2), channel_id=1, source_target_pairs={{0,24},{4,28},{8,16},{12,20},{16,8},{20,12},{24,0},{28,4},{1,25},{... | collective-permute-start | bytes 196616 | tf_op jit(solution)/shard_map/sum_columns/ppermute | solution.py:27
  38.5 6.5 %collective-permute-start.20 = (bf16[128,256]{1,0:T(8,128)(2,1)S(1)}, bf16[128,256]{1,0:T(8,128)(2,1)S(1)}, u32[]{:S(2)}, u32[]{:S(2)}) collective-permute-start(bf16[128,256]{1,0:T(8,128)(2,1)S(1)} %add_convert_fusion.1), channel_id=1, source_target_pairs={{0,16},{4,20},{8,24},{12,28},{16,0},{20,4},{24,8},{28,12},{1,17},{... | collective-permute-start | bytes 196616 | tf_op jit(solution)/shard_map/sum_columns/ppermute | solution.py:27
  39.7 4.3 %collective-permute-start.15 = (bf16[128,256]{1,0:T(8,128)(2,1)S(1)}, bf16[128,256]{1,0:T(8,128)(2,1)S(1)}, u32[]{:S(2)}, u32[]{:S(2)}) collective-permute-start(bf16[128,256]{1,0:T(8,128)(2,1)S(1)} %add_convert_fusion.5), channel_id=1, source_target_pairs={{0,4},{4,0},{8,12},{12,8},{16,20},{20,16},{24,28},{28,24},{1,5},{5... | collective-permute-start | bytes 196616 | tf_op jit(solution)/shard_map/sum_columns/sum_weight/sum_weight/ppermute | solution.py:27
  41.1 4.5 %collective-permute-start.18 = (bf16[128,256]{1,0:T(8,128)(2,1)S(1)}, bf16[128,256]{1,0:T(8,128)(2,1)S(1)}, u32[]{:S(2)}, u32[]{:S(2)}) collective-permute-start(bf16[128,256]{1,0:T(8,128)(2,1)S(1)} %add_convert_fusion.3), channel_id=1, source_target_pairs={{0,8},{4,12},{8,0},{12,4},{16,24},{20,28},{24,16},{28,20},{1,9},{5... | collective-permute-start | bytes 196616 | tf_op jit(solution)/shard_map/sum_columns/ppermute | solution.py:27
  44.0 1.6 %collective-permute-start.17 = (bf16[128,256]{1,0:T(8,128)(2,1)S(1)}, bf16[128,256]{1,0:T(8,128)(2,1)S(1)}, u32[]{:S(2)}, u32[]{:S(2)}) collective-permute-start(bf16[128,256]{1,0:T(8,128)(2,1)S(1)} %add_convert_fusion.4.mine), channel_id=1, source_target_pairs={{0,1},{1,0},{2,3},{3,2},{4,5},{5,4},{6,7},{7,6},{8,9},{9,8},{10,11... | collective-permute-start | bytes 196616 | tf_op jit(solution)/shard_map/sum_weight/ppermute | solution.py:27

commit v4 on v3

--- a/solution.py
+++ b/solution.py
@@ -25,6 +25,21 @@
 def swap(value, axis, mask):
     size = lax.axis_size(axis)
     return lax.ppermute(value, axis, [(i, i ^ mask) for i in range(size)])
+
+
+def swap_crossed(value, mask):
+    rows, cols = lax.axis_size("gr"), lax.axis_size("gc")
+    pairs = [
+        (r * cols + c, (r ^ mask) * cols + (c ^ 1)) for r in range(rows) for c in range(cols)
+    ]
+    return lax.ppermute(value, ("gr", "gc"), pairs)
+
+
+def weight_half():
+    half, rows = lax.axis_index("gc"), lax.axis_index("gr")
+    for b in range(lax.axis_size("gr").bit_length() - 1):
+        half = half ^ (rows >> b)
+    return half & 1
 
 
 def bits_of(axis):
@@ -147,7 +162,7 @@
         lax.dot_general(grad_pre, w, RIGHT_T, preferred_element_type=jnp.float32)
     )
     total[...] = lax.dot_general(hidden, grad_pre, LEFT_T, preferred_element_type=jnp.float32)
-    place = lax.axis_index("gc") & 1
+    place = weight_half()
     kept[...] = total[pl.ds(pl.multiple_of(place * half, half), half), :]
     message[pl.ds(blocks * side, half), :] = bf16(
         total[pl.ds(pl.multiple_of((1 - place) * half, half), half), :]
@@ -160,7 +175,7 @@
     parts = [f32(v[pl.ds(side, side), :]) for v in (kept, part)] + [f32(t[...]) for t in terms]
     grad_features[...] = functools.reduce(lambda a, b: a + b, parts)
     half = mine.shape[0]
-    place = lax.axis_index("gc") & 1
+    place = weight_half()
     grad_weight[pl.ds(pl.multiple_of(place * half, half), half), :] = f32(mine[...])
     grad_weight[pl.ds(pl.multiple_of((1 - place) * half, half), half), :] = f32(other[...])
 
@@ -241,13 +256,13 @@
     with jax.named_scope("swap_cores"):
         answer = swap(message, "gc", 1)
         running = kept + f32(answer[mine.shape[0]:])
-    stages = [("gr", bit) for bit in bits_of("gr")[:0:-1] + [1]]
+    stages = bits_of("gr")[:0:-1] + [1]
     sent, got, order = [], [], Line()
 
     def launch(running):
         with jax.named_scope("sum_weight"):
             sent.append(bf16(running))
-            got.append(swap(sent[-1], *stages[len(sent) - 1]))
+            got.append(swap_crossed(sent[-1], stages[len(sent) - 1]))
 
     def advance():
         if len(sent) > len(stages):
@@ -282,14 +297,15 @@
         arrived = [swap(v, "gr", 1) for v in sends]
         order(keeps[0])
         advance()
-        terms = []
+        parts = []
         for masks, kept, part in zip(kept_masks[:-1], keeps, arrived):
             total = bf16(f32(kept) + f32(order(part)))
-            terms.append(swap(total, "gr", masks[0]))
-        advance()
+            parts += [(m, total[n * side : (n + 1) * side]) for n, m in enumerate(masks)]
+        terms = [swap(v, "gr", m) for m, v in parts]
         own = (keeps[-1], order(arrived[-1]))
         total = bf16(f32(own[0][:side]) + f32(own[1][:side]))
         terms.append(swap(total, "gr", 2))
+        advance()
     while len(sent) <= len(stages):
         advance()
     terms = [order(term) for term in terms]

time: 46.6 us -> 46.4 us (level)
  starting transfers between devices: 25.6 us -> 23.7 us
  waiting for transfers between devices: 15.7 us -> 17.4 us
    ppermute x21 -> x18, starting transfers between devices: 25.6 us -> 21.1 us  [swap(): return lax.ppermute(value, axis, [(i, i ^ mask) for i in range(size)])]
    ppermute x0 -> x3, waiting for transfers between devices: none -> 2.63 us  [swap_crossed(): return lax.ppermute(value, ('gr', 'gc'), pairs)]
    ppermute x0 -> x3, starting transfers between devices: none -> 2.54 us  [swap_crossed(): return lax.ppermute(value, ('gr', 'gc'), pairs)]
    ppermute x21 -> x18, waiting for transfers between devices: 15.7 us -> 14.8 us  [swap(): return lax.ppermute(value, axis, [(i, i ^ mask) for i in range(size)])]
  transfers between devices with their start and end apart: 21 -> 21, of which waited for: 12 -> 11; matrix products, arithmetic and copies ran while one was open for 0% -> 0% of each run, Pallas kernels for 2% -> 2%
where the time goes in v4:
time: 46.4 us; the launch traced here: 46.2 us
  starting transfers between devices  23.7 us (51%)
  waiting for transfers between devices  17.4 us (37%)
  Pallas kernels  3.54 us (8%)
  between operations  1.43 us (3%)
    ppermute x18, starting transfers between devices, swap(): return lax.ppermute(value, axis, [(i, i ^ mask) for i in range(size)])  21.1 us
    ppermute x18, waiting for transfers between devices, swap(): return lax.ppermute(value, axis, [(i, i ^ mask) for i in range(size)])  14.8 us
    ppermute x3, waiting for transfers between devices, swap_crossed(): return lax.ppermute(value, ('gr', 'gc'), pairs)  2.63 us
    ppermute x3, starting transfers between devices, swap_crossed(): return lax.ppermute(value, ('gr', 'gc'), pairs)  2.54 us
    pallas_call x1, Pallas kernels, per_device(): pl.pallas_call(functools.partial(backward_kernel, [keep_masks, send_masks...  0.95 us
  transfers between devices with their start and end apart: 21, of which 11 were waited for; matrix products, arithmetic and copies ran while one was open for 0% of the time, Pallas kernels for 2%

profile of v4, /device:TPU:0, one launch (start us, length us, event | category | flops | bytes accessed | tf_op | source)
XLA Modules:
  0.0 46.2 jit_solution(8116711525099467411)
XLA Ops:
  0.6 3.1 %collective-permute-start = (bf16[128,256]{1,0:T(8,128)(2,1)}, bf16[128,256]{1,0:T(8,128)(2,1)S(1)}, u32[]{:S(2)}, u32[]{:S(2)}) collective-permute-start(bf16[128,256]{1,0:T(8,128)(2,1)} %bitcast.9), channel_id=1, source_target_pairs={{0,8},{4,12},{8,0},{12,4},{16,24},{20,28},{24,16},{28,20},{1,9},{5... | collective-permute-start | bytes 196616 | tf_op jit(solution)/shard_map/gather_features/ppermute | solution.py:27
  3.7 2.5 %collective-permute-start.3 = (bf16[128,256]{1,0:T(8,128)(2,1)}, bf16[128,256]{1,0:T(8,128)(2,1)S(1)}, u32[]{:S(2)}, u32[]{:S(2)}) collective-permute-start(bf16[128,256]{1,0:T(8,128)(2,1)} %bitcast.10), channel_id=1, source_target_pairs={{0,24},{4,28},{8,16},{12,20},{16,8},{20,12},{24,0},{28,4},{1,25},{... | collective-permute-start | bytes 196616 | tf_op jit(solution)/shard_map/gather_features/ppermute | solution.py:27
  6.2 0.1 collective-permute-start.2
  6.3 1.5 %collective-permute-start.1 = (bf16[128,256]{1,0:T(8,128)(2,1)}, bf16[128,256]{1,0:T(8,128)(2,1)S(1)}, u32[]{:S(2)}, u32[]{:S(2)}) collective-permute-start(bf16[128,256]{1,0:T(8,128)(2,1)} %bitcast.12), channel_id=1, source_target_pairs={{0,4},{4,0},{8,12},{12,8},{16,20},{20,16},{24,28},{28,24},{1,5},{5... | collective-permute-start | bytes 196616 | tf_op jit(solution)/shard_map/gather_features/ppermute | solution.py:27
  8.5 0.0 collective-permute-done.refs_2_
  8.5 0.0 copy-start.4
  8.5 0.0 copy-start.5
  8.5 0.0 copy-start
  8.5 0.0 copy-start.2
  8.5 1.6 %collective-permute-start.4 = (bf16[128,256]{1,0:T(8,128)(2,1)}, bf16[128,256]{1,0:T(8,128)(2,1)S(1)}, u32[]{:S(2)}, u32[]{:S(2)}) collective-permute-start(bf16[128,256]{1,0:T(8,128)(2,1)} %bitcast.14), channel_id=1, source_target_pairs={{0,2},{1,3},{2,0},{3,1},{4,6},{5,7},{6,4},{7,5},{8,10},{9,11},{10,... | collective-permute-start | bytes 196616 | tf_op jit(solution)/shard_map/gather_features/ppermute | solution.py:27
  10.1 0.5 %collective-permute-start.6 = (bf16[128,256]{1,0:T(8,128)(2,1)S(1)}, bf16[128,256]{1,0:T(8,128)(2,1)S(1)}, u32[]{:S(2)}, u32[]{:S(2)}) collective-permute-start(bf16[128,256]{1,0:T(8,128)(2,1)S(1)} %collective-permute-done.refs_2_), channel_id=1, source_target_pairs={{0,4},{4,0},{8,12},{12,8},{16,20},{20,16},{24,28},{28,24},{1,5},{5... | collective-permute-start | bytes 196616 | tf_op jit(solution)/shard_map/gather_features/ppermute | solution.py:27
  10.6 0.2 collective-permute-done.3.refs_3_
  10.8 1.5 %collective-permute-start.7 = (bf16[128,256]{1,0:T(8,128)(2,1)S(1)}, bf16[128,256]{1,0:T(8,128)(2,1)S(1)}, u32[]{:S(2)}, u32[]{:S(2)}) collective-permute-start(bf16[128,256]{1,0:T(8,128)(2,1)S(1)} %collective-permute-done.3.refs_3_), channel_id=1, source_target_pairs={{0,4},{4,0},{8,12},{12,8},{16,20},{20,16},{24,28},{28,24},{1,5},{5... | collective-permute-start | bytes 196616 | tf_op jit(solution)/shard_map/gather_features/ppermute | solution.py:27
  12.3 0.6 %collective-permute-done.2.refs_1_ = bf16[128,256]{1,0:T(8,128)(2,1)S(1)} collective-permute-done((bf16[128,256]{1,0:T(8,128)(2,1)}, bf16[128,256]{1,0:T(8,128)(2,1)S(1)}, u32[]{:S(2)}, u32[]{:S(2)}) %collective-permute-start.2) | collective-permute-done | bytes 65568 | tf_op jit(solution)/shard_map/gather_features/ppermute | solution.py:27
  12.9 1.5 %collective-permute-start.5 = (bf16[128,256]{1,0:T(8,128)(2,1)S(1)}, bf16[128,256]{1,0:T(8,128)(2,1)S(1)}, u32[]{:S(2)}, u32[]{:S(2)}) collective-permute-start(bf16[128,256]{1,0:T(8,128)(2,1)S(1)} %collective-permute-done.2.refs_1_), channel_id=1, source_target_pairs={{0,4},{4,0},{8,12},{12,8},{16,20},{20,16},{24,28},{28,24},{1,5},{5... | collective-permute-start | bytes 196616 | tf_op jit(solution)/shard_map/gather_features/ppermute | solution.py:27
  14.4 0.0 copy-done.4
  14.4 0.0 copy-done.5
  14.4 0.0 collective-permute-done.4.refs_1_
  14.4 0.0 collective-permute-done.1.refs_0_
  14.4 0.6 %collective-permute-done.7.refs_7_ = bf16[128,256]{1,0:T(8,128)(2,1)S(1)} collective-permute-done((bf16[128,256]{1,0:T(8,128)(2,1)S(1)}, bf16[128,256]{1,0:T(8,128)(2,1)S(1)}, u32[]{:S(2)}, u32[]{:S(2)}) %collective-permute-start.7) | collective-permute-done | bytes 65568 | tf_op jit(solution)/shard_map/gather_features/ppermute | solution.py:27
  15.1 2.1 %collective-permute-done.5.refs_5_ = bf16[128,256]{1,0:T(8,128)(2,1)S(1)} collective-permute-done((bf16[128,256]{1,0:T(8,128)(2,1)S(1)}, bf16[128,256]{1,0:T(8,128)(2,1)S(1)}, u32[]{:S(2)}, u32[]{:S(2)}) %collective-permute-start.5) | collective-permute-done | bytes 65568 | tf_op jit(solution)/shard_map/gather_features/ppermute | solution.py:27
  17.1 0.0 collective-permute-done.6.refs_6_
  17.1 0.0 copy-done
  17.1 0.0 copy-done.2
  17.1 0.9 %forward_blocks.1 = (bf16[256,256]{1,0:T(8,128)(2,1)S(1)}, bf16[256,256]{1,0:T(8,128)(2,1)S(1)}) custom-call(s32[8,128]{1,0:T(8,128)S(1)} %gather_features.1.info, bf16[6,128,128]{2,1,0:T(8,128)(2,1)S(1)} %bitcast.7, bf16[128,256]{1,0:T(8,128)(2,1)S(1)} %collective-permute-done.1.refs_0_, bf16[128,256]{1,0:T(8,128)(2,1)S(1)} %collective-permute-done.2.refs_1_, ...), custom_call_target="tpu_custom_call" | custom-call | tf_op jit(solution)/shard_map/forward_blocks/pallas_call | solution.py:219
  18.1 0.1 collective-permute-start.8
  18.2 1.3 %collective-permute-done.8 = bf16[256,256]{1,0:T(8,128)(2,1)S(1)} collective-permute-done((bf16[256,256]{1,0:T(8,128)(2,1)S(1)}, bf16[256,256]{1,0:T(8,128)(2,1)S(1)}, u32[]{:S(2)}, u32[]{:S(2)}) %collective-permute-start.8) | collective-permute-done | bytes 131104 | tf_op jit(solution)/shard_map/sum_rows/ppermute | solution.py:27
  19.5 0.0 copy-start.1
  19.5 0.0 copy-start.3
  19.5 1.6 %collective-permute-start.9 = (bf16[256,256]{1,0:T(8,128)(2,1)S(1)}, bf16[256,256]{1,0:T(8,128)(2,1)S(1)}, u32[]{:S(2)}, u32[]{:S(2)}) collective-permute-start(bf16[256,256]{1,0:T(8,128)(2,1)S(1)} %add_convert_fusion.mine), channel_id=1, source_target_pairs={{0,2},{1,3},{2,0},{3,1},{4,6},{5,7},{6,4},{7,5},{8,10},{9,11},{10,... | collective-permute-start | bytes 393224 | tf_op jit(solution)/shard_map/sum_rows/ppermute | solution.py:27
  21.1 4.1 %collective-permute-done.9.got = bf16[256,256]{1,0:T(8,128)(2,1)S(1)} collective-permute-done((bf16[256,256]{1,0:T(8,128)(2,1)S(1)}, bf16[256,256]{1,0:T(8,128)(2,1)S(1)}, u32[]{:S(2)}, u32[]{:S(2)}) %collective-permute-start.9) | collective-permute-done | bytes 131104 | tf_op jit(solution)/shard_map/sum_rows/ppermute | solution.py:27
  25.2 0.0 copy-done.1
  25.2 0.0 copy-done.3
  25.2 0.8 %dense.1 = (bf16[128,256]{1,0:T(8,128)(2,1)}, bf16[384,256]{1,0:T(8,128)(2,1)S(1)}, f32[128,256]{1,0:T(8,128)S(1)}) custom-call(bf16[256,256]{1,0:T(8,128)(2,1)S(1)} %add_convert_fusion.mine, bf16[256,256]{1,0:T(8,128)(2,1)S(1)} %collective-permute-done.9.got, bf16[256,256]{1,0:T(8,128)(2,1)S(1)} %copy-done.1, bf16[128,256]{1,0:T(8,128)(2,1)S(1)} %bitcast.15, ...), custom_call_target="tpu_custom_call" | custom-call | tf_op jit(solution)/shard_map/dense/pallas_call | solution.py:243
  26.0 0.0 collective-permute-start.10
  26.0 1.4 %collective-permute-done.10.refs_1_ = bf16[384,256]{1,0:T(8,128)(2,1)S(1)} collective-permute-done((bf16[384,256]{1,0:T(8,128)(2,1)S(1)}, bf16[384,256]{1,0:T(8,128)(2,1)S(1)}, u32[]{:S(2)}, u32[]{:S(2)}) %collective-permute-start.10) | collective-permute-done | bytes 196640 | tf_op jit(solution)/shard_map/swap_cores/ppermute | solution.py:27
  27.5 2.1 %collective-permute-start.11 = (bf16[128,256]{1,0:T(8,128)(2,1)S(1)}, bf16[128,256]{1,0:T(8,128)(2,1)S(1)}, u32[]{:S(2)}, u32[]{:S(2)}) collective-permute-start(bf16[128,256]{1,0:T(8,128)(2,1)S(1)} %add_convert_fusion.7), channel_id=1, source_target_pairs={{0,17},{1,16},{2,19},{3,18},{4,21},{5,20},{6,23},{7,22},{8,25},{9,... | collective-permute-start | bytes 196616 | tf_op jit(solution)/shard_map/sum_weight/ppermute | solution.py:35
  29.6 1.0 %backward_blocks.1 = (bf16[128,256]{1,0:T(8,128)(2,1)S(1)}, bf16[128,256]{1,0:T(8,128)(2,1)S(1)}, bf16[256,256]{1,0:T(8,128)(2,1)S(1)}, bf16[128,256]{1,0:T(8,12...) custom-call(s32[8,128]{1,0:T(8,128)S(1)} %gather_features.1.info, ...), custom_call_target="tpu_custom_call" | custom-call | tf_op jit(solution)/shard_map/backward_blocks/pallas_call | solution.py:283
  30.6 0.8 %collective-permute-start.14 = (bf16[128,256]{1,0:T(8,128)(2,1)S(1)}, bf16[128,256]{1,0:T(8,128)(2,1)S(1)}, u32[]{:S(2)}, u32[]{:S(2)}) collective-permute-start(bf16[128,256]{1,0:T(8,128)(2,1)S(1)} %get-tuple-element.44), channel_id=1, source_target_pairs={{0,4},{4,0},{8,12},{12,8},{16,20},{20,16},{24,28},{28,24},{1,5},{5... | collective-permute-start | bytes 196616 | tf_op jit(solution)/shard_map/sum_columns/ppermute | solution.py:27
  31.3 1.3 %collective-permute-start.15 = (bf16[128,256]{1,0:T(8,128)(2,1)S(1)}, bf16[128,256]{1,0:T(8,128)(2,1)S(1)}, u32[]{:S(2)}, u32[]{:S(2)}) collective-permute-start(bf16[128,256]{1,0:T(8,128)(2,1)S(1)} %get-tuple-element.45), channel_id=1, source_target_pairs={{0,4},{4,0},{8,12},{12,8},{16,20},{20,16},{24,28},{28,24},{1,5},{5... | collective-permute-start | bytes 196616 | tf_op jit(solution)/shard_map/sum_columns/ppermute | solution.py:27
  32.7 0.7 %collective-permute-start.13 = (bf16[256,256]{1,0:T(8,128)(2,1)S(1)}, bf16[256,256]{1,0:T(8,128)(2,1)S(1)}, u32[]{:S(2)}, u32[]{:S(2)}) collective-permute-start(bf16[256,256]{1,0:T(8,128)(2,1)S(1)} %get-tuple-element.43), channel_id=1, source_target_pairs={{0,4},{4,0},{8,12},{12,8},{16,20},{20,16},{24,28},{28,24},{1,5},{5... | collective-permute-start | bytes 393224 | tf_op jit(solution)/shard_map/sum_columns/ppermute | solution.py:27
  33.4 0.5 %collective-permute-done.11 = bf16[128,256]{1,0:T(8,128)(2,1)S(1)} collective-permute-done((bf16[128,256]{1,0:T(8,128)(2,1)S(1)}, bf16[128,256]{1,0:T(8,128)(2,1)S(1)}, u32[]{:S(2)}, u32[]{:S(2)}) %collective-permute-start.11) | collective-permute-done | bytes 65568 | tf_op jit(solution)/shard_map/sum_weight/ppermute | solution.py:35
  33.9 0.1 collective-permute-start.12
  34.0 2.9 %collective-permute-done.15 = bf16[128,256]{1,0:T(8,128)(2,1)S(1)} collective-permute-done((bf16[128,256]{1,0:T(8,128)(2,1)S(1)}, bf16[128,256]{1,0:T(8,128)(2,1)S(1)}, u32[]{:S(2)}, u32[]{:S(2)}) %collective-permute-start.15) | collective-permute-done | bytes 65568 | tf_op jit(solution)/shard_map/sum_columns/ppermute | solution.py:27
  37.0 0.0 collective-permute-done.14
  37.0 1.1 %collective-permute-start.19 = (bf16[128,256]{1,0:T(8,128)(2,1)S(1)}, bf16[128,256]{1,0:T(8,128)(2,1)S(1)}, u32[]{:S(2)}, u32[]{:S(2)}) collective-permute-start(bf16[128,256]{1,0:T(8,128)(2,1)S(1)} %add_convert_fusion.2), channel_id=1, source_target_pairs={{0,24},{4,28},{8,16},{12,20},{16,8},{20,12},{24,0},{28,4},{1,25},{... | collective-permute-start | bytes 196616 | tf_op jit(solution)/shard_map/sum_columns/ppermute | solution.py:27
  38.2 1.2 %collective-permute-start.20 = (bf16[128,256]{1,0:T(8,128)(2,1)S(1)}, bf16[128,256]{1,0:T(8,128)(2,1)S(1)}, u32[]{:S(2)}, u32[]{:S(2)}) collective-permute-start(bf16[128,256]{1,0:T(8,128)(2,1)S(1)} %add_convert_fusion.1), channel_id=1, source_target_pairs={{0,16},{4,20},{8,24},{12,28},{16,0},{20,4},{24,8},{28,12},{1,17},{... | collective-permute-start | bytes 196616 | tf_op jit(solution)/shard_map/sum_columns/ppermute | solution.py:27
  39.3 0.0 collective-permute-done.13.refs_1_
  39.3 0.0 collective-permute-done.12
  39.4 0.3 collective-permute-start.16
  39.7 2.0 %collective-permute-start.18 = (bf16[128,256]{1,0:T(8,128)(2,1)S(1)}, bf16[128,256]{1,0:T(8,128)(2,1)S(1)}, u32[]{:S(2)}, u32[]{:S(2)}) collective-permute-start(bf16[128,256]{1,0:T(8,128)(2,1)S(1)} %add_convert_fusion.3), channel_id=1, source_target_pairs={{0,8},{4,12},{8,0},{12,4},{16,24},{20,28},{24,16},{28,20},{1,9},{5... | collective-permute-start | bytes 196616 | tf_op jit(solution)/shard_map/sum_columns/ppermute | solution.py:27
  41.7 2.1 %collective-permute-done.16 = bf16[128,256]{1,0:T(8,128)(2,1)S(1)} collective-permute-done((bf16[128,256]{1,0:T(8,128)(2,1)S(1)}, bf16[128,256]{1,0:T(8,128)(2,1)S(1)}, u32[]{:S(2)}, u32[]{:S(2)}) %collective-permute-start.16) | collective-permute-done | bytes 65568 | tf_op jit(solution)/shard_map/sum_columns/sum_weight/sum_weight/ppermute | solution.py:35
  43.8 0.1 collective-permute-start.17
  43.9 1.5 %collective-permute-done.20.refs_2_ = bf16[128,256]{1,0:T(8,128)(2,1)S(1)} collective-permute-done((bf16[128,256]{1,0:T(8,128)(2,1)S(1)}, bf16[128,256]{1,0:T(8,128)(2,1)S(1)}, u32[]{:S(2)}, u32[]{:S(2)}) %collective-permute-start.20) | collective-permute-done | bytes 65568 | tf_op jit(solution)/shard_map/sum_columns/ppermute | solution.py:27
  45.4 0.0 collective-permute-done.19.refs_3_
  45.4 0.0 collective-permute-done.18.refs_4_
  45.4 0.0 collective-permute-done.17.other
  45.4 0.8 %shard_map.94 = (f32[128,256]{1,0:T(8,128)}, f32[256,256]{1,0:T(8,128)}) custom-call(bf16[128,256]{1,0:T(8,128)(2,1)S(1)} %add_convert_fusion.4.mine, bf16[128,256]{1,0:T(8,128)(2,1)S(1)} %collective-permute-done.17.other, bf16[256,256]{1,0:T(8,128)(2,1)S(1)} %get-tuple-element.51.refs_0_, bf16[256,256]{1,0:T(8,128)(2,1)S(1)} %collective-permute-done.13.refs_1_, ...), custom_call_target="tpu_custom_call" | custom-call | tf_op jit(solution)/shard_map/pallas_call | solution.py:314
  (9 shorter events, 0.2 us)
Async XLA Ops:
  0.6 7.9 %collective-permute-start = (bf16[128,256]{1,0:T(8,128)(2,1)}, bf16[128,256]{1,0:T(8,128)(2,1)S(1)}, u32[]{:S(2)}, u32[]{:S(2)}) collective-permute-start(bf16[128,256]{1,0:T(8,128)(2,1)} %bitcast.9), channel_id=1, source_target_pairs={{0,8},{4,12},{8,0},{12,4},{16,24},{20,28},{24,16},{28,20},{1,9},{5... | collective-permute-start | bytes 196616 | tf_op jit(solution)/shard_map/gather_features/ppermute | solution.py:27
  3.7 7.1 %collective-permute-start.3 = (bf16[128,256]{1,0:T(8,128)(2,1)}, bf16[128,256]{1,0:T(8,128)(2,1)S(1)}, u32[]{:S(2)}, u32[]{:S(2)}) collective-permute-start(bf16[128,256]{1,0:T(8,128)(2,1)} %bitcast.10), channel_id=1, source_target_pairs={{0,24},{4,28},{8,16},{12,20},{16,8},{20,12},{24,0},{28,4},{1,25},{... | collective-permute-start | bytes 196616 | tf_op jit(solution)/shard_map/gather_features/ppermute | solution.py:27
  6.2 6.7 %collective-permute-start.2 = (bf16[128,256]{1,0:T(8,128)(2,1)}, bf16[128,256]{1,0:T(8,128)(2,1)S(1)}, u32[]{:S(2)}, u32[]{:S(2)}) collective-permute-start(bf16[128,256]{1,0:T(8,128)(2,1)} %bitcast.11), channel_id=1, source_target_pairs={{0,16},{4,20},{8,24},{12,28},{16,0},{20,4},{24,8},{28,12},{1,17},{... | collective-permute-start | bytes 196616 | tf_op jit(solution)/shard_map/gather_features/ppermute | solution.py:27
  6.3 8.1 %collective-permute-start.1 = (bf16[128,256]{1,0:T(8,128)(2,1)}, bf16[128,256]{1,0:T(8,128)(2,1)S(1)}, u32[]{:S(2)}, u32[]{:S(2)}) collective-permute-start(bf16[128,256]{1,0:T(8,128)(2,1)} %bitcast.12), channel_id=1, source_target_pairs={{0,4},{4,0},{8,12},{12,8},{16,20},{20,16},{24,28},{28,24},{1,5},{5... | collective-permute-start | bytes 196616 | tf_op jit(solution)/shard_map/gather_features/ppermute | solution.py:27
  8.5 5.9 %copy-start.4 = (s32[1,1,6]{2,1,0:T(1,128)S(1)}, s32[1,1,6]{2,1,0:T(1,128)}, u32[]{:S(2)}) copy-start(s32[1,1,6]{2,1,0:T(1,128)} %param.10) | copy-start | bytes 76
  8.5 5.9 %copy-start.5 = (s32[1,1,6]{2,1,0:T(1,128)S(1)}, s32[1,1,6]{2,1,0:T(1,128)}, u32[]{:S(2)}) copy-start(s32[1,1,6]{2,1,0:T(1,128)} %param.11) | copy-start | bytes 76
  8.5 8.6 %copy-start = (bf16[1,1,6,128,128]{4,3,2,1,0:T(8,128)(2,1)S(1)}, bf16[1,1,6,128,128]{4,3,2,1,0:T(8,128)(2,1)}, u32[]{:S(2)}) copy-start(bf16[1,1,6,128,128]{4,3,2,1,0:T(8,128)(2,1)} %param.13) | copy-start | bytes 589828
  8.5 8.6 %copy-start.2 = (bf16[1,128,256]{2,1,0:T(8,128)(2,1)S(1)}, bf16[1,128,256]{2,1,0:T(8,128)(2,1)}, u32[]{:S(2)}) copy-start(bf16[1,128,256]{2,1,0:T(8,128)(2,1)} %param.7) | copy-start | bytes 196612
  8.5 5.9 %collective-permute-start.4 = (bf16[128,256]{1,0:T(8,128)(2,1)}, bf16[128,256]{1,0:T(8,128)(2,1)S(1)}, u32[]{:S(2)}, u32[]{:S(2)}) collective-permute-start(bf16[128,256]{1,0:T(8,128)(2,1)} %bitcast.14), channel_id=1, source_target_pairs={{0,2},{1,3},{2,0},{3,1},{4,6},{5,7},{6,4},{7,5},{8,10},{9,11},{10,... | collective-permute-start | bytes 196616 | tf_op jit(solution)/shard_map/gather_features/ppermute | solution.py:27
  10.1 7.0 %collective-permute-start.6 = (bf16[128,256]{1,0:T(8,128)(2,1)S(1)}, bf16[128,256]{1,0:T(8,128)(2,1)S(1)}, u32[]{:S(2)}, u32[]{:S(2)}) collective-permute-start(bf16[128,256]{1,0:T(8,128)(2,1)S(1)} %collective-permute-done.refs_2_), channel_id=1, source_target_pairs={{0,4},{4,0},{8,12},{12,8},{16,20},{20,16},{24,28},{28,24},{1,5},{5... | collective-permute-start | bytes 196616 | tf_op jit(solution)/shard_map/gather_features/ppermute | solution.py:27
  10.8 4.3 %collective-permute-start.7 = (bf16[128,256]{1,0:T(8,128)(2,1)S(1)}, bf16[128,256]{1,0:T(8,128)(2,1)S(1)}, u32[]{:S(2)}, u32[]{:S(2)}) collective-permute-start(bf16[128,256]{1,0:T(8,128)(2,1)S(1)} %collective-permute-done.3.refs_3_), channel_id=1, source_target_pairs={{0,4},{4,0},{8,12},{12,8},{16,20},{20,16},{24,28},{28,24},{1,5},{5... | collective-permute-start | bytes 196616 | tf_op jit(solution)/shard_map/gather_features/ppermute | solution.py:27
  12.9 4.3 %collective-permute-start.5 = (bf16[128,256]{1,0:T(8,128)(2,1)S(1)}, bf16[128,256]{1,0:T(8,128)(2,1)S(1)}, u32[]{:S(2)}, u32[]{:S(2)}) collective-permute-start(bf16[128,256]{1,0:T(8,128)(2,1)S(1)} %collective-permute-done.2.refs_1_), channel_id=1, source_target_pairs={{0,4},{4,0},{8,12},{12,8},{16,20},{20,16},{24,28},{28,24},{1,5},{5... | collective-permute-start | bytes 196616 | tf_op jit(solution)/shard_map/gather_features/ppermute | solution.py:27
  18.1 1.4 %collective-permute-start.8 = (bf16[256,256]{1,0:T(8,128)(2,1)S(1)}, bf16[256,256]{1,0:T(8,128)(2,1)S(1)}, u32[]{:S(2)}, u32[]{:S(2)}) collective-permute-start(bf16[256,256]{1,0:T(8,128)(2,1)S(1)} %get-tuple-element.37), channel_id=1, source_target_pairs={{0,1},{1,0},{2,3},{3,2},{4,5},{5,4},{6,7},{7,6},{8,9},{9,8},{10,11... | collective-permute-start | bytes 393224 | tf_op jit(solution)/shard_map/sum_rows/ppermute | solution.py:27
  19.5 5.7 %copy-start.1 = (bf16[256,256]{1,0:T(8,128)(2,1)S(1)}, bf16[256,256]{1,0:T(8,128)(2,1)}, u32[]{:S(2)}) copy-start(bf16[256,256]{1,0:T(8,128)(2,1)} %weight.1) | copy-start | bytes 393220
  19.5 5.7 %copy-start.3 = (bf16[1,128,256]{2,1,0:T(8,128)(2,1)S(1)}, bf16[1,128,256]{2,1,0:T(8,128)(2,1)}, u32[]{:S(2)}) copy-start(bf16[1,128,256]{2,1,0:T(8,128)(2,1)} %param.9) | copy-start | bytes 196612
  19.5 5.6 %collective-permute-start.9 = (bf16[256,256]{1,0:T(8,128)(2,1)S(1)}, bf16[256,256]{1,0:T(8,128)(2,1)S(1)}, u32[]{:S(2)}, u32[]{:S(2)}) collective-permute-start(bf16[256,256]{1,0:T(8,128)(2,1)S(1)} %add_convert_fusion.mine), channel_id=1, source_target_pairs={{0,2},{1,3},{2,0},{3,1},{4,6},{5,7},{6,4},{7,5},{8,10},{9,11},{10,... | collective-permute-start | bytes 393224 | tf_op jit(solution)/shard_map/sum_rows/ppermute | solution.py:27
  26.0 1.4 %collective-permute-start.10 = (bf16[384,256]{1,0:T(8,128)(2,1)S(1)}, bf16[384,256]{1,0:T(8,128)(2,1)S(1)}, u32[]{:S(2)}, u32[]{:S(2)}) collective-permute-start(bf16[384,256]{1,0:T(8,128)(2,1)S(1)} %get-tuple-element.40.refs_0_), channel_id=1, source_target_pairs={{0,1},{1,0},{2,3},{3,2},{4,5},{5,4},{6,7},{7,6},{8,9},{9,8},{10,11... | collective-permute-start | bytes 589832 | tf_op jit(solution)/shard_map/swap_cores/ppermute | solution.py:27
  27.5 6.4 %collective-permute-start.11 = (bf16[128,256]{1,0:T(8,128)(2,1)S(1)}, bf16[128,256]{1,0:T(8,128)(2,1)S(1)}, u32[]{:S(2)}, u32[]{:S(2)}) collective-permute-start(bf16[128,256]{1,0:T(8,128)(2,1)S(1)} %add_convert_fusion.7), channel_id=1, source_target_pairs={{0,17},{1,16},{2,19},{3,18},{4,21},{5,20},{6,23},{7,22},{8,25},{9,... | collective-permute-start | bytes 196616 | tf_op jit(solution)/shard_map/sum_weight/ppermute | solution.py:35
  30.6 6.4 %collective-permute-start.14 = (bf16[128,256]{1,0:T(8,128)(2,1)S(1)}, bf16[128,256]{1,0:T(8,128)(2,1)S(1)}, u32[]{:S(2)}, u32[]{:S(2)}) collective-permute-start(bf16[128,256]{1,0:T(8,128)(2,1)S(1)} %get-tuple-element.44), channel_id=1, source_target_pairs={{0,4},{4,0},{8,12},{12,8},{16,20},{20,16},{24,28},{28,24},{1,5},{5... | collective-permute-start | bytes 196616 | tf_op jit(solution)/shard_map/sum_columns/ppermute | solution.py:27
  31.3 5.6 %collective-permute-start.15 = (bf16[128,256]{1,0:T(8,128)(2,1)S(1)}, bf16[128,256]{1,0:T(8,128)(2,1)S(1)}, u32[]{:S(2)}, u32[]{:S(2)}) collective-permute-start(bf16[128,256]{1,0:T(8,128)(2,1)S(1)} %get-tuple-element.45), channel_id=1, source_target_pairs={{0,4},{4,0},{8,12},{12,8},{16,20},{20,16},{24,28},{28,24},{1,5},{5... | collective-permute-start | bytes 196616 | tf_op jit(solution)/shard_map/sum_columns/ppermute | solution.py:27
  32.7 6.7 %collective-permute-start.13 = (bf16[256,256]{1,0:T(8,128)(2,1)S(1)}, bf16[256,256]{1,0:T(8,128)(2,1)S(1)}, u32[]{:S(2)}, u32[]{:S(2)}) collective-permute-start(bf16[256,256]{1,0:T(8,128)(2,1)S(1)} %get-tuple-element.43), channel_id=1, source_target_pairs={{0,4},{4,0},{8,12},{12,8},{16,20},{20,16},{24,28},{28,24},{1,5},{5... | collective-permute-start | bytes 393224 | tf_op jit(solution)/shard_map/sum_columns/ppermute | solution.py:27
  33.9 5.4 %collective-permute-start.12 = (bf16[128,256]{1,0:T(8,128)(2,1)S(1)}, bf16[128,256]{1,0:T(8,128)(2,1)S(1)}, u32[]{:S(2)}, u32[]{:S(2)}) collective-permute-start(bf16[128,256]{1,0:T(8,128)(2,1)S(1)} %add_convert_fusion.6), channel_id=1, source_target_pairs={{0,9},{1,8},{2,11},{3,10},{4,13},{5,12},{6,15},{7,14},{8,1},{9,0},... | collective-permute-start | bytes 196616 | tf_op jit(solution)/shard_map/sum_columns/sum_weight/sum_weight/ppermute | solution.py:35
  37.0 8.4 %collective-permute-start.19 = (bf16[128,256]{1,0:T(8,128)(2,1)S(1)}, bf16[128,256]{1,0:T(8,128)(2,1)S(1)}, u32[]{:S(2)}, u32[]{:S(2)}) collective-permute-start(bf16[128,256]{1,0:T(8,128)(2,1)S(1)} %add_convert_fusion.2), channel_id=1, source_target_pairs={{0,24},{4,28},{8,16},{12,20},{16,8},{20,12},{24,0},{28,4},{1,25},{... | collective-permute-start | bytes 196616 | tf_op jit(solution)/shard_map/sum_columns/ppermute | solution.py:27
  38.2 7.2 %collective-permute-start.20 = (bf16[128,256]{1,0:T(8,128)(2,1)S(1)}, bf16[128,256]{1,0:T(8,128)(2,1)S(1)}, u32[]{:S(2)}, u32[]{:S(2)}) collective-permute-start(bf16[128,256]{1,0:T(8,128)(2,1)S(1)} %add_convert_fusion.1), channel_id=1, source_target_pairs={{0,16},{4,20},{8,24},{12,28},{16,0},{20,4},{24,8},{28,12},{1,17},{... | collective-permute-start | bytes 196616 | tf_op jit(solution)/shard_map/sum_columns/ppermute | solution.py:27
  39.4 4.4 %collective-permute-start.16 = (bf16[128,256]{1,0:T(8,128)(2,1)S(1)}, bf16[128,256]{1,0:T(8,128)(2,1)S(1)}, u32[]{:S(2)}, u32[]{:S(2)}) collective-permute-start(bf16[128,256]{1,0:T(8,128)(2,1)S(1)} %add_convert_fusion.5), channel_id=1, source_target_pairs={{0,5},{1,4},{2,7},{3,6},{4,1},{5,0},{6,3},{7,2},{8,13},{9,12},{10,... | collective-permute-start | bytes 196616 | tf_op jit(solution)/shard_map/sum_columns/sum_weight/sum_weight/ppermute | solution.py:35
  39.7 5.7 %collective-permute-start.18 = (bf16[128,256]{1,0:T(8,128)(2,1)S(1)}, bf16[128,256]{1,0:T(8,128)(2,1)S(1)}, u32[]{:S(2)}, u32[]{:S(2)}) collective-permute-start(bf16[128,256]{1,0:T(8,128)(2,1)S(1)} %add_convert_fusion.3), channel_id=1, source_target_pairs={{0,8},{4,12},{8,0},{12,4},{16,24},{20,28},{24,16},{28,20},{1,9},{5... | collective-permute-start | bytes 196616 | tf_op jit(solution)/shard_map/sum_columns/ppermute | solution.py:27
  43.8 1.6 %collective-permute-start.17 = (bf16[128,256]{1,0:T(8,128)(2,1)S(1)}, bf16[128,256]{1,0:T(8,128)(2,1)S(1)}, u32[]{:S(2)}, u32[]{:S(2)}) collective-permute-start(bf16[128,256]{1,0:T(8,128)(2,1)S(1)} %add_convert_fusion.4.mine), channel_id=1, source_target_pairs={{0,1},{1,0},{2,3},{3,2},{4,5},{5,4},{6,7},{7,6},{8,9},{9,8},{10,11... | collective-permute-start | bytes 196616 | tf_op jit(solution)/shard_map/sum_weight/ppermute | solution.py:27

commit v5 on v4

--- a/solution.py
+++ b/solution.py
@@ -89,24 +89,6 @@
             return 0
 
         lax.fori_loop(0, count, one, 0)
-
-
-def join_kernel(*refs):
-    *parts, out = refs
-    rows = parts[0].shape[0]
-    for n, part in enumerate(parts):
-        out[pl.ds(n * rows, rows), :] = part[...]
-
-
-def join(*parts):
-    shape = (len(parts) * parts[0].shape[0], parts[0].shape[1])
-    return pl.pallas_call(
-        join_kernel,
-        out_shape=jax.ShapeDtypeStruct(shape, parts[0].dtype),
-        in_specs=[VMEM] * len(parts),
-        out_specs=VMEM,
-        compiler_params=params(16 * 2**20),
-    )(*parts)
 
 
 def info_kernel(rows, cols, counts, info):

time: 46.4 us -> 46.4 us (level)
  no operation moved by 1% of the time
where the time goes in v5:
time: 46.4 us; the launch traced here: 46.2 us
  starting transfers between devices  23.7 us (51%)
  waiting for transfers between devices  17.4 us (37%)
  Pallas kernels  3.54 us (8%)
  between operations  1.43 us (3%)
    ppermute x18, starting transfers between devices, swap(): return lax.ppermute(value, axis, [(i, i ^ mask) for i in range(size)])  21.1 us
    ppermute x18, waiting for transfers between devices, swap(): return lax.ppermute(value, axis, [(i, i ^ mask) for i in range(size)])  14.8 us
    ppermute x3, waiting for transfers between devices, swap_crossed(): return lax.ppermute(value, ('gr', 'gc'), pairs)  2.63 us
    ppermute x3, starting transfers between devices, swap_crossed(): return lax.ppermute(value, ('gr', 'gc'), pairs)  2.54 us
    pallas_call x1, Pallas kernels, per_device(): pl.pallas_call(functools.partial(backward_kernel, [keep_masks, send_masks...  0.95 us
  transfers between devices with their start and end apart: 21, of which 11 were waited for; matrix products, arithmetic and copies ran while one was open for 0% of the time, Pallas kernels for 2%

profile of v5, /device:TPU:0, one launch (start us, length us, event | category | flops | bytes accessed | tf_op | source)
XLA Modules:
  0.0 46.2 jit_solution(8116711525099467411)
XLA Ops:
  0.6 3.1 %collective-permute-start = (bf16[128,256]{1,0:T(8,128)(2,1)}, bf16[128,256]{1,0:T(8,128)(2,1)S(1)}, u32[]{:S(2)}, u32[]{:S(2)}) collective-permute-start(bf16[128,256]{1,0:T(8,128)(2,1)} %bitcast.9), channel_id=1, source_target_pairs={{0,8},{4,12},{8,0},{12,4},{16,24},{20,28},{24,16},{28,20},{1,9},{5... | collective-permute-start | bytes 196616 | tf_op jit(solution)/shard_map/gather_features/ppermute | solution.py:27
  3.7 2.5 %collective-permute-start.3 = (bf16[128,256]{1,0:T(8,128)(2,1)}, bf16[128,256]{1,0:T(8,128)(2,1)S(1)}, u32[]{:S(2)}, u32[]{:S(2)}) collective-permute-start(bf16[128,256]{1,0:T(8,128)(2,1)} %bitcast.10), channel_id=1, source_target_pairs={{0,24},{4,28},{8,16},{12,20},{16,8},{20,12},{24,0},{28,4},{1,25},{... | collective-permute-start | bytes 196616 | tf_op jit(solution)/shard_map/gather_features/ppermute | solution.py:27
  6.2 0.1 collective-permute-start.2
  6.3 1.5 %collective-permute-start.1 = (bf16[128,256]{1,0:T(8,128)(2,1)}, bf16[128,256]{1,0:T(8,128)(2,1)S(1)}, u32[]{:S(2)}, u32[]{:S(2)}) collective-permute-start(bf16[128,256]{1,0:T(8,128)(2,1)} %bitcast.12), channel_id=1, source_target_pairs={{0,4},{4,0},{8,12},{12,8},{16,20},{20,16},{24,28},{28,24},{1,5},{5... | collective-permute-start | bytes 196616 | tf_op jit(solution)/shard_map/gather_features/ppermute | solution.py:27
  8.5 0.0 collective-permute-done.refs_2_
  8.5 0.0 copy-start.4
  8.5 0.0 copy-start.5
  8.5 0.0 copy-start
  8.5 0.0 copy-start.2
  8.5 1.6 %collective-permute-start.4 = (bf16[128,256]{1,0:T(8,128)(2,1)}, bf16[128,256]{1,0:T(8,128)(2,1)S(1)}, u32[]{:S(2)}, u32[]{:S(2)}) collective-permute-start(bf16[128,256]{1,0:T(8,128)(2,1)} %bitcast.14), channel_id=1, source_target_pairs={{0,2},{1,3},{2,0},{3,1},{4,6},{5,7},{6,4},{7,5},{8,10},{9,11},{10,... | collective-permute-start | bytes 196616 | tf_op jit(solution)/shard_map/gather_features/ppermute | solution.py:27
  10.1 0.5 %collective-permute-start.6 = (bf16[128,256]{1,0:T(8,128)(2,1)S(1)}, bf16[128,256]{1,0:T(8,128)(2,1)S(1)}, u32[]{:S(2)}, u32[]{:S(2)}) collective-permute-start(bf16[128,256]{1,0:T(8,128)(2,1)S(1)} %collective-permute-done.refs_2_), channel_id=1, source_target_pairs={{0,4},{4,0},{8,12},{12,8},{16,20},{20,16},{24,28},{28,24},{1,5},{5... | collective-permute-start | bytes 196616 | tf_op jit(solution)/shard_map/gather_features/ppermute | solution.py:27
  10.6 0.2 collective-permute-done.3.refs_3_
  10.8 1.5 %collective-permute-start.7 = (bf16[128,256]{1,0:T(8,128)(2,1)S(1)}, bf16[128,256]{1,0:T(8,128)(2,1)S(1)}, u32[]{:S(2)}, u32[]{:S(2)}) collective-permute-start(bf16[128,256]{1,0:T(8,128)(2,1)S(1)} %collective-permute-done.3.refs_3_), channel_id=1, source_target_pairs={{0,4},{4,0},{8,12},{12,8},{16,20},{20,16},{24,28},{28,24},{1,5},{5... | collective-permute-start | bytes 196616 | tf_op jit(solution)/shard_map/gather_features/ppermute | solution.py:27
  12.3 0.6 %collective-permute-done.2.refs_1_ = bf16[128,256]{1,0:T(8,128)(2,1)S(1)} collective-permute-done((bf16[128,256]{1,0:T(8,128)(2,1)}, bf16[128,256]{1,0:T(8,128)(2,1)S(1)}, u32[]{:S(2)}, u32[]{:S(2)}) %collective-permute-start.2) | collective-permute-done | bytes 65568 | tf_op jit(solution)/shard_map/gather_features/ppermute | solution.py:27
  12.9 1.5 %collective-permute-start.5 = (bf16[128,256]{1,0:T(8,128)(2,1)S(1)}, bf16[128,256]{1,0:T(8,128)(2,1)S(1)}, u32[]{:S(2)}, u32[]{:S(2)}) collective-permute-start(bf16[128,256]{1,0:T(8,128)(2,1)S(1)} %collective-permute-done.2.refs_1_), channel_id=1, source_target_pairs={{0,4},{4,0},{8,12},{12,8},{16,20},{20,16},{24,28},{28,24},{1,5},{5... | collective-permute-start | bytes 196616 | tf_op jit(solution)/shard_map/gather_features/ppermute | solution.py:27
  14.4 0.0 copy-done.4
  14.4 0.0 copy-done.5
  14.4 0.0 collective-permute-done.4.refs_1_
  14.4 0.0 collective-permute-done.1.refs_0_
  14.4 0.6 %collective-permute-done.7.refs_7_ = bf16[128,256]{1,0:T(8,128)(2,1)S(1)} collective-permute-done((bf16[128,256]{1,0:T(8,128)(2,1)S(1)}, bf16[128,256]{1,0:T(8,128)(2,1)S(1)}, u32[]{:S(2)}, u32[]{:S(2)}) %collective-permute-start.7) | collective-permute-done | bytes 65568 | tf_op jit(solution)/shard_map/gather_features/ppermute | solution.py:27
  15.1 2.1 %collective-permute-done.5.refs_5_ = bf16[128,256]{1,0:T(8,128)(2,1)S(1)} collective-permute-done((bf16[128,256]{1,0:T(8,128)(2,1)S(1)}, bf16[128,256]{1,0:T(8,128)(2,1)S(1)}, u32[]{:S(2)}, u32[]{:S(2)}) %collective-permute-start.5) | collective-permute-done | bytes 65568 | tf_op jit(solution)/shard_map/gather_features/ppermute | solution.py:27
  17.1 0.0 collective-permute-done.6.refs_6_
  17.1 0.0 copy-done
  17.1 0.0 copy-done.2
  17.1 0.9 %forward_blocks.1 = (bf16[256,256]{1,0:T(8,128)(2,1)S(1)}, bf16[256,256]{1,0:T(8,128)(2,1)S(1)}) custom-call(s32[8,128]{1,0:T(8,128)S(1)} %gather_features.1.info, bf16[6,128,128]{2,1,0:T(8,128)(2,1)S(1)} %bitcast.7, bf16[128,256]{1,0:T(8,128)(2,1)S(1)} %collective-permute-done.1.refs_0_, bf16[128,256]{1,0:T(8,128)(2,1)S(1)} %collective-permute-done.2.refs_1_, ...), custom_call_target="tpu_custom_call" | custom-call | tf_op jit(solution)/shard_map/forward_blocks/pallas_call | solution.py:201
  18.1 0.1 collective-permute-start.8
  18.2 1.3 %collective-permute-done.8 = bf16[256,256]{1,0:T(8,128)(2,1)S(1)} collective-permute-done((bf16[256,256]{1,0:T(8,128)(2,1)S(1)}, bf16[256,256]{1,0:T(8,128)(2,1)S(1)}, u32[]{:S(2)}, u32[]{:S(2)}) %collective-permute-start.8) | collective-permute-done | bytes 131104 | tf_op jit(solution)/shard_map/sum_rows/ppermute | solution.py:27
  19.5 0.0 copy-start.1
  19.5 0.0 copy-start.3
  19.5 1.6 %collective-permute-start.9 = (bf16[256,256]{1,0:T(8,128)(2,1)S(1)}, bf16[256,256]{1,0:T(8,128)(2,1)S(1)}, u32[]{:S(2)}, u32[]{:S(2)}) collective-permute-start(bf16[256,256]{1,0:T(8,128)(2,1)S(1)} %add_convert_fusion.mine), channel_id=1, source_target_pairs={{0,2},{1,3},{2,0},{3,1},{4,6},{5,7},{6,4},{7,5},{8,10},{9,11},{10,... | collective-permute-start | bytes 393224 | tf_op jit(solution)/shard_map/sum_rows/ppermute | solution.py:27
  21.1 4.1 %collective-permute-done.9.got = bf16[256,256]{1,0:T(8,128)(2,1)S(1)} collective-permute-done((bf16[256,256]{1,0:T(8,128)(2,1)S(1)}, bf16[256,256]{1,0:T(8,128)(2,1)S(1)}, u32[]{:S(2)}, u32[]{:S(2)}) %collective-permute-start.9) | collective-permute-done | bytes 131104 | tf_op jit(solution)/shard_map/sum_rows/ppermute | solution.py:27
  25.2 0.0 copy-done.1
  25.2 0.0 copy-done.3
  25.2 0.8 %dense.1 = (bf16[128,256]{1,0:T(8,128)(2,1)}, bf16[384,256]{1,0:T(8,128)(2,1)S(1)}, f32[128,256]{1,0:T(8,128)S(1)}) custom-call(bf16[256,256]{1,0:T(8,128)(2,1)S(1)} %add_convert_fusion.mine, bf16[256,256]{1,0:T(8,128)(2,1)S(1)} %collective-permute-done.9.got, bf16[256,256]{1,0:T(8,128)(2,1)S(1)} %copy-done.1, bf16[128,256]{1,0:T(8,128)(2,1)S(1)} %bitcast.15, ...), custom_call_target="tpu_custom_call" | custom-call | tf_op jit(solution)/shard_map/dense/pallas_call | solution.py:225
  26.0 0.0 collective-permute-start.10
  26.0 1.4 %collective-permute-done.10.refs_1_ = bf16[384,256]{1,0:T(8,128)(2,1)S(1)} collective-permute-done((bf16[384,256]{1,0:T(8,128)(2,1)S(1)}, bf16[384,256]{1,0:T(8,128)(2,1)S(1)}, u32[]{:S(2)}, u32[]{:S(2)}) %collective-permute-start.10) | collective-permute-done | bytes 196640 | tf_op jit(solution)/shard_map/swap_cores/ppermute | solution.py:27
  27.5 2.1 %collective-permute-start.11 = (bf16[128,256]{1,0:T(8,128)(2,1)S(1)}, bf16[128,256]{1,0:T(8,128)(2,1)S(1)}, u32[]{:S(2)}, u32[]{:S(2)}) collective-permute-start(bf16[128,256]{1,0:T(8,128)(2,1)S(1)} %add_convert_fusion.7), channel_id=1, source_target_pairs={{0,17},{1,16},{2,19},{3,18},{4,21},{5,20},{6,23},{7,22},{8,25},{9,... | collective-permute-start | bytes 196616 | tf_op jit(solution)/shard_map/sum_weight/ppermute | solution.py:35
  29.6 1.0 %backward_blocks.1 = (bf16[128,256]{1,0:T(8,128)(2,1)S(1)}, bf16[128,256]{1,0:T(8,128)(2,1)S(1)}, bf16[256,256]{1,0:T(8,128)(2,1)S(1)}, bf16[128,256]{1,0:T(8,12...) custom-call(s32[8,128]{1,0:T(8,128)S(1)} %gather_features.1.info, ...), custom_call_target="tpu_custom_call" | custom-call | tf_op jit(solution)/shard_map/backward_blocks/pallas_call | solution.py:265
  30.6 0.8 %collective-permute-start.14 = (bf16[128,256]{1,0:T(8,128)(2,1)S(1)}, bf16[128,256]{1,0:T(8,128)(2,1)S(1)}, u32[]{:S(2)}, u32[]{:S(2)}) collective-permute-start(bf16[128,256]{1,0:T(8,128)(2,1)S(1)} %get-tuple-element.44), channel_id=1, source_target_pairs={{0,4},{4,0},{8,12},{12,8},{16,20},{20,16},{24,28},{28,24},{1,5},{5... | collective-permute-start | bytes 196616 | tf_op jit(solution)/shard_map/sum_columns/ppermute | solution.py:27
  31.3 1.3 %collective-permute-start.15 = (bf16[128,256]{1,0:T(8,128)(2,1)S(1)}, bf16[128,256]{1,0:T(8,128)(2,1)S(1)}, u32[]{:S(2)}, u32[]{:S(2)}) collective-permute-start(bf16[128,256]{1,0:T(8,128)(2,1)S(1)} %get-tuple-element.45), channel_id=1, source_target_pairs={{0,4},{4,0},{8,12},{12,8},{16,20},{20,16},{24,28},{28,24},{1,5},{5... | collective-permute-start | bytes 196616 | tf_op jit(solution)/shard_map/sum_columns/ppermute | solution.py:27
  32.7 0.7 %collective-permute-start.13 = (bf16[256,256]{1,0:T(8,128)(2,1)S(1)}, bf16[256,256]{1,0:T(8,128)(2,1)S(1)}, u32[]{:S(2)}, u32[]{:S(2)}) collective-permute-start(bf16[256,256]{1,0:T(8,128)(2,1)S(1)} %get-tuple-element.43), channel_id=1, source_target_pairs={{0,4},{4,0},{8,12},{12,8},{16,20},{20,16},{24,28},{28,24},{1,5},{5... | collective-permute-start | bytes 393224 | tf_op jit(solution)/shard_map/sum_columns/ppermute | solution.py:27
  33.4 0.5 %collective-permute-done.11 = bf16[128,256]{1,0:T(8,128)(2,1)S(1)} collective-permute-done((bf16[128,256]{1,0:T(8,128)(2,1)S(1)}, bf16[128,256]{1,0:T(8,128)(2,1)S(1)}, u32[]{:S(2)}, u32[]{:S(2)}) %collective-permute-start.11) | collective-permute-done | bytes 65568 | tf_op jit(solution)/shard_map/sum_weight/ppermute | solution.py:35
  33.9 0.1 collective-permute-start.12
  34.0 2.9 %collective-permute-done.15 = bf16[128,256]{1,0:T(8,128)(2,1)S(1)} collective-permute-done((bf16[128,256]{1,0:T(8,128)(2,1)S(1)}, bf16[128,256]{1,0:T(8,128)(2,1)S(1)}, u32[]{:S(2)}, u32[]{:S(2)}) %collective-permute-start.15) | collective-permute-done | bytes 65568 | tf_op jit(solution)/shard_map/sum_columns/ppermute | solution.py:27
  37.0 0.0 collective-permute-done.14
  37.0 1.1 %collective-permute-start.19 = (bf16[128,256]{1,0:T(8,128)(2,1)S(1)}, bf16[128,256]{1,0:T(8,128)(2,1)S(1)}, u32[]{:S(2)}, u32[]{:S(2)}) collective-permute-start(bf16[128,256]{1,0:T(8,128)(2,1)S(1)} %add_convert_fusion.2), channel_id=1, source_target_pairs={{0,24},{4,28},{8,16},{12,20},{16,8},{20,12},{24,0},{28,4},{1,25},{... | collective-permute-start | bytes 196616 | tf_op jit(solution)/shard_map/sum_columns/ppermute | solution.py:27
  38.2 1.2 %collective-permute-start.20 = (bf16[128,256]{1,0:T(8,128)(2,1)S(1)}, bf16[128,256]{1,0:T(8,128)(2,1)S(1)}, u32[]{:S(2)}, u32[]{:S(2)}) collective-permute-start(bf16[128,256]{1,0:T(8,128)(2,1)S(1)} %add_convert_fusion.1), channel_id=1, source_target_pairs={{0,16},{4,20},{8,24},{12,28},{16,0},{20,4},{24,8},{28,12},{1,17},{... | collective-permute-start | bytes 196616 | tf_op jit(solution)/shard_map/sum_columns/ppermute | solution.py:27
  39.3 0.0 collective-permute-done.13.refs_1_
  39.3 0.0 collective-permute-done.12
  39.4 0.3 collective-permute-start.16
  39.7 2.0 %collective-permute-start.18 = (bf16[128,256]{1,0:T(8,128)(2,1)S(1)}, bf16[128,256]{1,0:T(8,128)(2,1)S(1)}, u32[]{:S(2)}, u32[]{:S(2)}) collective-permute-start(bf16[128,256]{1,0:T(8,128)(2,1)S(1)} %add_convert_fusion.3), channel_id=1, source_target_pairs={{0,8},{4,12},{8,0},{12,4},{16,24},{20,28},{24,16},{28,20},{1,9},{5... | collective-permute-start | bytes 196616 | tf_op jit(solution)/shard_map/sum_columns/ppermute | solution.py:27
  41.7 2.1 %collective-permute-done.16 = bf16[128,256]{1,0:T(8,128)(2,1)S(1)} collective-permute-done((bf16[128,256]{1,0:T(8,128)(2,1)S(1)}, bf16[128,256]{1,0:T(8,128)(2,1)S(1)}, u32[]{:S(2)}, u32[]{:S(2)}) %collective-permute-start.16) | collective-permute-done | bytes 65568 | tf_op jit(solution)/shard_map/sum_columns/sum_weight/sum_weight/ppermute | solution.py:35
  43.8 0.1 collective-permute-start.17
  43.9 1.5 %collective-permute-done.20.refs_2_ = bf16[128,256]{1,0:T(8,128)(2,1)S(1)} collective-permute-done((bf16[128,256]{1,0:T(8,128)(2,1)S(1)}, bf16[128,256]{1,0:T(8,128)(2,1)S(1)}, u32[]{:S(2)}, u32[]{:S(2)}) %collective-permute-start.20) | collective-permute-done | bytes 65568 | tf_op jit(solution)/shard_map/sum_columns/ppermute | solution.py:27
  45.4 0.0 collective-permute-done.19.refs_3_
  45.4 0.0 collective-permute-done.18.refs_4_
  45.4 0.0 collective-permute-done.17.other
  45.4 0.8 %shard_map.94 = (f32[128,256]{1,0:T(8,128)}, f32[256,256]{1,0:T(8,128)}) custom-call(bf16[128,256]{1,0:T(8,128)(2,1)S(1)} %add_convert_fusion.4.mine, bf16[128,256]{1,0:T(8,128)(2,1)S(1)} %collective-permute-done.17.other, bf16[256,256]{1,0:T(8,128)(2,1)S(1)} %get-tuple-element.51.refs_0_, bf16[256,256]{1,0:T(8,128)(2,1)S(1)} %collective-permute-done.13.refs_1_, ...), custom_call_target="tpu_custom_call" | custom-call | tf_op jit(solution)/shard_map/pallas_call | solution.py:296
  (9 shorter events, 0.2 us)
Async XLA Ops:
  0.6 7.9 %collective-permute-start = (bf16[128,256]{1,0:T(8,128)(2,1)}, bf16[128,256]{1,0:T(8,128)(2,1)S(1)}, u32[]{:S(2)}, u32[]{:S(2)}) collective-permute-start(bf16[128,256]{1,0:T(8,128)(2,1)} %bitcast.9), channel_id=1, source_target_pairs={{0,8},{4,12},{8,0},{12,4},{16,24},{20,28},{24,16},{28,20},{1,9},{5... | collective-permute-start | bytes 196616 | tf_op jit(solution)/shard_map/gather_features/ppermute | solution.py:27
  3.7 7.1 %collective-permute-start.3 = (bf16[128,256]{1,0:T(8,128)(2,1)}, bf16[128,256]{1,0:T(8,128)(2,1)S(1)}, u32[]{:S(2)}, u32[]{:S(2)}) collective-permute-start(bf16[128,256]{1,0:T(8,128)(2,1)} %bitcast.10), channel_id=1, source_target_pairs={{0,24},{4,28},{8,16},{12,20},{16,8},{20,12},{24,0},{28,4},{1,25},{... | collective-permute-start | bytes 196616 | tf_op jit(solution)/shard_map/gather_features/ppermute | solution.py:27
  6.2 6.7 %collective-permute-start.2 = (bf16[128,256]{1,0:T(8,128)(2,1)}, bf16[128,256]{1,0:T(8,128)(2,1)S(1)}, u32[]{:S(2)}, u32[]{:S(2)}) collective-permute-start(bf16[128,256]{1,0:T(8,128)(2,1)} %bitcast.11), channel_id=1, source_target_pairs={{0,16},{4,20},{8,24},{12,28},{16,0},{20,4},{24,8},{28,12},{1,17},{... | collective-permute-start | bytes 196616 | tf_op jit(solution)/shard_map/gather_features/ppermute | solution.py:27
  6.3 8.1 %collective-permute-start.1 = (bf16[128,256]{1,0:T(8,128)(2,1)}, bf16[128,256]{1,0:T(8,128)(2,1)S(1)}, u32[]{:S(2)}, u32[]{:S(2)}) collective-permute-start(bf16[128,256]{1,0:T(8,128)(2,1)} %bitcast.12), channel_id=1, source_target_pairs={{0,4},{4,0},{8,12},{12,8},{16,20},{20,16},{24,28},{28,24},{1,5},{5... | collective-permute-start | bytes 196616 | tf_op jit(solution)/shard_map/gather_features/ppermute | solution.py:27
  8.5 5.9 %copy-start.4 = (s32[1,1,6]{2,1,0:T(1,128)S(1)}, s32[1,1,6]{2,1,0:T(1,128)}, u32[]{:S(2)}) copy-start(s32[1,1,6]{2,1,0:T(1,128)} %param.10) | copy-start | bytes 76
  8.5 5.9 %copy-start.5 = (s32[1,1,6]{2,1,0:T(1,128)S(1)}, s32[1,1,6]{2,1,0:T(1,128)}, u32[]{:S(2)}) copy-start(s32[1,1,6]{2,1,0:T(1,128)} %param.11) | copy-start | bytes 76
  8.5 8.6 %copy-start = (bf16[1,1,6,128,128]{4,3,2,1,0:T(8,128)(2,1)S(1)}, bf16[1,1,6,128,128]{4,3,2,1,0:T(8,128)(2,1)}, u32[]{:S(2)}) copy-start(bf16[1,1,6,128,128]{4,3,2,1,0:T(8,128)(2,1)} %param.13) | copy-start | bytes 589828
  8.5 8.6 %copy-start.2 = (bf16[1,128,256]{2,1,0:T(8,128)(2,1)S(1)}, bf16[1,128,256]{2,1,0:T(8,128)(2,1)}, u32[]{:S(2)}) copy-start(bf16[1,128,256]{2,1,0:T(8,128)(2,1)} %param.7) | copy-start | bytes 196612
  8.5 5.9 %collective-permute-start.4 = (bf16[128,256]{1,0:T(8,128)(2,1)}, bf16[128,256]{1,0:T(8,128)(2,1)S(1)}, u32[]{:S(2)}, u32[]{:S(2)}) collective-permute-start(bf16[128,256]{1,0:T(8,128)(2,1)} %bitcast.14), channel_id=1, source_target_pairs={{0,2},{1,3},{2,0},{3,1},{4,6},{5,7},{6,4},{7,5},{8,10},{9,11},{10,... | collective-permute-start | bytes 196616 | tf_op jit(solution)/shard_map/gather_features/ppermute | solution.py:27
  10.1 7.0 %collective-permute-start.6 = (bf16[128,256]{1,0:T(8,128)(2,1)S(1)}, bf16[128,256]{1,0:T(8,128)(2,1)S(1)}, u32[]{:S(2)}, u32[]{:S(2)}) collective-permute-start(bf16[128,256]{1,0:T(8,128)(2,1)S(1)} %collective-permute-done.refs_2_), channel_id=1, source_target_pairs={{0,4},{4,0},{8,12},{12,8},{16,20},{20,16},{24,28},{28,24},{1,5},{5... | collective-permute-start | bytes 196616 | tf_op jit(solution)/shard_map/gather_features/ppermute | solution.py:27
  10.8 4.3 %collective-permute-start.7 = (bf16[128,256]{1,0:T(8,128)(2,1)S(1)}, bf16[128,256]{1,0:T(8,128)(2,1)S(1)}, u32[]{:S(2)}, u32[]{:S(2)}) collective-permute-start(bf16[128,256]{1,0:T(8,128)(2,1)S(1)} %collective-permute-done.3.refs_3_), channel_id=1, source_target_pairs={{0,4},{4,0},{8,12},{12,8},{16,20},{20,16},{24,28},{28,24},{1,5},{5... | collective-permute-start | bytes 196616 | tf_op jit(solution)/shard_map/gather_features/ppermute | solution.py:27
  12.9 4.3 %collective-permute-start.5 = (bf16[128,256]{1,0:T(8,128)(2,1)S(1)}, bf16[128,256]{1,0:T(8,128)(2,1)S(1)}, u32[]{:S(2)}, u32[]{:S(2)}) collective-permute-start(bf16[128,256]{1,0:T(8,128)(2,1)S(1)} %collective-permute-done.2.refs_1_), channel_id=1, source_target_pairs={{0,4},{4,0},{8,12},{12,8},{16,20},{20,16},{24,28},{28,24},{1,5},{5... | collective-permute-start | bytes 196616 | tf_op jit(solution)/shard_map/gather_features/ppermute | solution.py:27
  18.1 1.4 %collective-permute-start.8 = (bf16[256,256]{1,0:T(8,128)(2,1)S(1)}, bf16[256,256]{1,0:T(8,128)(2,1)S(1)}, u32[]{:S(2)}, u32[]{:S(2)}) collective-permute-start(bf16[256,256]{1,0:T(8,128)(2,1)S(1)} %get-tuple-element.37), channel_id=1, source_target_pairs={{0,1},{1,0},{2,3},{3,2},{4,5},{5,4},{6,7},{7,6},{8,9},{9,8},{10,11... | collective-permute-start | bytes 393224 | tf_op jit(solution)/shard_map/sum_rows/ppermute | solution.py:27
  19.5 5.7 %copy-start.1 = (bf16[256,256]{1,0:T(8,128)(2,1)S(1)}, bf16[256,256]{1,0:T(8,128)(2,1)}, u32[]{:S(2)}) copy-start(bf16[256,256]{1,0:T(8,128)(2,1)} %weight.1) | copy-start | bytes 393220
  19.5 5.7 %copy-start.3 = (bf16[1,128,256]{2,1,0:T(8,128)(2,1)S(1)}, bf16[1,128,256]{2,1,0:T(8,128)(2,1)}, u32[]{:S(2)}) copy-start(bf16[1,128,256]{2,1,0:T(8,128)(2,1)} %param.9) | copy-start | bytes 196612
  19.5 5.6 %collective-permute-start.9 = (bf16[256,256]{1,0:T(8,128)(2,1)S(1)}, bf16[256,256]{1,0:T(8,128)(2,1)S(1)}, u32[]{:S(2)}, u32[]{:S(2)}) collective-permute-start(bf16[256,256]{1,0:T(8,128)(2,1)S(1)} %add_convert_fusion.mine), channel_id=1, source_target_pairs={{0,2},{1,3},{2,0},{3,1},{4,6},{5,7},{6,4},{7,5},{8,10},{9,11},{10,... | collective-permute-start | bytes 393224 | tf_op jit(solution)/shard_map/sum_rows/ppermute | solution.py:27
  26.0 1.4 %collective-permute-start.10 = (bf16[384,256]{1,0:T(8,128)(2,1)S(1)}, bf16[384,256]{1,0:T(8,128)(2,1)S(1)}, u32[]{:S(2)}, u32[]{:S(2)}) collective-permute-start(bf16[384,256]{1,0:T(8,128)(2,1)S(1)} %get-tuple-element.40.refs_0_), channel_id=1, source_target_pairs={{0,1},{1,0},{2,3},{3,2},{4,5},{5,4},{6,7},{7,6},{8,9},{9,8},{10,11... | collective-permute-start | bytes 589832 | tf_op jit(solution)/shard_map/swap_cores/ppermute | solution.py:27
  27.5 6.4 %collective-permute-start.11 = (bf16[128,256]{1,0:T(8,128)(2,1)S(1)}, bf16[128,256]{1,0:T(8,128)(2,1)S(1)}, u32[]{:S(2)}, u32[]{:S(2)}) collective-permute-start(bf16[128,256]{1,0:T(8,128)(2,1)S(1)} %add_convert_fusion.7), channel_id=1, source_target_pairs={{0,17},{1,16},{2,19},{3,18},{4,21},{5,20},{6,23},{7,22},{8,25},{9,... | collective-permute-start | bytes 196616 | tf_op jit(solution)/shard_map/sum_weight/ppermute | solution.py:35
  30.6 6.4 %collective-permute-start.14 = (bf16[128,256]{1,0:T(8,128)(2,1)S(1)}, bf16[128,256]{1,0:T(8,128)(2,1)S(1)}, u32[]{:S(2)}, u32[]{:S(2)}) collective-permute-start(bf16[128,256]{1,0:T(8,128)(2,1)S(1)} %get-tuple-element.44), channel_id=1, source_target_pairs={{0,4},{4,0},{8,12},{12,8},{16,20},{20,16},{24,28},{28,24},{1,5},{5... | collective-permute-start | bytes 196616 | tf_op jit(solution)/shard_map/sum_columns/ppermute | solution.py:27
  31.3 5.6 %collective-permute-start.15 = (bf16[128,256]{1,0:T(8,128)(2,1)S(1)}, bf16[128,256]{1,0:T(8,128)(2,1)S(1)}, u32[]{:S(2)}, u32[]{:S(2)}) collective-permute-start(bf16[128,256]{1,0:T(8,128)(2,1)S(1)} %get-tuple-element.45), channel_id=1, source_target_pairs={{0,4},{4,0},{8,12},{12,8},{16,20},{20,16},{24,28},{28,24},{1,5},{5... | collective-permute-start | bytes 196616 | tf_op jit(solution)/shard_map/sum_columns/ppermute | solution.py:27
  32.7 6.7 %collective-permute-start.13 = (bf16[256,256]{1,0:T(8,128)(2,1)S(1)}, bf16[256,256]{1,0:T(8,128)(2,1)S(1)}, u32[]{:S(2)}, u32[]{:S(2)}) collective-permute-start(bf16[256,256]{1,0:T(8,128)(2,1)S(1)} %get-tuple-element.43), channel_id=1, source_target_pairs={{0,4},{4,0},{8,12},{12,8},{16,20},{20,16},{24,28},{28,24},{1,5},{5... | collective-permute-start | bytes 393224 | tf_op jit(solution)/shard_map/sum_columns/ppermute | solution.py:27
  33.9 5.4 %collective-permute-start.12 = (bf16[128,256]{1,0:T(8,128)(2,1)S(1)}, bf16[128,256]{1,0:T(8,128)(2,1)S(1)}, u32[]{:S(2)}, u32[]{:S(2)}) collective-permute-start(bf16[128,256]{1,0:T(8,128)(2,1)S(1)} %add_convert_fusion.6), channel_id=1, source_target_pairs={{0,9},{1,8},{2,11},{3,10},{4,13},{5,12},{6,15},{7,14},{8,1},{9,0},... | collective-permute-start | bytes 196616 | tf_op jit(solution)/shard_map/sum_columns/sum_weight/sum_weight/ppermute | solution.py:35
  37.0 8.4 %collective-permute-start.19 = (bf16[128,256]{1,0:T(8,128)(2,1)S(1)}, bf16[128,256]{1,0:T(8,128)(2,1)S(1)}, u32[]{:S(2)}, u32[]{:S(2)}) collective-permute-start(bf16[128,256]{1,0:T(8,128)(2,1)S(1)} %add_convert_fusion.2), channel_id=1, source_target_pairs={{0,24},{4,28},{8,16},{12,20},{16,8},{20,12},{24,0},{28,4},{1,25},{... | collective-permute-start | bytes 196616 | tf_op jit(solution)/shard_map/sum_columns/ppermute | solution.py:27
  38.2 7.2 %collective-permute-start.20 = (bf16[128,256]{1,0:T(8,128)(2,1)S(1)}, bf16[128,256]{1,0:T(8,128)(2,1)S(1)}, u32[]{:S(2)}, u32[]{:S(2)}) collective-permute-start(bf16[128,256]{1,0:T(8,128)(2,1)S(1)} %add_convert_fusion.1), channel_id=1, source_target_pairs={{0,16},{4,20},{8,24},{12,28},{16,0},{20,4},{24,8},{28,12},{1,17},{... | collective-permute-start | bytes 196616 | tf_op jit(solution)/shard_map/sum_columns/ppermute | solution.py:27
  39.4 4.4 %collective-permute-start.16 = (bf16[128,256]{1,0:T(8,128)(2,1)S(1)}, bf16[128,256]{1,0:T(8,128)(2,1)S(1)}, u32[]{:S(2)}, u32[]{:S(2)}) collective-permute-start(bf16[128,256]{1,0:T(8,128)(2,1)S(1)} %add_convert_fusion.5), channel_id=1, source_target_pairs={{0,5},{1,4},{2,7},{3,6},{4,1},{5,0},{6,3},{7,2},{8,13},{9,12},{10,... | collective-permute-start | bytes 196616 | tf_op jit(solution)/shard_map/sum_columns/sum_weight/sum_weight/ppermute | solution.py:35
  39.7 5.7 %collective-permute-start.18 = (bf16[128,256]{1,0:T(8,128)(2,1)S(1)}, bf16[128,256]{1,0:T(8,128)(2,1)S(1)}, u32[]{:S(2)}, u32[]{:S(2)}) collective-permute-start(bf16[128,256]{1,0:T(8,128)(2,1)S(1)} %add_convert_fusion.3), channel_id=1, source_target_pairs={{0,8},{4,12},{8,0},{12,4},{16,24},{20,28},{24,16},{28,20},{1,9},{5... | collective-permute-start | bytes 196616 | tf_op jit(solution)/shard_map/sum_columns/ppermute | solution.py:27
  43.8 1.6 %collective-permute-start.17 = (bf16[128,256]{1,0:T(8,128)(2,1)S(1)}, bf16[128,256]{1,0:T(8,128)(2,1)S(1)}, u32[]{:S(2)}, u32[]{:S(2)}) collective-permute-start(bf16[128,256]{1,0:T(8,128)(2,1)S(1)} %add_convert_fusion.4.mine), channel_id=1, source_target_pairs={{0,1},{1,0},{2,3},{3,2},{4,5},{5,4},{6,7},{7,6},{8,9},{9,8},{10,11... | collective-permute-start | bytes 196616 | tf_op jit(solution)/shard_map/sum_weight/ppermute | solution.py:27

commit v6 on v5

--- a/solution.py
+++ b/solution.py
@@ -126,7 +126,7 @@
 
 
 def dense_kernel(bit, mine, got, weight, *refs):
-    *grads, activated, message, kept, total = refs
+    *grads, activated, message, passed, kept, total = refs
     side, half = activated.shape[0], kept.shape[0]
     blocks = mine.shape[0] // side
     w = weight[...]
@@ -146,7 +146,7 @@
     total[...] = lax.dot_general(hidden, grad_pre, LEFT_T, preferred_element_type=jnp.float32)
     place = weight_half()
     kept[...] = total[pl.ds(pl.multiple_of(place * half, half), half), :]
-    message[pl.ds(blocks * side, half), :] = bf16(
+    passed[...] = bf16(
         total[pl.ds(pl.multiple_of((1 - place) * half, half), half), :]
     )
 
@@ -222,22 +222,24 @@
 
     half = width // 2
     with jax.named_scope("dense"):
-        activated, message, kept = pl.pallas_call(
+        activated, message, passed, kept = pl.pallas_call(
             functools.partial(dense_kernel, last >> 1),
             out_shape=[
                 block,
-                jax.ShapeDtypeStruct((mine.shape[0] + half, width), jnp.bfloat16),
+                jax.ShapeDtypeStruct(mine.shape, jnp.bfloat16),
+                jax.ShapeDtypeStruct((half, width), jnp.bfloat16),
                 jax.ShapeDtypeStruct((half, width), jnp.float32),
             ],
             in_specs=[VMEM] * (3 + len(grads)),
-            out_specs=[VMEM] * 3,
+            out_specs=[VMEM] * 4,
             scratch_shapes=[pltpu.VMEM((width, width), jnp.float32)],
             compiler_params=params(limit),
         )(mine, got, weight, *[grads[m] for m in keep_masks])
 
     with jax.named_scope("swap_cores"):
         answer = swap(message, "gc", 1)
-        running = kept + f32(answer[mine.shape[0]:])
+        passed = swap(passed, "gc", 1)
+        running = kept + f32(after(passed, answer))
     stages = bits_of("gr")[:0:-1] + [1]
     sent, got, order = [], [], Line()
 

time: 46.4 us -> 46.3 us (level)
  waiting for transfers between devices: 17.4 us -> 16.5 us
  starting transfers between devices: 23.7 us -> 24.5 us
    ppermute x18 -> x19, starting transfers between devices: 21.1 us -> 21.8 us  [swap(): return lax.ppermute(value, axis, [(i, i ^ mask) for i in range(size)])]
    ppermute x18 -> x19, waiting for transfers between devices: 14.8 us -> 14.2 us  [swap(): return lax.ppermute(value, axis, [(i, i ^ mask) for i in range(size)])]
  transfers between devices with their start and end apart: 21 -> 22, of which waited for: 11 -> 12; matrix products, arithmetic and copies ran while one was open for 0% -> 0% of each run, Pallas kernels for 2% -> 2%
where the time goes in v6:
time: 46.3 us; the launch traced here: 46.2 us
  starting transfers between devices  24.5 us (53%)
  waiting for transfers between devices  16.5 us (36%)
  Pallas kernels  3.58 us (8%)
  between operations  1.43 us (3%)
    ppermute x19, starting transfers between devices, swap(): return lax.ppermute(value, axis, [(i, i ^ mask) for i in range(size)])  21.8 us
    ppermute x19, waiting for transfers between devices, swap(): return lax.ppermute(value, axis, [(i, i ^ mask) for i in range(size)])  14.2 us
    ppermute x3, starting transfers between devices, swap_crossed(): return lax.ppermute(value, ('gr', 'gc'), pairs)  2.64 us
    ppermute x3, waiting for transfers between devices, swap_crossed(): return lax.ppermute(value, ('gr', 'gc'), pairs)  2.35 us
    pallas_call x1, Pallas kernels, per_device(): pl.pallas_call(functools.partial(backward_kernel, [keep_masks, send_masks...  0.95 us
    pallas_call x1, Pallas kernels, per_device(): pl.pallas_call(functools.partial(forward_kernel, layout, send_masks, keep...  0.93 us
  transfers between devices with their start and end apart: 22, of which 12 were waited for; matrix products, arithmetic and copies ran while one was open for 0% of the time, Pallas kernels for 2%

profile of v6, /device:TPU:0, one launch (start us, length us, event | category | flops | bytes accessed | tf_op | source)
XLA Modules:
  0.0 46.2 jit_solution(2539105042564108986)
XLA Ops:
  0.6 3.1 %collective-permute-start = (bf16[128,256]{1,0:T(8,128)(2,1)}, bf16[128,256]{1,0:T(8,128)(2,1)S(1)}, u32[]{:S(2)}, u32[]{:S(2)}) collective-permute-start(bf16[128,256]{1,0:T(8,128)(2,1)} %bitcast.9), channel_id=1, source_target_pairs={{0,8},{4,12},{8,0},{12,4},{16,24},{20,28},{24,16},{28,20},{1,9},{5... | collective-permute-start | bytes 196616 | tf_op jit(solution)/shard_map/gather_features/ppermute | solution.py:27
  3.7 2.5 %collective-permute-start.3 = (bf16[128,256]{1,0:T(8,128)(2,1)}, bf16[128,256]{1,0:T(8,128)(2,1)S(1)}, u32[]{:S(2)}, u32[]{:S(2)}) collective-permute-start(bf16[128,256]{1,0:T(8,128)(2,1)} %bitcast.10), channel_id=1, source_target_pairs={{0,24},{4,28},{8,16},{12,20},{16,8},{20,12},{24,0},{28,4},{1,25},{... | collective-permute-start | bytes 196616 | tf_op jit(solution)/shard_map/gather_features/ppermute | solution.py:27
  6.2 0.1 collective-permute-start.2
  6.3 1.5 %collective-permute-start.1 = (bf16[128,256]{1,0:T(8,128)(2,1)}, bf16[128,256]{1,0:T(8,128)(2,1)S(1)}, u32[]{:S(2)}, u32[]{:S(2)}) collective-permute-start(bf16[128,256]{1,0:T(8,128)(2,1)} %bitcast.12), channel_id=1, source_target_pairs={{0,4},{4,0},{8,12},{12,8},{16,20},{20,16},{24,28},{28,24},{1,5},{5... | collective-permute-start | bytes 196616 | tf_op jit(solution)/shard_map/gather_features/ppermute | solution.py:27
  8.5 0.0 collective-permute-done.refs_2_
  8.5 0.0 copy-start.4
  8.5 0.0 copy-start.5
  8.5 0.0 copy-start
  8.5 0.0 copy-start.2
  8.5 1.6 %collective-permute-start.4 = (bf16[128,256]{1,0:T(8,128)(2,1)}, bf16[128,256]{1,0:T(8,128)(2,1)S(1)}, u32[]{:S(2)}, u32[]{:S(2)}) collective-permute-start(bf16[128,256]{1,0:T(8,128)(2,1)} %bitcast.14), channel_id=1, source_target_pairs={{0,2},{1,3},{2,0},{3,1},{4,6},{5,7},{6,4},{7,5},{8,10},{9,11},{10,... | collective-permute-start | bytes 196616 | tf_op jit(solution)/shard_map/gather_features/ppermute | solution.py:27
  10.1 0.5 %collective-permute-start.6 = (bf16[128,256]{1,0:T(8,128)(2,1)S(1)}, bf16[128,256]{1,0:T(8,128)(2,1)S(1)}, u32[]{:S(2)}, u32[]{:S(2)}) collective-permute-start(bf16[128,256]{1,0:T(8,128)(2,1)S(1)} %collective-permute-done.refs_2_), channel_id=1, source_target_pairs={{0,4},{4,0},{8,12},{12,8},{16,20},{20,16},{24,28},{28,24},{1,5},{5... | collective-permute-start | bytes 196616 | tf_op jit(solution)/shard_map/gather_features/ppermute | solution.py:27
  10.6 0.2 collective-permute-done.3.refs_3_
  10.8 1.5 %collective-permute-start.7 = (bf16[128,256]{1,0:T(8,128)(2,1)S(1)}, bf16[128,256]{1,0:T(8,128)(2,1)S(1)}, u32[]{:S(2)}, u32[]{:S(2)}) collective-permute-start(bf16[128,256]{1,0:T(8,128)(2,1)S(1)} %collective-permute-done.3.refs_3_), channel_id=1, source_target_pairs={{0,4},{4,0},{8,12},{12,8},{16,20},{20,16},{24,28},{28,24},{1,5},{5... | collective-permute-start | bytes 196616 | tf_op jit(solution)/shard_map/gather_features/ppermute | solution.py:27
  12.3 0.6 %collective-permute-done.2.refs_1_ = bf16[128,256]{1,0:T(8,128)(2,1)S(1)} collective-permute-done((bf16[128,256]{1,0:T(8,128)(2,1)}, bf16[128,256]{1,0:T(8,128)(2,1)S(1)}, u32[]{:S(2)}, u32[]{:S(2)}) %collective-permute-start.2) | collective-permute-done | bytes 65568 | tf_op jit(solution)/shard_map/gather_features/ppermute | solution.py:27
  12.9 1.5 %collective-permute-start.5 = (bf16[128,256]{1,0:T(8,128)(2,1)S(1)}, bf16[128,256]{1,0:T(8,128)(2,1)S(1)}, u32[]{:S(2)}, u32[]{:S(2)}) collective-permute-start(bf16[128,256]{1,0:T(8,128)(2,1)S(1)} %collective-permute-done.2.refs_1_), channel_id=1, source_target_pairs={{0,4},{4,0},{8,12},{12,8},{16,20},{20,16},{24,28},{28,24},{1,5},{5... | collective-permute-start | bytes 196616 | tf_op jit(solution)/shard_map/gather_features/ppermute | solution.py:27
  14.4 0.0 copy-done.4
  14.4 0.0 copy-done.5
  14.4 0.0 collective-permute-done.4.refs_1_
  14.4 0.0 collective-permute-done.1.refs_0_
  14.4 0.6 %collective-permute-done.7.refs_7_ = bf16[128,256]{1,0:T(8,128)(2,1)S(1)} collective-permute-done((bf16[128,256]{1,0:T(8,128)(2,1)S(1)}, bf16[128,256]{1,0:T(8,128)(2,1)S(1)}, u32[]{:S(2)}, u32[]{:S(2)}) %collective-permute-start.7) | collective-permute-done | bytes 65568 | tf_op jit(solution)/shard_map/gather_features/ppermute | solution.py:27
  15.1 2.1 %collective-permute-done.5.refs_5_ = bf16[128,256]{1,0:T(8,128)(2,1)S(1)} collective-permute-done((bf16[128,256]{1,0:T(8,128)(2,1)S(1)}, bf16[128,256]{1,0:T(8,128)(2,1)S(1)}, u32[]{:S(2)}, u32[]{:S(2)}) %collective-permute-start.5) | collective-permute-done | bytes 65568 | tf_op jit(solution)/shard_map/gather_features/ppermute | solution.py:27
  17.1 0.0 collective-permute-done.6.refs_6_
  17.1 0.0 copy-done
  17.1 0.0 copy-done.2
  17.1 0.9 %forward_blocks.1 = (bf16[256,256]{1,0:T(8,128)(2,1)S(1)}, bf16[256,256]{1,0:T(8,128)(2,1)S(1)}) custom-call(s32[8,128]{1,0:T(8,128)S(1)} %gather_features.1.info, bf16[6,128,128]{2,1,0:T(8,128)(2,1)S(1)} %bitcast.7, bf16[128,256]{1,0:T(8,128)(2,1)S(1)} %collective-permute-done.1.refs_0_, bf16[128,256]{1,0:T(8,128)(2,1)S(1)} %collective-permute-done.2.refs_1_, ...), custom_call_target="tpu_custom_call" | custom-call | tf_op jit(solution)/shard_map/forward_blocks/pallas_call | solution.py:201
  18.1 0.1 collective-permute-start.8
  18.2 1.3 %collective-permute-done.8 = bf16[256,256]{1,0:T(8,128)(2,1)S(1)} collective-permute-done((bf16[256,256]{1,0:T(8,128)(2,1)S(1)}, bf16[256,256]{1,0:T(8,128)(2,1)S(1)}, u32[]{:S(2)}, u32[]{:S(2)}) %collective-permute-start.8) | collective-permute-done | bytes 131104 | tf_op jit(solution)/shard_map/sum_rows/ppermute | solution.py:27
  19.5 0.0 copy-start.1
  19.5 0.0 copy-start.3
  19.5 1.6 %collective-permute-start.9 = (bf16[256,256]{1,0:T(8,128)(2,1)S(1)}, bf16[256,256]{1,0:T(8,128)(2,1)S(1)}, u32[]{:S(2)}, u32[]{:S(2)}) collective-permute-start(bf16[256,256]{1,0:T(8,128)(2,1)S(1)} %add_convert_fusion.mine), channel_id=1, source_target_pairs={{0,2},{1,3},{2,0},{3,1},{4,6},{5,7},{6,4},{7,5},{8,10},{9,11},{10,... | collective-permute-start | bytes 393224 | tf_op jit(solution)/shard_map/sum_rows/ppermute | solution.py:27
  21.1 4.1 %collective-permute-done.9.got = bf16[256,256]{1,0:T(8,128)(2,1)S(1)} collective-permute-done((bf16[256,256]{1,0:T(8,128)(2,1)S(1)}, bf16[256,256]{1,0:T(8,128)(2,1)S(1)}, u32[]{:S(2)}, u32[]{:S(2)}) %collective-permute-start.9) | collective-permute-done | bytes 131104 | tf_op jit(solution)/shard_map/sum_rows/ppermute | solution.py:27
  25.2 0.0 copy-done.1
  25.2 0.0 copy-done.3
  25.2 0.9 %dense.1 = (bf16[128,256]{1,0:T(8,128)(2,1)}, bf16[256,256]{1,0:T(8,128)(2,1)S(1)}, bf16[128,256]{1,0:T(8,128)(2,1)S(1)}, f32[128,256]{1,0:T(8,128)S(1)}) custom-call(bf16[256,256]{1,0:T(8,128)(2,1)S(1)} %add_convert_fusion.mine, bf16[256,256]{1,0:T(8,128)(2,1)S(1)} %collective-permute-done.9.got, bf16[256,256]{1,0:T(8,128)(2,1)S(1)} %copy-done.1, ...), custom_call_target="tpu_custom_call" | custom-call | tf_op jit(solution)/shard_map/dense/pallas_call | solution.py:225
  26.0 0.0 collective-permute-start.11
  26.0 0.5 %collective-permute-start.10 = (bf16[128,256]{1,0:T(8,128)(2,1)S(1)}, bf16[128,256]{1,0:T(8,128)(2,1)S(1)}, u32[]{:S(2)}, u32[]{:S(2)}) collective-permute-start(bf16[128,256]{1,0:T(8,128)(2,1)S(1)} %get-tuple-element.42), channel_id=1, source_target_pairs={{0,1},{1,0},{2,3},{3,2},{4,5},{5,4},{6,7},{7,6},{8,9},{9,8},{10,11... | collective-permute-start | bytes 196616 | tf_op jit(solution)/shard_map/swap_cores/ppermute | solution.py:27
  26.6 0.9 %collective-permute-done.10 = bf16[128,256]{1,0:T(8,128)(2,1)S(1)} collective-permute-done((bf16[128,256]{1,0:T(8,128)(2,1)S(1)}, bf16[128,256]{1,0:T(8,128)(2,1)S(1)}, u32[]{:S(2)}, u32[]{:S(2)}) %collective-permute-start.10) | collective-permute-done | bytes 65568 | tf_op jit(solution)/shard_map/swap_cores/ppermute | solution.py:27
  27.5 0.0 collective-permute-done.11.refs_1_
  27.5 2.3 %collective-permute-start.12 = (bf16[128,256]{1,0:T(8,128)(2,1)S(1)}, bf16[128,256]{1,0:T(8,128)(2,1)S(1)}, u32[]{:S(2)}, u32[]{:S(2)}) collective-permute-start(bf16[128,256]{1,0:T(8,128)(2,1)S(1)} %add_convert_fusion.7), channel_id=1, source_target_pairs={{0,17},{1,16},{2,19},{3,18},{4,21},{5,20},{6,23},{7,22},{8,25},{9,... | collective-permute-start | bytes 196616 | tf_op jit(solution)/shard_map/sum_weight/ppermute | solution.py:35
  29.8 1.0 %backward_blocks.1 = (bf16[128,256]{1,0:T(8,128)(2,1)S(1)}, bf16[128,256]{1,0:T(8,128)(2,1)S(1)}, bf16[256,256]{1,0:T(8,128)(2,1)S(1)}, bf16[128,256]{1,0:T(8,12...) custom-call(s32[8,128]{1,0:T(8,128)S(1)} %gather_features.1.info, ...), custom_call_target="tpu_custom_call" | custom-call | tf_op jit(solution)/shard_map/backward_blocks/pallas_call | solution.py:267
  30.8 0.8 %collective-permute-start.15 = (bf16[128,256]{1,0:T(8,128)(2,1)S(1)}, bf16[128,256]{1,0:T(8,128)(2,1)S(1)}, u32[]{:S(2)}, u32[]{:S(2)}) collective-permute-start(bf16[128,256]{1,0:T(8,128)(2,1)S(1)} %get-tuple-element.48), channel_id=1, source_target_pairs={{0,4},{4,0},{8,12},{12,8},{16,20},{20,16},{24,28},{28,24},{1,5},{5... | collective-permute-start | bytes 196616 | tf_op jit(solution)/shard_map/sum_columns/ppermute | solution.py:27
  31.6 1.3 %collective-permute-start.16 = (bf16[128,256]{1,0:T(8,128)(2,1)S(1)}, bf16[128,256]{1,0:T(8,128)(2,1)S(1)}, u32[]{:S(2)}, u32[]{:S(2)}) collective-permute-start(bf16[128,256]{1,0:T(8,128)(2,1)S(1)} %get-tuple-element.49), channel_id=1, source_target_pairs={{0,4},{4,0},{8,12},{12,8},{16,20},{20,16},{24,28},{28,24},{1,5},{5... | collective-permute-start | bytes 196616 | tf_op jit(solution)/shard_map/sum_columns/ppermute | solution.py:27
  32.9 0.7 %collective-permute-start.14 = (bf16[256,256]{1,0:T(8,128)(2,1)S(1)}, bf16[256,256]{1,0:T(8,128)(2,1)S(1)}, u32[]{:S(2)}, u32[]{:S(2)}) collective-permute-start(bf16[256,256]{1,0:T(8,128)(2,1)S(1)} %get-tuple-element.47), channel_id=1, source_target_pairs={{0,4},{4,0},{8,12},{12,8},{16,20},{20,16},{24,28},{28,24},{1,5},{5... | collective-permute-start | bytes 393224 | tf_op jit(solution)/shard_map/sum_columns/ppermute | solution.py:27
  33.6 0.3 collective-permute-done.12
  33.9 0.2 collective-permute-start.13
  34.1 3.1 %collective-permute-done.16 = bf16[128,256]{1,0:T(8,128)(2,1)S(1)} collective-permute-done((bf16[128,256]{1,0:T(8,128)(2,1)S(1)}, bf16[128,256]{1,0:T(8,128)(2,1)S(1)}, u32[]{:S(2)}, u32[]{:S(2)}) %collective-permute-start.16) | collective-permute-done | bytes 65568 | tf_op jit(solution)/shard_map/sum_columns/ppermute | solution.py:27
  37.2 0.0 collective-permute-done.15
  37.3 1.2 %collective-permute-start.20 = (bf16[128,256]{1,0:T(8,128)(2,1)S(1)}, bf16[128,256]{1,0:T(8,128)(2,1)S(1)}, u32[]{:S(2)}, u32[]{:S(2)}) collective-permute-start(bf16[128,256]{1,0:T(8,128)(2,1)S(1)} %add_convert_fusion.2), channel_id=1, source_target_pairs={{0,24},{4,28},{8,16},{12,20},{16,8},{20,12},{24,0},{28,4},{1,25},{... | collective-permute-start | bytes 196616 | tf_op jit(solution)/shard_map/sum_columns/ppermute | solution.py:27
  38.4 1.2 %collective-permute-start.21 = (bf16[128,256]{1,0:T(8,128)(2,1)S(1)}, bf16[128,256]{1,0:T(8,128)(2,1)S(1)}, u32[]{:S(2)}, u32[]{:S(2)}) collective-permute-start(bf16[128,256]{1,0:T(8,128)(2,1)S(1)} %add_convert_fusion.1), channel_id=1, source_target_pairs={{0,16},{4,20},{8,24},{12,28},{16,0},{20,4},{24,8},{28,12},{1,17},{... | collective-permute-start | bytes 196616 | tf_op jit(solution)/shard_map/sum_columns/ppermute | solution.py:27
  39.6 0.0 collective-permute-done.14.refs_1_
  39.6 0.0 collective-permute-done.13
  39.6 0.1 collective-permute-start.17
  39.7 2.2 %collective-permute-start.19 = (bf16[128,256]{1,0:T(8,128)(2,1)S(1)}, bf16[128,256]{1,0:T(8,128)(2,1)S(1)}, u32[]{:S(2)}, u32[]{:S(2)}) collective-permute-start(bf16[128,256]{1,0:T(8,128)(2,1)S(1)} %add_convert_fusion.3), channel_id=1, source_target_pairs={{0,8},{4,12},{8,0},{12,4},{16,24},{20,28},{24,16},{28,20},{1,9},{5... | collective-permute-start | bytes 196616 | tf_op jit(solution)/shard_map/sum_columns/ppermute | solution.py:27
  41.9 2.1 %collective-permute-done.17 = bf16[128,256]{1,0:T(8,128)(2,1)S(1)} collective-permute-done((bf16[128,256]{1,0:T(8,128)(2,1)S(1)}, bf16[128,256]{1,0:T(8,128)(2,1)S(1)}, u32[]{:S(2)}, u32[]{:S(2)}) %collective-permute-start.17) | collective-permute-done | bytes 65568 | tf_op jit(solution)/shard_map/sum_columns/sum_weight/sum_weight/ppermute | solution.py:35
  44.0 0.1 collective-permute-start.18
  44.1 1.2 %collective-permute-done.21.refs_2_ = bf16[128,256]{1,0:T(8,128)(2,1)S(1)} collective-permute-done((bf16[128,256]{1,0:T(8,128)(2,1)S(1)}, bf16[128,256]{1,0:T(8,128)(2,1)S(1)}, u32[]{:S(2)}, u32[]{:S(2)}) %collective-permute-start.21) | collective-permute-done | bytes 65568 | tf_op jit(solution)/shard_map/sum_columns/ppermute | solution.py:27
  45.3 0.0 collective-permute-done.20.refs_3_
  45.3 0.1 collective-permute-done.19.refs_4_
  45.4 0.0 collective-permute-done.18.other
  45.4 0.8 %shard_map.94 = (f32[128,256]{1,0:T(8,128)}, f32[256,256]{1,0:T(8,128)}) custom-call(bf16[128,256]{1,0:T(8,128)(2,1)S(1)} %add_convert_fusion.4.mine, bf16[128,256]{1,0:T(8,128)(2,1)S(1)} %collective-permute-done.18.other, bf16[256,256]{1,0:T(8,128)(2,1)S(1)} %get-tuple-element.55.refs_0_, bf16[256,256]{1,0:T(8,128)(2,1)S(1)} %collective-permute-done.14.refs_1_, ...), custom_call_target="tpu_custom_call" | custom-call | tf_op jit(solution)/shard_map/pallas_call | solution.py:298
  (9 shorter events, 0.2 us)
Async XLA Ops:
  0.6 7.9 %collective-permute-start = (bf16[128,256]{1,0:T(8,128)(2,1)}, bf16[128,256]{1,0:T(8,128)(2,1)S(1)}, u32[]{:S(2)}, u32[]{:S(2)}) collective-permute-start(bf16[128,256]{1,0:T(8,128)(2,1)} %bitcast.9), channel_id=1, source_target_pairs={{0,8},{4,12},{8,0},{12,4},{16,24},{20,28},{24,16},{28,20},{1,9},{5... | collective-permute-start | bytes 196616 | tf_op jit(solution)/shard_map/gather_features/ppermute | solution.py:27
  3.7 7.1 %collective-permute-start.3 = (bf16[128,256]{1,0:T(8,128)(2,1)}, bf16[128,256]{1,0:T(8,128)(2,1)S(1)}, u32[]{:S(2)}, u32[]{:S(2)}) collective-permute-start(bf16[128,256]{1,0:T(8,128)(2,1)} %bitcast.10), channel_id=1, source_target_pairs={{0,24},{4,28},{8,16},{12,20},{16,8},{20,12},{24,0},{28,4},{1,25},{... | collective-permute-start | bytes 196616 | tf_op jit(solution)/shard_map/gather_features/ppermute | solution.py:27
  6.2 6.7 %collective-permute-start.2 = (bf16[128,256]{1,0:T(8,128)(2,1)}, bf16[128,256]{1,0:T(8,128)(2,1)S(1)}, u32[]{:S(2)}, u32[]{:S(2)}) collective-permute-start(bf16[128,256]{1,0:T(8,128)(2,1)} %bitcast.11), channel_id=1, source_target_pairs={{0,16},{4,20},{8,24},{12,28},{16,0},{20,4},{24,8},{28,12},{1,17},{... | collective-permute-start | bytes 196616 | tf_op jit(solution)/shard_map/gather_features/ppermute | solution.py:27
  6.3 8.1 %collective-permute-start.1 = (bf16[128,256]{1,0:T(8,128)(2,1)}, bf16[128,256]{1,0:T(8,128)(2,1)S(1)}, u32[]{:S(2)}, u32[]{:S(2)}) collective-permute-start(bf16[128,256]{1,0:T(8,128)(2,1)} %bitcast.12), channel_id=1, source_target_pairs={{0,4},{4,0},{8,12},{12,8},{16,20},{20,16},{24,28},{28,24},{1,5},{5... | collective-permute-start | bytes 196616 | tf_op jit(solution)/shard_map/gather_features/ppermute | solution.py:27
  8.5 5.9 %copy-start.4 = (s32[1,1,6]{2,1,0:T(1,128)S(1)}, s32[1,1,6]{2,1,0:T(1,128)}, u32[]{:S(2)}) copy-start(s32[1,1,6]{2,1,0:T(1,128)} %param.10) | copy-start | bytes 76
  8.5 5.9 %copy-start.5 = (s32[1,1,6]{2,1,0:T(1,128)S(1)}, s32[1,1,6]{2,1,0:T(1,128)}, u32[]{:S(2)}) copy-start(s32[1,1,6]{2,1,0:T(1,128)} %param.11) | copy-start | bytes 76
  8.5 8.6 %copy-start = (bf16[1,1,6,128,128]{4,3,2,1,0:T(8,128)(2,1)S(1)}, bf16[1,1,6,128,128]{4,3,2,1,0:T(8,128)(2,1)}, u32[]{:S(2)}) copy-start(bf16[1,1,6,128,128]{4,3,2,1,0:T(8,128)(2,1)} %param.13) | copy-start | bytes 589828
  8.5 8.6 %copy-start.2 = (bf16[1,128,256]{2,1,0:T(8,128)(2,1)S(1)}, bf16[1,128,256]{2,1,0:T(8,128)(2,1)}, u32[]{:S(2)}) copy-start(bf16[1,128,256]{2,1,0:T(8,128)(2,1)} %param.7) | copy-start | bytes 196612
  8.5 5.9 %collective-permute-start.4 = (bf16[128,256]{1,0:T(8,128)(2,1)}, bf16[128,256]{1,0:T(8,128)(2,1)S(1)}, u32[]{:S(2)}, u32[]{:S(2)}) collective-permute-start(bf16[128,256]{1,0:T(8,128)(2,1)} %bitcast.14), channel_id=1, source_target_pairs={{0,2},{1,3},{2,0},{3,1},{4,6},{5,7},{6,4},{7,5},{8,10},{9,11},{10,... | collective-permute-start | bytes 196616 | tf_op jit(solution)/shard_map/gather_features/ppermute | solution.py:27
  10.1 7.0 %collective-permute-start.6 = (bf16[128,256]{1,0:T(8,128)(2,1)S(1)}, bf16[128,256]{1,0:T(8,128)(2,1)S(1)}, u32[]{:S(2)}, u32[]{:S(2)}) collective-permute-start(bf16[128,256]{1,0:T(8,128)(2,1)S(1)} %collective-permute-done.refs_2_), channel_id=1, source_target_pairs={{0,4},{4,0},{8,12},{12,8},{16,20},{20,16},{24,28},{28,24},{1,5},{5... | collective-permute-start | bytes 196616 | tf_op jit(solution)/shard_map/gather_features/ppermute | solution.py:27
  10.8 4.3 %collective-permute-start.7 = (bf16[128,256]{1,0:T(8,128)(2,1)S(1)}, bf16[128,256]{1,0:T(8,128)(2,1)S(1)}, u32[]{:S(2)}, u32[]{:S(2)}) collective-permute-start(bf16[128,256]{1,0:T(8,128)(2,1)S(1)} %collective-permute-done.3.refs_3_), channel_id=1, source_target_pairs={{0,4},{4,0},{8,12},{12,8},{16,20},{20,16},{24,28},{28,24},{1,5},{5... | collective-permute-start | bytes 196616 | tf_op jit(solution)/shard_map/gather_features/ppermute | solution.py:27
  12.9 4.3 %collective-permute-start.5 = (bf16[128,256]{1,0:T(8,128)(2,1)S(1)}, bf16[128,256]{1,0:T(8,128)(2,1)S(1)}, u32[]{:S(2)}, u32[]{:S(2)}) collective-permute-start(bf16[128,256]{1,0:T(8,128)(2,1)S(1)} %collective-permute-done.2.refs_1_), channel_id=1, source_target_pairs={{0,4},{4,0},{8,12},{12,8},{16,20},{20,16},{24,28},{28,24},{1,5},{5... | collective-permute-start | bytes 196616 | tf_op jit(solution)/shard_map/gather_features/ppermute | solution.py:27
  18.1 1.4 %collective-permute-start.8 = (bf16[256,256]{1,0:T(8,128)(2,1)S(1)}, bf16[256,256]{1,0:T(8,128)(2,1)S(1)}, u32[]{:S(2)}, u32[]{:S(2)}) collective-permute-start(bf16[256,256]{1,0:T(8,128)(2,1)S(1)} %get-tuple-element.39), channel_id=1, source_target_pairs={{0,1},{1,0},{2,3},{3,2},{4,5},{5,4},{6,7},{7,6},{8,9},{9,8},{10,11... | collective-permute-start | bytes 393224 | tf_op jit(solution)/shard_map/sum_rows/ppermute | solution.py:27
  19.5 5.7 %copy-start.1 = (bf16[256,256]{1,0:T(8,128)(2,1)S(1)}, bf16[256,256]{1,0:T(8,128)(2,1)}, u32[]{:S(2)}) copy-start(bf16[256,256]{1,0:T(8,128)(2,1)} %weight.1) | copy-start | bytes 393220
  19.5 5.7 %copy-start.3 = (bf16[1,128,256]{2,1,0:T(8,128)(2,1)S(1)}, bf16[1,128,256]{2,1,0:T(8,128)(2,1)}, u32[]{:S(2)}) copy-start(bf16[1,128,256]{2,1,0:T(8,128)(2,1)} %param.9) | copy-start | bytes 196612
  19.5 5.6 %collective-permute-start.9 = (bf16[256,256]{1,0:T(8,128)(2,1)S(1)}, bf16[256,256]{1,0:T(8,128)(2,1)S(1)}, u32[]{:S(2)}, u32[]{:S(2)}) collective-permute-start(bf16[256,256]{1,0:T(8,128)(2,1)S(1)} %add_convert_fusion.mine), channel_id=1, source_target_pairs={{0,2},{1,3},{2,0},{3,1},{4,6},{5,7},{6,4},{7,5},{8,10},{9,11},{10,... | collective-permute-start | bytes 393224 | tf_op jit(solution)/shard_map/sum_rows/ppermute | solution.py:27
  26.0 1.4 %collective-permute-start.11 = (bf16[256,256]{1,0:T(8,128)(2,1)S(1)}, bf16[256,256]{1,0:T(8,128)(2,1)S(1)}, u32[]{:S(2)}, u32[]{:S(2)}) collective-permute-start(bf16[256,256]{1,0:T(8,128)(2,1)S(1)} %get-tuple-element.43.refs_0_), channel_id=1, source_target_pairs={{0,1},{1,0},{2,3},{3,2},{4,5},{5,4},{6,7},{7,6},{8,9},{9,8},{10,11... | collective-permute-start | bytes 393224 | tf_op jit(solution)/shard_map/swap_cores/ppermute | solution.py:27
  26.0 1.4 %collective-permute-start.10 = (bf16[128,256]{1,0:T(8,128)(2,1)S(1)}, bf16[128,256]{1,0:T(8,128)(2,1)S(1)}, u32[]{:S(2)}, u32[]{:S(2)}) collective-permute-start(bf16[128,256]{1,0:T(8,128)(2,1)S(1)} %get-tuple-element.42), channel_id=1, source_target_pairs={{0,1},{1,0},{2,3},{3,2},{4,5},{5,4},{6,7},{7,6},{8,9},{9,8},{10,11... | collective-permute-start | bytes 196616 | tf_op jit(solution)/shard_map/swap_cores/ppermute | solution.py:27
  27.5 6.3 %collective-permute-start.12 = (bf16[128,256]{1,0:T(8,128)(2,1)S(1)}, bf16[128,256]{1,0:T(8,128)(2,1)S(1)}, u32[]{:S(2)}, u32[]{:S(2)}) collective-permute-start(bf16[128,256]{1,0:T(8,128)(2,1)S(1)} %add_convert_fusion.7), channel_id=1, source_target_pairs={{0,17},{1,16},{2,19},{3,18},{4,21},{5,20},{6,23},{7,22},{8,25},{9,... | collective-permute-start | bytes 196616 | tf_op jit(solution)/shard_map/sum_weight/ppermute | solution.py:35
  30.8 6.4 %collective-permute-start.15 = (bf16[128,256]{1,0:T(8,128)(2,1)S(1)}, bf16[128,256]{1,0:T(8,128)(2,1)S(1)}, u32[]{:S(2)}, u32[]{:S(2)}) collective-permute-start(bf16[128,256]{1,0:T(8,128)(2,1)S(1)} %get-tuple-element.48), channel_id=1, source_target_pairs={{0,4},{4,0},{8,12},{12,8},{16,20},{20,16},{24,28},{28,24},{1,5},{5... | collective-permute-start | bytes 196616 | tf_op jit(solution)/shard_map/sum_columns/ppermute | solution.py:27
  31.6 5.6 %collective-permute-start.16 = (bf16[128,256]{1,0:T(8,128)(2,1)S(1)}, bf16[128,256]{1,0:T(8,128)(2,1)S(1)}, u32[]{:S(2)}, u32[]{:S(2)}) collective-permute-start(bf16[128,256]{1,0:T(8,128)(2,1)S(1)} %get-tuple-element.49), channel_id=1, source_target_pairs={{0,4},{4,0},{8,12},{12,8},{16,20},{20,16},{24,28},{28,24},{1,5},{5... | collective-permute-start | bytes 196616 | tf_op jit(solution)/shard_map/sum_columns/ppermute | solution.py:27
  32.9 6.7 %collective-permute-start.14 = (bf16[256,256]{1,0:T(8,128)(2,1)S(1)}, bf16[256,256]{1,0:T(8,128)(2,1)S(1)}, u32[]{:S(2)}, u32[]{:S(2)}) collective-permute-start(bf16[256,256]{1,0:T(8,128)(2,1)S(1)} %get-tuple-element.47), channel_id=1, source_target_pairs={{0,4},{4,0},{8,12},{12,8},{16,20},{20,16},{24,28},{28,24},{1,5},{5... | collective-permute-start | bytes 393224 | tf_op jit(solution)/shard_map/sum_columns/ppermute | solution.py:27
  33.9 5.7 %collective-permute-start.13 = (bf16[128,256]{1,0:T(8,128)(2,1)S(1)}, bf16[128,256]{1,0:T(8,128)(2,1)S(1)}, u32[]{:S(2)}, u32[]{:S(2)}) collective-permute-start(bf16[128,256]{1,0:T(8,128)(2,1)S(1)} %add_convert_fusion.6), channel_id=1, source_target_pairs={{0,9},{1,8},{2,11},{3,10},{4,13},{5,12},{6,15},{7,14},{8,1},{9,0},... | collective-permute-start | bytes 196616 | tf_op jit(solution)/shard_map/sum_columns/sum_weight/sum_weight/ppermute | solution.py:35
  37.3 8.0 %collective-permute-start.20 = (bf16[128,256]{1,0:T(8,128)(2,1)S(1)}, bf16[128,256]{1,0:T(8,128)(2,1)S(1)}, u32[]{:S(2)}, u32[]{:S(2)}) collective-permute-start(bf16[128,256]{1,0:T(8,128)(2,1)S(1)} %add_convert_fusion.2), channel_id=1, source_target_pairs={{0,24},{4,28},{8,16},{12,20},{16,8},{20,12},{24,0},{28,4},{1,25},{... | collective-permute-start | bytes 196616 | tf_op jit(solution)/shard_map/sum_columns/ppermute | solution.py:27
  38.4 6.8 %collective-permute-start.21 = (bf16[128,256]{1,0:T(8,128)(2,1)S(1)}, bf16[128,256]{1,0:T(8,128)(2,1)S(1)}, u32[]{:S(2)}, u32[]{:S(2)}) collective-permute-start(bf16[128,256]{1,0:T(8,128)(2,1)S(1)} %add_convert_fusion.1), channel_id=1, source_target_pairs={{0,16},{4,20},{8,24},{12,28},{16,0},{20,4},{24,8},{28,12},{1,17},{... | collective-permute-start | bytes 196616 | tf_op jit(solution)/shard_map/sum_columns/ppermute | solution.py:27
  39.6 4.4 %collective-permute-start.17 = (bf16[128,256]{1,0:T(8,128)(2,1)S(1)}, bf16[128,256]{1,0:T(8,128)(2,1)S(1)}, u32[]{:S(2)}, u32[]{:S(2)}) collective-permute-start(bf16[128,256]{1,0:T(8,128)(2,1)S(1)} %add_convert_fusion.5), channel_id=1, source_target_pairs={{0,5},{1,4},{2,7},{3,6},{4,1},{5,0},{6,3},{7,2},{8,13},{9,12},{10,... | collective-permute-start | bytes 196616 | tf_op jit(solution)/shard_map/sum_columns/sum_weight/sum_weight/ppermute | solution.py:35
  39.7 5.6 %collective-permute-start.19 = (bf16[128,256]{1,0:T(8,128)(2,1)S(1)}, bf16[128,256]{1,0:T(8,128)(2,1)S(1)}, u32[]{:S(2)}, u32[]{:S(2)}) collective-permute-start(bf16[128,256]{1,0:T(8,128)(2,1)S(1)} %add_convert_fusion.3), channel_id=1, source_target_pairs={{0,8},{4,12},{8,0},{12,4},{16,24},{20,28},{24,16},{28,20},{1,9},{5... | collective-permute-start | bytes 196616 | tf_op jit(solution)/shard_map/sum_columns/ppermute | solution.py:27
  44.0 1.4 %collective-permute-start.18 = (bf16[128,256]{1,0:T(8,128)(2,1)S(1)}, bf16[128,256]{1,0:T(8,128)(2,1)S(1)}, u32[]{:S(2)}, u32[]{:S(2)}) collective-permute-start(bf16[128,256]{1,0:T(8,128)(2,1)S(1)} %add_convert_fusion.4.mine), channel_id=1, source_target_pairs={{0,1},{1,0},{2,3},{3,2},{4,5},{5,4},{6,7},{7,6},{8,9},{9,8},{10,11... | collective-permute-start | bytes 196616 | tf_op jit(solution)/shard_map/sum_weight/ppermute | solution.py:27

commit v7 on v6

--- a/solution.py
+++ b/solution.py
@@ -92,11 +92,15 @@
 
 
 def info_kernel(rows, cols, counts, info):
-    slots = rows.shape[1]
-    info[...] = jnp.zeros_like(info)
-    info[0:1, pl.ds(0, slots)] = rows[...] ^ lax.axis_index("gc")
-    info[1:2, pl.ds(0, slots)] = cols[...] ^ lax.axis_index("gr")
-    info[2:3, pl.ds(0, 1)] = counts[...]
+    gr, gc = lax.axis_index("gr"), lax.axis_index("gc")
+
+    def one(s, _):
+        info[0, s] = rows[0, s] ^ gc
+        info[1, s] = cols[0, s] ^ gr
+        return 0
+
+    lax.fori_loop(0, rows.shape[1], one, 0)
+    info[2, 0] = counts[0, 0]
 
 
 def forward_kernel(layout, send_masks, keep_masks, info, values, *refs):
@@ -185,9 +189,9 @@
         values = block_values[0, 0]
         info = pl.pallas_call(
             info_kernel,
-            out_shape=jax.ShapeDtypeStruct((8, 128 * pl.cdiv(values.shape[0], 128)), jnp.int32),
-            in_specs=[VMEM] * 3,
-            out_specs=VMEM,
+            out_shape=jax.ShapeDtypeStruct((3, values.shape[0]), jnp.int32),
+            in_specs=[SMEM] * 3,
+            out_specs=SMEM,
             compiler_params=params(limit),
             cost_estimate=pl.CostEstimate(flops=5 * 10**9, bytes_accessed=0, transcendentals=0),
         )(*[after(v, held[2]) for v in (block_rows[0], block_cols[0], block_counts)])

time: 46.3 us -> 46.3 us (level)
  waiting for transfers between devices: 16.5 us -> 15.3 us
  Pallas kernels: 3.58 us -> 4.71 us
    ppermute x19, waiting for transfers between devices: 14.2 us -> 13 us  [swap(): return lax.ppermute(value, axis, [(i, i ^ mask) for i in range(size)])]
    pallas_call x1, Pallas kernels: 0.01 us -> 1.21 us  [per_device(): pl.pallas_call(info_kernel, out_shape=jax.ShapeDtypeStruct((3, values.sha...]
  transfers between devices with their start and end apart: 22 -> 22, of which waited for: 12 -> 11; matrix products, arithmetic and copies ran while one was open for 0% -> 0% of each run, Pallas kernels for 2% -> 5%
where the time goes in v7:
time: 46.3 us; the launch traced here: 46.1 us
  starting transfers between devices  24.4 us (53%)
  waiting for transfers between devices  15.3 us (33%)
  Pallas kernels  4.71 us (10%)
  between operations  1.45 us (3%)
    ppermute x19, starting transfers between devices, swap(): return lax.ppermute(value, axis, [(i, i ^ mask) for i in range(size)])  21.8 us
    ppermute x19, waiting for transfers between devices, swap(): return lax.ppermute(value, axis, [(i, i ^ mask) for i in range(size)])  13 us
    ppermute x3, starting transfers between devices, swap_crossed(): return lax.ppermute(value, ('gr', 'gc'), pairs)  2.64 us
    ppermute x3, waiting for transfers between devices, swap_crossed(): return lax.ppermute(value, ('gr', 'gc'), pairs)  2.38 us
    pallas_call x1, Pallas kernels, per_device(): pl.pallas_call(info_kernel, out_shape=jax.ShapeDtypeStruct((3, values.sha...  1.21 us
  transfers between devices with their start and end apart: 22, of which 11 were waited for; matrix products, arithmetic and copies ran while one was open for 0% of the time, Pallas kernels for 5%

profile of v7, /device:TPU:0, one launch (start us, length us, event | category | flops | bytes accessed | tf_op | source)
XLA Modules:
  0.0 46.1 jit_solution(11170283754247220977)
XLA Ops:
  0.6 3.1 %collective-permute-start = (bf16[128,256]{1,0:T(8,128)(2,1)}, bf16[128,256]{1,0:T(8,128)(2,1)S(1)}, u32[]{:S(2)}, u32[]{:S(2)}) collective-permute-start(bf16[128,256]{1,0:T(8,128)(2,1)} %bitcast.9), channel_id=1, source_target_pairs={{0,8},{4,12},{8,0},{12,4},{16,24},{20,28},{24,16},{28,20},{1,9},{5... | collective-permute-start | bytes 196616 | tf_op jit(solution)/shard_map/gather_features/ppermute | solution.py:27
  3.7 2.5 %collective-permute-start.3 = (bf16[128,256]{1,0:T(8,128)(2,1)}, bf16[128,256]{1,0:T(8,128)(2,1)S(1)}, u32[]{:S(2)}, u32[]{:S(2)}) collective-permute-start(bf16[128,256]{1,0:T(8,128)(2,1)} %bitcast.10), channel_id=1, source_target_pairs={{0,24},{4,28},{8,16},{12,20},{16,8},{20,12},{24,0},{28,4},{1,25},{... | collective-permute-start | bytes 196616 | tf_op jit(solution)/shard_map/gather_features/ppermute | solution.py:27
  6.2 0.1 collective-permute-start.2
  6.3 1.5 %collective-permute-start.1 = (bf16[128,256]{1,0:T(8,128)(2,1)}, bf16[128,256]{1,0:T(8,128)(2,1)S(1)}, u32[]{:S(2)}, u32[]{:S(2)}) collective-permute-start(bf16[128,256]{1,0:T(8,128)(2,1)} %bitcast.12), channel_id=1, source_target_pairs={{0,4},{4,0},{8,12},{12,8},{16,20},{20,16},{24,28},{28,24},{1,5},{5... | collective-permute-start | bytes 196616 | tf_op jit(solution)/shard_map/gather_features/ppermute | solution.py:27
  8.5 0.0 collective-permute-done.refs_2_
  8.5 0.0 copy-start.4
  8.5 0.0 copy-start.5
  8.5 0.0 copy-start
  8.5 0.0 copy-start.2
  8.5 1.6 %collective-permute-start.4 = (bf16[128,256]{1,0:T(8,128)(2,1)}, bf16[128,256]{1,0:T(8,128)(2,1)S(1)}, u32[]{:S(2)}, u32[]{:S(2)}) collective-permute-start(bf16[128,256]{1,0:T(8,128)(2,1)} %bitcast.14), channel_id=1, source_target_pairs={{0,2},{1,3},{2,0},{3,1},{4,6},{5,7},{6,4},{7,5},{8,10},{9,11},{10,... | collective-permute-start | bytes 196616 | tf_op jit(solution)/shard_map/gather_features/ppermute | solution.py:27
  10.1 0.5 %collective-permute-start.6 = (bf16[128,256]{1,0:T(8,128)(2,1)S(1)}, bf16[128,256]{1,0:T(8,128)(2,1)S(1)}, u32[]{:S(2)}, u32[]{:S(2)}) collective-permute-start(bf16[128,256]{1,0:T(8,128)(2,1)S(1)} %collective-permute-done.refs_2_), channel_id=1, source_target_pairs={{0,4},{4,0},{8,12},{12,8},{16,20},{20,16},{24,28},{28,24},{1,5},{5... | collective-permute-start | bytes 196616 | tf_op jit(solution)/shard_map/gather_features/ppermute | solution.py:27
  10.6 0.2 collective-permute-done.3.refs_3_
  10.8 1.5 %collective-permute-start.7 = (bf16[128,256]{1,0:T(8,128)(2,1)S(1)}, bf16[128,256]{1,0:T(8,128)(2,1)S(1)}, u32[]{:S(2)}, u32[]{:S(2)}) collective-permute-start(bf16[128,256]{1,0:T(8,128)(2,1)S(1)} %collective-permute-done.3.refs_3_), channel_id=1, source_target_pairs={{0,4},{4,0},{8,12},{12,8},{16,20},{20,16},{24,28},{28,24},{1,5},{5... | collective-permute-start | bytes 196616 | tf_op jit(solution)/shard_map/gather_features/ppermute | solution.py:27
  12.3 0.6 %collective-permute-done.2.refs_1_ = bf16[128,256]{1,0:T(8,128)(2,1)S(1)} collective-permute-done((bf16[128,256]{1,0:T(8,128)(2,1)}, bf16[128,256]{1,0:T(8,128)(2,1)S(1)}, u32[]{:S(2)}, u32[]{:S(2)}) %collective-permute-start.2) | collective-permute-done | bytes 65568 | tf_op jit(solution)/shard_map/gather_features/ppermute | solution.py:27
  12.9 1.5 %collective-permute-start.5 = (bf16[128,256]{1,0:T(8,128)(2,1)S(1)}, bf16[128,256]{1,0:T(8,128)(2,1)S(1)}, u32[]{:S(2)}, u32[]{:S(2)}) collective-permute-start(bf16[128,256]{1,0:T(8,128)(2,1)S(1)} %collective-permute-done.2.refs_1_), channel_id=1, source_target_pairs={{0,4},{4,0},{8,12},{12,8},{16,20},{20,16},{24,28},{28,24},{1,5},{5... | collective-permute-start | bytes 196616 | tf_op jit(solution)/shard_map/gather_features/ppermute | solution.py:27
  14.4 0.0 copy-done.4
  14.4 0.0 copy-done.5
  14.4 1.2 %gather_features.1.info = s32[3,6]{1,0:T(4,128)S(1)} custom-call(s32[1,6]{1,0:T(1,128)S(1)} %bitcast.16, s32[1,6]{1,0:T(1,128)S(1)} %bitcast.17, s32[1,1]{1,0:T(1,128)S(6)} %copy.10.counts), custom_call_target="tpu_custom_call" | custom-call | flops 5000000000 | tf_op jit(solution)/shard_map/gather_features/pallas_call | solution.py:190
  15.6 0.0 collective-permute-done.4.refs_1_
  15.6 0.0 collective-permute-done.1.refs_0_
  15.6 0.0 collective-permute-done.7.refs_7_
  15.6 1.5 %collective-permute-done.5.refs_5_ = bf16[128,256]{1,0:T(8,128)(2,1)S(1)} collective-permute-done((bf16[128,256]{1,0:T(8,128)(2,1)S(1)}, bf16[128,256]{1,0:T(8,128)(2,1)S(1)}, u32[]{:S(2)}, u32[]{:S(2)}) %collective-permute-start.5) | collective-permute-done | bytes 65568 | tf_op jit(solution)/shard_map/gather_features/ppermute | solution.py:27
  17.1 0.0 collective-permute-done.6.refs_6_
  17.1 0.0 copy-done
  17.1 0.0 copy-done.2
  17.1 0.9 %forward_blocks.1 = (bf16[256,256]{1,0:T(8,128)(2,1)S(1)}, bf16[256,256]{1,0:T(8,128)(2,1)S(1)}) custom-call(s32[3,6]{1,0:T(4,128)S(1)} %gather_features.1.info, bf16[6,128,128]{2,1,0:T(8,128)(2,1)S(1)} %bitcast.7, bf16[128,256]{1,0:T(8,128)(2,1)S(1)} %collective-permute-done.1.refs_0_, bf16[128,256]{1,0:T(8,128)(2,1)S(1)} %collective-permute-done.2.refs_1_, ...), custom_call_target="tpu_custom_call" | custom-call | tf_op jit(solution)/shard_map/forward_blocks/pallas_call | solution.py:205
  18.0 0.1 collective-permute-start.8
  18.1 1.3 %collective-permute-done.8 = bf16[256,256]{1,0:T(8,128)(2,1)S(1)} collective-permute-done((bf16[256,256]{1,0:T(8,128)(2,1)S(1)}, bf16[256,256]{1,0:T(8,128)(2,1)S(1)}, u32[]{:S(2)}, u32[]{:S(2)}) %collective-permute-start.8) | collective-permute-done | bytes 131104 | tf_op jit(solution)/shard_map/sum_rows/ppermute | solution.py:27
  19.5 0.0 copy-start.1
  19.5 0.0 copy-start.3
  19.5 1.6 %collective-permute-start.9 = (bf16[256,256]{1,0:T(8,128)(2,1)S(1)}, bf16[256,256]{1,0:T(8,128)(2,1)S(1)}, u32[]{:S(2)}, u32[]{:S(2)}) collective-permute-start(bf16[256,256]{1,0:T(8,128)(2,1)S(1)} %add_convert_fusion.mine), channel_id=1, source_target_pairs={{0,2},{1,3},{2,0},{3,1},{4,6},{5,7},{6,4},{7,5},{8,10},{9,11},{10,... | collective-permute-start | bytes 393224 | tf_op jit(solution)/shard_map/sum_rows/ppermute | solution.py:27
  21.1 4.1 %collective-permute-done.9.got = bf16[256,256]{1,0:T(8,128)(2,1)S(1)} collective-permute-done((bf16[256,256]{1,0:T(8,128)(2,1)S(1)}, bf16[256,256]{1,0:T(8,128)(2,1)S(1)}, u32[]{:S(2)}, u32[]{:S(2)}) %collective-permute-start.9) | collective-permute-done | bytes 131104 | tf_op jit(solution)/shard_map/sum_rows/ppermute | solution.py:27
  25.1 0.0 copy-done.1
  25.1 0.0 copy-done.3
  25.1 0.9 %dense.1 = (bf16[128,256]{1,0:T(8,128)(2,1)}, bf16[256,256]{1,0:T(8,128)(2,1)S(1)}, bf16[128,256]{1,0:T(8,128)(2,1)S(1)}, f32[128,256]{1,0:T(8,128)S(1)}) custom-call(bf16[256,256]{1,0:T(8,128)(2,1)S(1)} %add_convert_fusion.mine, bf16[256,256]{1,0:T(8,128)(2,1)S(1)} %collective-permute-done.9.got, bf16[256,256]{1,0:T(8,128)(2,1)S(1)} %copy-done.1, ...), custom_call_target="tpu_custom_call" | custom-call | tf_op jit(solution)/shard_map/dense/pallas_call | solution.py:229
  26.0 0.0 collective-permute-start.11
  26.0 0.5 %collective-permute-start.10 = (bf16[128,256]{1,0:T(8,128)(2,1)S(1)}, bf16[128,256]{1,0:T(8,128)(2,1)S(1)}, u32[]{:S(2)}, u32[]{:S(2)}) collective-permute-start(bf16[128,256]{1,0:T(8,128)(2,1)S(1)} %get-tuple-element.42), channel_id=1, source_target_pairs={{0,1},{1,0},{2,3},{3,2},{4,5},{5,4},{6,7},{7,6},{8,9},{9,8},{10,11... | collective-permute-start | bytes 196616 | tf_op jit(solution)/shard_map/swap_cores/ppermute | solution.py:27
  26.5 0.9 %collective-permute-done.10 = bf16[128,256]{1,0:T(8,128)(2,1)S(1)} collective-permute-done((bf16[128,256]{1,0:T(8,128)(2,1)S(1)}, bf16[128,256]{1,0:T(8,128)(2,1)S(1)}, u32[]{:S(2)}, u32[]{:S(2)}) %collective-permute-start.10) | collective-permute-done | bytes 65568 | tf_op jit(solution)/shard_map/swap_cores/ppermute | solution.py:27
  27.5 0.0 collective-permute-done.11.refs_1_
  27.5 2.3 %collective-permute-start.12 = (bf16[128,256]{1,0:T(8,128)(2,1)S(1)}, bf16[128,256]{1,0:T(8,128)(2,1)S(1)}, u32[]{:S(2)}, u32[]{:S(2)}) collective-permute-start(bf16[128,256]{1,0:T(8,128)(2,1)S(1)} %add_convert_fusion.7), channel_id=1, source_target_pairs={{0,17},{1,16},{2,19},{3,18},{4,21},{5,20},{6,23},{7,22},{8,25},{9,... | collective-permute-start | bytes 196616 | tf_op jit(solution)/shard_map/sum_weight/ppermute | solution.py:35
  29.8 0.9 %backward_blocks.1 = (bf16[128,256]{1,0:T(8,128)(2,1)S(1)}, bf16[128,256]{1,0:T(8,128)(2,1)S(1)}, bf16[256,256]{1,0:T(8,128)(2,1)S(1)}, bf16[128,256]{1,0:T(8,12...) custom-call(s32[3,6]{1,0:T(4,128)S(1)} %gather_features.1.info, ...), custom_call_target="tpu_custom_call" | custom-call | tf_op jit(solution)/shard_map/backward_blocks/pallas_call | solution.py:271
  30.7 0.8 %collective-permute-start.15 = (bf16[128,256]{1,0:T(8,128)(2,1)S(1)}, bf16[128,256]{1,0:T(8,128)(2,1)S(1)}, u32[]{:S(2)}, u32[]{:S(2)}) collective-permute-start(bf16[128,256]{1,0:T(8,128)(2,1)S(1)} %get-tuple-element.48), channel_id=1, source_target_pairs={{0,4},{4,0},{8,12},{12,8},{16,20},{20,16},{24,28},{28,24},{1,5},{5... | collective-permute-start | bytes 196616 | tf_op jit(solution)/shard_map/sum_columns/ppermute | solution.py:27
  31.5 1.3 %collective-permute-start.16 = (bf16[128,256]{1,0:T(8,128)(2,1)S(1)}, bf16[128,256]{1,0:T(8,128)(2,1)S(1)}, u32[]{:S(2)}, u32[]{:S(2)}) collective-permute-start(bf16[128,256]{1,0:T(8,128)(2,1)S(1)} %get-tuple-element.49), channel_id=1, source_target_pairs={{0,4},{4,0},{8,12},{12,8},{16,20},{20,16},{24,28},{28,24},{1,5},{5... | collective-permute-start | bytes 196616 | tf_op jit(solution)/shard_map/sum_columns/ppermute | solution.py:27
  32.8 0.7 %collective-permute-start.14 = (bf16[256,256]{1,0:T(8,128)(2,1)S(1)}, bf16[256,256]{1,0:T(8,128)(2,1)S(1)}, u32[]{:S(2)}, u32[]{:S(2)}) collective-permute-start(bf16[256,256]{1,0:T(8,128)(2,1)S(1)} %get-tuple-element.47), channel_id=1, source_target_pairs={{0,4},{4,0},{8,12},{12,8},{16,20},{20,16},{24,28},{28,24},{1,5},{5... | collective-permute-start | bytes 393224 | tf_op jit(solution)/shard_map/sum_columns/ppermute | solution.py:27
  33.5 0.3 collective-permute-done.12
  33.8 0.2 collective-permute-start.13
  34.0 3.1 %collective-permute-done.16 = bf16[128,256]{1,0:T(8,128)(2,1)S(1)} collective-permute-done((bf16[128,256]{1,0:T(8,128)(2,1)S(1)}, bf16[128,256]{1,0:T(8,128)(2,1)S(1)}, u32[]{:S(2)}, u32[]{:S(2)}) %collective-permute-start.16) | collective-permute-done | bytes 65568 | tf_op jit(solution)/shard_map/sum_columns/ppermute | solution.py:27
  37.1 0.0 collective-permute-done.15
  37.2 1.2 %collective-permute-start.20 = (bf16[128,256]{1,0:T(8,128)(2,1)S(1)}, bf16[128,256]{1,0:T(8,128)(2,1)S(1)}, u32[]{:S(2)}, u32[]{:S(2)}) collective-permute-start(bf16[128,256]{1,0:T(8,128)(2,1)S(1)} %add_convert_fusion.2), channel_id=1, source_target_pairs={{0,24},{4,28},{8,16},{12,20},{16,8},{20,12},{24,0},{28,4},{1,25},{... | collective-permute-start | bytes 196616 | tf_op jit(solution)/shard_map/sum_columns/ppermute | solution.py:27
  38.3 1.2 %collective-permute-start.21 = (bf16[128,256]{1,0:T(8,128)(2,1)S(1)}, bf16[128,256]{1,0:T(8,128)(2,1)S(1)}, u32[]{:S(2)}, u32[]{:S(2)}) collective-permute-start(bf16[128,256]{1,0:T(8,128)(2,1)S(1)} %add_convert_fusion.1), channel_id=1, source_target_pairs={{0,16},{4,20},{8,24},{12,28},{16,0},{20,4},{24,8},{28,12},{1,17},{... | collective-permute-start | bytes 196616 | tf_op jit(solution)/shard_map/sum_columns/ppermute | solution.py:27
  39.5 0.0 collective-permute-done.14.refs_1_
  39.5 0.0 collective-permute-done.13
  39.5 0.2 collective-permute-start.17
  39.7 2.1 %collective-permute-start.19 = (bf16[128,256]{1,0:T(8,128)(2,1)S(1)}, bf16[128,256]{1,0:T(8,128)(2,1)S(1)}, u32[]{:S(2)}, u32[]{:S(2)}) collective-permute-start(bf16[128,256]{1,0:T(8,128)(2,1)S(1)} %add_convert_fusion.3), channel_id=1, source_target_pairs={{0,8},{4,12},{8,0},{12,4},{16,24},{20,28},{24,16},{28,20},{1,9},{5... | collective-permute-start | bytes 196616 | tf_op jit(solution)/shard_map/sum_columns/ppermute | solution.py:27
  41.8 2.1 %collective-permute-done.17 = bf16[128,256]{1,0:T(8,128)(2,1)S(1)} collective-permute-done((bf16[128,256]{1,0:T(8,128)(2,1)S(1)}, bf16[128,256]{1,0:T(8,128)(2,1)S(1)}, u32[]{:S(2)}, u32[]{:S(2)}) %collective-permute-start.17) | collective-permute-done | bytes 65568 | tf_op jit(solution)/shard_map/sum_columns/sum_weight/sum_weight/ppermute | solution.py:35
  43.9 0.1 collective-permute-start.18
  44.0 1.2 %collective-permute-done.21.refs_2_ = bf16[128,256]{1,0:T(8,128)(2,1)S(1)} collective-permute-done((bf16[128,256]{1,0:T(8,128)(2,1)S(1)}, bf16[128,256]{1,0:T(8,128)(2,1)S(1)}, u32[]{:S(2)}, u32[]{:S(2)}) %collective-permute-start.21) | collective-permute-done | bytes 65568 | tf_op jit(solution)/shard_map/sum_columns/ppermute | solution.py:27
  45.2 0.0 collective-permute-done.20.refs_3_
  45.2 0.1 collective-permute-done.19.refs_4_
  45.3 0.0 collective-permute-done.18.other
  45.3 0.8 %shard_map.94 = (f32[128,256]{1,0:T(8,128)}, f32[256,256]{1,0:T(8,128)}) custom-call(bf16[128,256]{1,0:T(8,128)(2,1)S(1)} %add_convert_fusion.4.mine, bf16[128,256]{1,0:T(8,128)(2,1)S(1)} %collective-permute-done.18.other, bf16[256,256]{1,0:T(8,128)(2,1)S(1)} %get-tuple-element.55.refs_0_, bf16[256,256]{1,0:T(8,128)(2,1)S(1)} %collective-permute-done.14.refs_1_, ...), custom_call_target="tpu_custom_call" | custom-call | tf_op jit(solution)/shard_map/pallas_call | solution.py:302
  (8 shorter events, 0.2 us)
Async XLA Ops:
  0.6 7.9 %collective-permute-start = (bf16[128,256]{1,0:T(8,128)(2,1)}, bf16[128,256]{1,0:T(8,128)(2,1)S(1)}, u32[]{:S(2)}, u32[]{:S(2)}) collective-permute-start(bf16[128,256]{1,0:T(8,128)(2,1)} %bitcast.9), channel_id=1, source_target_pairs={{0,8},{4,12},{8,0},{12,4},{16,24},{20,28},{24,16},{28,20},{1,9},{5... | collective-permute-start | bytes 196616 | tf_op jit(solution)/shard_map/gather_features/ppermute | solution.py:27
  3.7 7.1 %collective-permute-start.3 = (bf16[128,256]{1,0:T(8,128)(2,1)}, bf16[128,256]{1,0:T(8,128)(2,1)S(1)}, u32[]{:S(2)}, u32[]{:S(2)}) collective-permute-start(bf16[128,256]{1,0:T(8,128)(2,1)} %bitcast.10), channel_id=1, source_target_pairs={{0,24},{4,28},{8,16},{12,20},{16,8},{20,12},{24,0},{28,4},{1,25},{... | collective-permute-start | bytes 196616 | tf_op jit(solution)/shard_map/gather_features/ppermute | solution.py:27
  6.2 6.7 %collective-permute-start.2 = (bf16[128,256]{1,0:T(8,128)(2,1)}, bf16[128,256]{1,0:T(8,128)(2,1)S(1)}, u32[]{:S(2)}, u32[]{:S(2)}) collective-permute-start(bf16[128,256]{1,0:T(8,128)(2,1)} %bitcast.11), channel_id=1, source_target_pairs={{0,16},{4,20},{8,24},{12,28},{16,0},{20,4},{24,8},{28,12},{1,17},{... | collective-permute-start | bytes 196616 | tf_op jit(solution)/shard_map/gather_features/ppermute | solution.py:27
  6.3 9.3 %collective-permute-start.1 = (bf16[128,256]{1,0:T(8,128)(2,1)}, bf16[128,256]{1,0:T(8,128)(2,1)S(1)}, u32[]{:S(2)}, u32[]{:S(2)}) collective-permute-start(bf16[128,256]{1,0:T(8,128)(2,1)} %bitcast.12), channel_id=1, source_target_pairs={{0,4},{4,0},{8,12},{12,8},{16,20},{20,16},{24,28},{28,24},{1,5},{5... | collective-permute-start | bytes 196616 | tf_op jit(solution)/shard_map/gather_features/ppermute | solution.py:27
  8.5 5.9 %copy-start.4 = (s32[1,1,6]{2,1,0:T(1,128)S(1)}, s32[1,1,6]{2,1,0:T(1,128)}, u32[]{:S(2)}) copy-start(s32[1,1,6]{2,1,0:T(1,128)} %param.10) | copy-start | bytes 76
  8.5 5.9 %copy-start.5 = (s32[1,1,6]{2,1,0:T(1,128)S(1)}, s32[1,1,6]{2,1,0:T(1,128)}, u32[]{:S(2)}) copy-start(s32[1,1,6]{2,1,0:T(1,128)} %param.11) | copy-start | bytes 76
  8.5 8.6 %copy-start = (bf16[1,1,6,128,128]{4,3,2,1,0:T(8,128)(2,1)S(1)}, bf16[1,1,6,128,128]{4,3,2,1,0:T(8,128)(2,1)}, u32[]{:S(2)}) copy-start(bf16[1,1,6,128,128]{4,3,2,1,0:T(8,128)(2,1)} %param.13) | copy-start | bytes 589828
  8.5 8.6 %copy-start.2 = (bf16[1,128,256]{2,1,0:T(8,128)(2,1)S(1)}, bf16[1,128,256]{2,1,0:T(8,128)(2,1)}, u32[]{:S(2)}) copy-start(bf16[1,128,256]{2,1,0:T(8,128)(2,1)} %param.7) | copy-start | bytes 196612
  8.5 7.1 %collective-permute-start.4 = (bf16[128,256]{1,0:T(8,128)(2,1)}, bf16[128,256]{1,0:T(8,128)(2,1)S(1)}, u32[]{:S(2)}, u32[]{:S(2)}) collective-permute-start(bf16[128,256]{1,0:T(8,128)(2,1)} %bitcast.14), channel_id=1, source_target_pairs={{0,2},{1,3},{2,0},{3,1},{4,6},{5,7},{6,4},{7,5},{8,10},{9,11},{10,... | collective-permute-start | bytes 196616 | tf_op jit(solution)/shard_map/gather_features/ppermute | solution.py:27
  10.1 7.0 %collective-permute-start.6 = (bf16[128,256]{1,0:T(8,128)(2,1)S(1)}, bf16[128,256]{1,0:T(8,128)(2,1)S(1)}, u32[]{:S(2)}, u32[]{:S(2)}) collective-permute-start(bf16[128,256]{1,0:T(8,128)(2,1)S(1)} %collective-permute-done.refs_2_), channel_id=1, source_target_pairs={{0,4},{4,0},{8,12},{12,8},{16,20},{20,16},{24,28},{28,24},{1,5},{5... | collective-permute-start | bytes 196616 | tf_op jit(solution)/shard_map/gather_features/ppermute | solution.py:27
  10.8 4.8 %collective-permute-start.7 = (bf16[128,256]{1,0:T(8,128)(2,1)S(1)}, bf16[128,256]{1,0:T(8,128)(2,1)S(1)}, u32[]{:S(2)}, u32[]{:S(2)}) collective-permute-start(bf16[128,256]{1,0:T(8,128)(2,1)S(1)} %collective-permute-done.3.refs_3_), channel_id=1, source_target_pairs={{0,4},{4,0},{8,12},{12,8},{16,20},{20,16},{24,28},{28,24},{1,5},{5... | collective-permute-start | bytes 196616 | tf_op jit(solution)/shard_map/gather_features/ppermute | solution.py:27
  12.9 4.3 %collective-permute-start.5 = (bf16[128,256]{1,0:T(8,128)(2,1)S(1)}, bf16[128,256]{1,0:T(8,128)(2,1)S(1)}, u32[]{:S(2)}, u32[]{:S(2)}) collective-permute-start(bf16[128,256]{1,0:T(8,128)(2,1)S(1)} %collective-permute-done.2.refs_1_), channel_id=1, source_target_pairs={{0,4},{4,0},{8,12},{12,8},{16,20},{20,16},{24,28},{28,24},{1,5},{5... | collective-permute-start | bytes 196616 | tf_op jit(solution)/shard_map/gather_features/ppermute | solution.py:27
  18.0 1.4 %collective-permute-start.8 = (bf16[256,256]{1,0:T(8,128)(2,1)S(1)}, bf16[256,256]{1,0:T(8,128)(2,1)S(1)}, u32[]{:S(2)}, u32[]{:S(2)}) collective-permute-start(bf16[256,256]{1,0:T(8,128)(2,1)S(1)} %get-tuple-element.39), channel_id=1, source_target_pairs={{0,1},{1,0},{2,3},{3,2},{4,5},{5,4},{6,7},{7,6},{8,9},{9,8},{10,11... | collective-permute-start | bytes 393224 | tf_op jit(solution)/shard_map/sum_rows/ppermute | solution.py:27
  19.5 5.7 %copy-start.1 = (bf16[256,256]{1,0:T(8,128)(2,1)S(1)}, bf16[256,256]{1,0:T(8,128)(2,1)}, u32[]{:S(2)}) copy-start(bf16[256,256]{1,0:T(8,128)(2,1)} %weight.1) | copy-start | bytes 393220
  19.5 5.7 %copy-start.3 = (bf16[1,128,256]{2,1,0:T(8,128)(2,1)S(1)}, bf16[1,128,256]{2,1,0:T(8,128)(2,1)}, u32[]{:S(2)}) copy-start(bf16[1,128,256]{2,1,0:T(8,128)(2,1)} %param.9) | copy-start | bytes 196612
  19.5 5.6 %collective-permute-start.9 = (bf16[256,256]{1,0:T(8,128)(2,1)S(1)}, bf16[256,256]{1,0:T(8,128)(2,1)S(1)}, u32[]{:S(2)}, u32[]{:S(2)}) collective-permute-start(bf16[256,256]{1,0:T(8,128)(2,1)S(1)} %add_convert_fusion.mine), channel_id=1, source_target_pairs={{0,2},{1,3},{2,0},{3,1},{4,6},{5,7},{6,4},{7,5},{8,10},{9,11},{10,... | collective-permute-start | bytes 393224 | tf_op jit(solution)/shard_map/sum_rows/ppermute | solution.py:27
  26.0 1.4 %collective-permute-start.11 = (bf16[256,256]{1,0:T(8,128)(2,1)S(1)}, bf16[256,256]{1,0:T(8,128)(2,1)S(1)}, u32[]{:S(2)}, u32[]{:S(2)}) collective-permute-start(bf16[256,256]{1,0:T(8,128)(2,1)S(1)} %get-tuple-element.43.refs_0_), channel_id=1, source_target_pairs={{0,1},{1,0},{2,3},{3,2},{4,5},{5,4},{6,7},{7,6},{8,9},{9,8},{10,11... | collective-permute-start | bytes 393224 | tf_op jit(solution)/shard_map/swap_cores/ppermute | solution.py:27
  26.0 1.4 %collective-permute-start.10 = (bf16[128,256]{1,0:T(8,128)(2,1)S(1)}, bf16[128,256]{1,0:T(8,128)(2,1)S(1)}, u32[]{:S(2)}, u32[]{:S(2)}) collective-permute-start(bf16[128,256]{1,0:T(8,128)(2,1)S(1)} %get-tuple-element.42), channel_id=1, source_target_pairs={{0,1},{1,0},{2,3},{3,2},{4,5},{5,4},{6,7},{7,6},{8,9},{9,8},{10,11... | collective-permute-start | bytes 196616 | tf_op jit(solution)/shard_map/swap_cores/ppermute | solution.py:27
  27.5 6.3 %collective-permute-start.12 = (bf16[128,256]{1,0:T(8,128)(2,1)S(1)}, bf16[128,256]{1,0:T(8,128)(2,1)S(1)}, u32[]{:S(2)}, u32[]{:S(2)}) collective-permute-start(bf16[128,256]{1,0:T(8,128)(2,1)S(1)} %add_convert_fusion.7), channel_id=1, source_target_pairs={{0,17},{1,16},{2,19},{3,18},{4,21},{5,20},{6,23},{7,22},{8,25},{9,... | collective-permute-start | bytes 196616 | tf_op jit(solution)/shard_map/sum_weight/ppermute | solution.py:35
  30.7 6.4 %collective-permute-start.15 = (bf16[128,256]{1,0:T(8,128)(2,1)S(1)}, bf16[128,256]{1,0:T(8,128)(2,1)S(1)}, u32[]{:S(2)}, u32[]{:S(2)}) collective-permute-start(bf16[128,256]{1,0:T(8,128)(2,1)S(1)} %get-tuple-element.48), channel_id=1, source_target_pairs={{0,4},{4,0},{8,12},{12,8},{16,20},{20,16},{24,28},{28,24},{1,5},{5... | collective-permute-start | bytes 196616 | tf_op jit(solution)/shard_map/sum_columns/ppermute | solution.py:27
  31.5 5.6 %collective-permute-start.16 = (bf16[128,256]{1,0:T(8,128)(2,1)S(1)}, bf16[128,256]{1,0:T(8,128)(2,1)S(1)}, u32[]{:S(2)}, u32[]{:S(2)}) collective-permute-start(bf16[128,256]{1,0:T(8,128)(2,1)S(1)} %get-tuple-element.49), channel_id=1, source_target_pairs={{0,4},{4,0},{8,12},{12,8},{16,20},{20,16},{24,28},{28,24},{1,5},{5... | collective-permute-start | bytes 196616 | tf_op jit(solution)/shard_map/sum_columns/ppermute | solution.py:27
  32.8 6.7 %collective-permute-start.14 = (bf16[256,256]{1,0:T(8,128)(2,1)S(1)}, bf16[256,256]{1,0:T(8,128)(2,1)S(1)}, u32[]{:S(2)}, u32[]{:S(2)}) collective-permute-start(bf16[256,256]{1,0:T(8,128)(2,1)S(1)} %get-tuple-element.47), channel_id=1, source_target_pairs={{0,4},{4,0},{8,12},{12,8},{16,20},{20,16},{24,28},{28,24},{1,5},{5... | collective-permute-start | bytes 393224 | tf_op jit(solution)/shard_map/sum_columns/ppermute | solution.py:27
  33.8 5.7 %collective-permute-start.13 = (bf16[128,256]{1,0:T(8,128)(2,1)S(1)}, bf16[128,256]{1,0:T(8,128)(2,1)S(1)}, u32[]{:S(2)}, u32[]{:S(2)}) collective-permute-start(bf16[128,256]{1,0:T(8,128)(2,1)S(1)} %add_convert_fusion.6), channel_id=1, source_target_pairs={{0,9},{1,8},{2,11},{3,10},{4,13},{5,12},{6,15},{7,14},{8,1},{9,0},... | collective-permute-start | bytes 196616 | tf_op jit(solution)/shard_map/sum_columns/sum_weight/sum_weight/ppermute | solution.py:35
  37.2 8.0 %collective-permute-start.20 = (bf16[128,256]{1,0:T(8,128)(2,1)S(1)}, bf16[128,256]{1,0:T(8,128)(2,1)S(1)}, u32[]{:S(2)}, u32[]{:S(2)}) collective-permute-start(bf16[128,256]{1,0:T(8,128)(2,1)S(1)} %add_convert_fusion.2), channel_id=1, source_target_pairs={{0,24},{4,28},{8,16},{12,20},{16,8},{20,12},{24,0},{28,4},{1,25},{... | collective-permute-start | bytes 196616 | tf_op jit(solution)/shard_map/sum_columns/ppermute | solution.py:27
  38.3 6.8 %collective-permute-start.21 = (bf16[128,256]{1,0:T(8,128)(2,1)S(1)}, bf16[128,256]{1,0:T(8,128)(2,1)S(1)}, u32[]{:S(2)}, u32[]{:S(2)}) collective-permute-start(bf16[128,256]{1,0:T(8,128)(2,1)S(1)} %add_convert_fusion.1), channel_id=1, source_target_pairs={{0,16},{4,20},{8,24},{12,28},{16,0},{20,4},{24,8},{28,12},{1,17},{... | collective-permute-start | bytes 196616 | tf_op jit(solution)/shard_map/sum_columns/ppermute | solution.py:27
  39.5 4.4 %collective-permute-start.17 = (bf16[128,256]{1,0:T(8,128)(2,1)S(1)}, bf16[128,256]{1,0:T(8,128)(2,1)S(1)}, u32[]{:S(2)}, u32[]{:S(2)}) collective-permute-start(bf16[128,256]{1,0:T(8,128)(2,1)S(1)} %add_convert_fusion.5), channel_id=1, source_target_pairs={{0,5},{1,4},{2,7},{3,6},{4,1},{5,0},{6,3},{7,2},{8,13},{9,12},{10,... | collective-permute-start | bytes 196616 | tf_op jit(solution)/shard_map/sum_columns/sum_weight/sum_weight/ppermute | solution.py:35
  39.7 5.6 %collective-permute-start.19 = (bf16[128,256]{1,0:T(8,128)(2,1)S(1)}, bf16[128,256]{1,0:T(8,128)(2,1)S(1)}, u32[]{:S(2)}, u32[]{:S(2)}) collective-permute-start(bf16[128,256]{1,0:T(8,128)(2,1)S(1)} %add_convert_fusion.3), channel_id=1, source_target_pairs={{0,8},{4,12},{8,0},{12,4},{16,24},{20,28},{24,16},{28,20},{1,9},{5... | collective-permute-start | bytes 196616 | tf_op jit(solution)/shard_map/sum_columns/ppermute | solution.py:27
  43.9 1.4 %collective-permute-start.18 = (bf16[128,256]{1,0:T(8,128)(2,1)S(1)}, bf16[128,256]{1,0:T(8,128)(2,1)S(1)}, u32[]{:S(2)}, u32[]{:S(2)}) collective-permute-start(bf16[128,256]{1,0:T(8,128)(2,1)S(1)} %add_convert_fusion.4.mine), channel_id=1, source_target_pairs={{0,1},{1,0},{2,3},{3,2},{4,5},{5,4},{6,7},{7,6},{8,9},{9,8},{10,11... | collective-permute-start | bytes 196616 | tf_op jit(solution)/shard_map/sum_weight/ppermute | solution.py:27
